TPU v7x, 32 devices: a whole 2x2x4 slice. The times are simulated.
32 devices in a mesh: dp: 8 (over y, x, core), tensor: 4 (over z).
Axes of the slice: x: 2, y: 2, z: 4, core: 2. Of those that a mesh axis runs over, the one named last changes fastest.
Arguments:
- gradient: bfloat16 [8, 256, 28672], P('dp', None, 'tensor'), may hold values from -6 to 6
- feedback: float32 [8, 256, 28672], P('dp', None, 'tensor'), may hold values from -4 to 4
- right_factor: float32 [28672, 32], P('tensor'), may hold values from -6 to 6
Outputs:
- new_feedback: float32 [8, 256, 28672], P('dp', None, 'tensor')
- left_factor: float32 [256, 32], replicated
- new_right: float32 [28672, 32], P('tensor')
All inputs are finite; a program needn't handle non-finite values.
Results may differ from a plain program's by a relative error of at most 0.0003.
Values sent between devices are 32-bit elements; how exact they have to be, the bound alone decides.
No kernel may reach another device: no remote copies, remote signals or barrier semaphores. Data moves between devices by JAX's collectives and lax.ppermute only.
A program may use at most 64 MiB of HBM per device.

v0:
```python
import jax
import jax.numpy as jnp
from jax import lax
from jax.sharding import PartitionSpec as P


def orthonormal(matrix, gram_matrix):
    lower = jnp.linalg.cholesky(gram_matrix)
    return lax.linalg.triangular_solve(lower, matrix, left_side=False, lower=True, transpose_a=True)


def per_device(gradient, feedback, right_factor):
    combined = gradient[0].astype(jnp.float32) + feedback[0]
    replicas = lax.axis_size("dp")
    left_part = jnp.dot(
        combined, right_factor, precision=lax.Precision.HIGHEST, preferred_element_type=jnp.float32
    )
    left_sum = lax.psum(left_part, ("dp", "tensor")) / replicas
    gram_matrix = jnp.dot(
        left_sum.T, left_sum, precision=lax.Precision.HIGHEST, preferred_element_type=jnp.float32
    )
    left_factor = orthonormal(left_sum, gram_matrix)
    right_part = lax.dot_general(
        combined,
        left_factor,
        (((0,), (0,)), ((), ())),
        precision=lax.Precision.HIGHEST,
        preferred_element_type=jnp.float32,
    )
    new_right = lax.psum(right_part, "dp") / replicas
    approx = lax.dot_general(
        left_factor,
        new_right,
        (((1,), (1,)), ((), ())),
        precision=lax.Precision.HIGHEST,
        preferred_element_type=jnp.float32,
    )
    new_feedback = combined - approx
    return (new_feedback[None], left_factor, new_right)


def solution(mesh):
    return jax.shard_map(
        per_device,
        mesh=mesh,
        in_specs=(P("dp", None, "tensor"), P("dp", None, "tensor"), P("tensor", None)),
        out_specs=(P("dp", None, "tensor"), P(), P("tensor", None)),
        check_vma=False,
    )
```

profile of v0, /device:TPU:1, one launch (start us, length us, event | category | flops | bytes accessed | tf_op | source)
XLA Modules:
  0.0 150.5 jit_solution(5859092277018020917)
XLA Ops:
  7.2 0.0 copy-start
  7.2 0.0 all-reduce.2.cloned.1.call-start
  7.2 1.1 copy-done
  8.3 9.0 %fusion.3 = f32[256,32]{0,1:T(8,128)S(1)} fusion(f32[7168,32]{0,1:T(8,128)S(1)} %copy-done, f32[1,256,7168]{2,1,0:T(8,128)} %param.4, bf16[1,256,7168]{2,1,0:T(8,128)(2,1)} %param.3), kind=kOutput, calls=%fused_computation.4 | convolution fusion | flops 708313088 | bytes 11960320 | tf_op jit(solution)/shard_map/dot_general | solution.py:15
  17.4 40.8 %psum.14 = f32[256,32]{0,1:T(8,128)S(1)} all-reduce(f32[256,32]{0,1:T(8,128)S(1)} %fusion.3), channel_id=1, replica_groups=mesh['dp'=8,'tensor'=4] {'dp','tensor'}, use_global_device_ids=true, to_apply=%region_0.0 | all-reduce | flops 8192 | bytes 65536 | tf_op jit(solution)/shard_map/psum | solution.py:18
  58.2 0.2 fusion.7
  58.4 0.1 copy.6
  58.4 2.9 %cholesky.16 = f32[32,32]{1,0:T(8,128)S(1)} custom-call(f32[32,32]{1,0:T(8,128)S(1)} %fusion.11), custom_call_target="Cholesky" | custom-call | tf_op jit(solution)/shard_map/jit(cholesky)/cholesky | solution.py:8
  61.4 0.6 compare_reduce_fusion
  62.0 0.7 fusion.9
  62.7 2.4 %custom-call.6 = f32[1,32,32]{1,2,0:T(8,128)S(1)} custom-call(f32[1,32,32]{2,1,0:T(8,128)S(1)} %fusion.9), custom_call_target="InvertDiagBlocksLowerTriangular" | custom-call | tf_op jit(solution)/shard_map/triangular_solve | solution.py:9
  65.1 0.2 fusion.5
  65.4 0.0 copy-start.2
  65.4 9.9 %fusion.1 = f32[7168,32]{0,1:T(8,128)} fusion(f32[256,32]{0,1:T(8,128)S(1)} %fusion.5, f32[1,256,7168]{2,1,0:T(8,128)} %param.4, bf16[1,256,7168]{2,1,0:T(8,128)(2,1)} %param.3), kind=kOutput, calls=%fused_computation.2 | convolution fusion | flops 708313088 | bytes 11960320 | tf_op jit(solution)/shard_map/dot_general | solution.py:23
  75.3 0.0 all-reduce.2.cloned.1.call-update
  75.3 55.7 %all-reduce.2.cloned.1.call-done = f32[7168,32]{0,1:T(8,128)} async-done(((f32[7168,32]{0,1:T(8,128)}), f32[7168,32]{0,1:T(8,128)}) %all-reduce.2.cloned.1.call-update) | async-done | bytes 917520 | tf_op jit(solution)/shard_map/psum | solution.py:30
  131.0 1.2 broadcast_multiply_fusion
  132.2 0.0 copy-done.2
  132.2 0.0 copy-start.1
  132.2 11.4 %fusion = f32[1,256,7168]{2,1,0:T(8,128)} fusion(f32[256,32]{0,1:T(8,128)S(1)} %fusion.5, f32[7168,32]{0,1:T(8,128)S(1)} %broadcast_multiply_fusion, f32[1,256,7168]{2,1,0:T(8,128)} %param.4, bf16[1,256,7168]{2,1,0:T(8,128)(2,1)} %param.3), kind=kOutput, calls=%fused_computation.1 | convolution fusion | flops 710148096 | bytes 19300352 | tf_op jit(solution)/shard_map/dot_general | solution.py:31
  143.7 0.0 copy-done.1
  (2 shorter events, 0.0 us)
Async XLA Ops:
  7.2 1.2 copy-start
  7.2 123.8 %all-reduce.2.cloned.1.call-start = ((), (), s32[]{:S(2)}) async-start(), calls=%async_computation | async-start | bytes 1835008 | tf_op jit(solution)/shard_map/psum | solution.py:30
  65.4 66.8 %copy-start.2 = (f32[256,32]{0,1:T(8,128)}, f32[256,32]{0,1:T(8,128)S(1)}, u32[]{:S(2)}) copy-start(f32[256,32]{0,1:T(8,128)S(1)} %fusion.5) | copy-start | bytes 98308
  132.2 11.4 %copy-start.1 = (f32[7168,32]{0,1:T(8,128)}, f32[7168,32]{0,1:T(8,128)S(1)}, u32[]{:S(2)}) copy-start(f32[7168,32]{0,1:T(8,128)S(1)} %broadcast_multiply_fusion) | copy-start | bytes 2752516
Sparse Core Ops, SparseCore 0:
  75.4 55.5 all-reduce.1
where the time goes:
time: 152 us; the launch traced here: 151 us
  waiting for transfers between devices  55.7 us (37%)
  blocking collectives  40.8 us (27%)
  matrix products  30.7 us (20%)
  between operations  14.1 us (9%)
  other arithmetic  7.93 us (5%)
    psum x1, waiting for transfers between devices, per_device(): new_right = lax.psum(right_part, 'dp') / replicas  55.7 us
    psum x1, blocking collectives, per_device(): left_sum = lax.psum(left_part, ('dp', 'tensor')) / replicas  40.8 us
    dot_general x1, matrix products, per_device(): lax.dot_general(left_factor, new_right, (((1,), (1,)), ((), ())), precisi...  11.4 us
    dot_general x1, matrix products, per_device(): lax.dot_general(combined, left_factor, (((0,), (0,)), ((), ())), precisio...  9.87 us
    dot_general x1, matrix products, per_device(): jnp.dot(combined, right_factor, precision=lax.Precision.HIGHEST, preferre...  9.05 us
    another operation x3, other arithmetic, orthonormal(): lower = jnp.linalg.cholesky(gram_matrix)  3.6 us
    another operation x2, other arithmetic, orthonormal(): lax.linalg.triangular_solve(lower, matrix, left_side=False, lower=True, t...  3.09 us
  transfers between devices with their start and end apart: 1, of which 1 were waited for; matrix products, arithmetic and copies ran while one was open for 0% of the time, Pallas kernels for 0%

commit v1 on v0

v1 whole, which is shorter than its diff:
```python
import jax
import jax.numpy as jnp
from jax import lax
from jax.sharding import PartitionSpec as P

HIGH = lax.Precision.HIGH
HIGHEST = lax.Precision.HIGHEST


def swap(x, axis, mask):
    size = lax.axis_size(axis)
    return lax.ppermute(x, axis, [(i, i ^ mask) for i in range(size)])


def tree(terms):
    while len(terms) > 1:
        terms = [a + b for a, b in zip(terms[::2], terms[1::2])]
    return terms[0]


def sum_over(x, axis, low, high):
    while low < high:
        step = min(2, high - low)
        x = tree([x] + [swap(x, axis, k << low) for k in range(1, 1 << step)])
        low += step
    return x


def bits(axis):
    size = lax.axis_size(axis)
    assert size & (size - 1) == 0
    return size.bit_length() - 1


def pick(x, index):
    return lax.dynamic_index_in_dim(x, index, 0, keepdims=False)


def per_device(gradient, feedback, right_factor):
    combined = gradient[0].astype(jnp.float32) + feedback[0]
    rows, columns = combined.shape
    rank = right_factor.shape[1]
    replicas = lax.axis_size("dp")
    me = lax.axis_index("dp")
    core, chip = me % 2, me // 2
    chips = replicas // 2

    left = jnp.dot(combined, right_factor, precision=HIGH, preferred_element_type=jnp.float32)
    left = sum_over(left, "dp", 0, 1)
    left = sum_over(left, "dp", 1, bits("dp"))
    left = sum_over(left, "tensor", 0, bits("tensor")) / replicas

    right = lax.dot_general(
        left, combined, (((0,), (0,)), ((), ())), precision=HIGH, preferred_element_type=jnp.float32
    )
    pieces = right.reshape(rank, 2, chips, columns // replicas).transpose(1, 2, 0, 3)
    half = pick(pieces, core) + swap(pick(pieces, 1 - core), "dp", 1)
    own = tree([pick(half, chip)] + [swap(pick(half, chip ^ k), "dp", 2 * k) for k in range(1, chips)])

    gram = lax.dot_general(
        left, left, (((0,), (0,)), ((), ())), precision=HIGHEST, preferred_element_type=jnp.float32
    )
    lower = jnp.linalg.cholesky(gram)
    inverse = lax.linalg.triangular_solve(lower, jnp.eye(rank, dtype=jnp.float32), left_side=True, lower=True)
    left_factor = lax.dot_general(
        left, inverse, (((1,), (1,)), ((), ())), precision=HIGHEST, preferred_element_type=jnp.float32
    )
    own = jnp.dot(inverse, own, precision=HIGHEST, preferred_element_type=jnp.float32) / replicas

    got = jnp.stack([own] + [swap(own, "dp", 2 * k) for k in range(1, chips)])
    mine = jnp.stack([pick(got, chip ^ k) for k in range(chips)])
    other = swap(mine, "dp", 1)
    both = jnp.stack([jnp.where(core == 0, mine, other), jnp.where(core == 0, other, mine)])
    new_right = both.transpose(2, 0, 1, 3).reshape(rank, columns)
    approx = jnp.dot(left_factor, new_right, precision=HIGH, preferred_element_type=jnp.float32)
    return ((combined - approx)[None], left_factor, new_right.T)


def solution(mesh):
    return jax.shard_map(
        per_device,
        mesh=mesh,
        in_specs=(P("dp", None, "tensor"), P("dp", None, "tensor"), P("tensor", None)),
        out_specs=(P("dp", None, "tensor"), P(), P("tensor", None)),
        check_vma=False,
    )
```

time: 152 us -> 79.6 us (0.52)
  blocking collectives: 40.8 us -> 0 us
  waiting for transfers between devices: 55.7 us -> 15.4 us
  starting transfers between devices: 0.04 us -> 17.7 us
  between operations: 14.1 us -> 0.84 us
  local copies, waits for them, and re-layouts: 1.22 us -> 10.7 us
  matrix products: 30.7 us -> 23.5 us
  other arithmetic: 7.93 us -> 10.9 us
    psum x1 -> x0, waiting for transfers between devices: 55.7 us -> none  [per_device(): new_right = lax.psum(right_part, 'dp') / replicas]
    psum x1 -> x0, blocking collectives: 40.8 us -> none  [per_device(): left_sum = lax.psum(left_part, ('dp', 'tensor')) / replicas]
    ppermute x0 -> x15, starting transfers between devices: none -> 17.7 us  [swap(): return lax.ppermute(x, axis, [(i, i ^ mask) for i in range(size)])]
    ppermute x0 -> x15, waiting for transfers between devices: none -> 15.4 us  [swap(): return lax.ppermute(x, axis, [(i, i ^ mask) for i in range(size)])]
    dot_general x1 -> x2, local copies, waits for them, and re-layouts: 0.07 us -> 8.46 us  [the longest x1 8.39 us: per_device(): lax.dot_general(left, combined, (((0,), (0,)), ((), ())), precision=HIGH,...]
    dot_general x4 -> x6, matrix products: 30.5 us -> 23.3 us  [the longest x1 8.37 us: per_device(): jnp.dot(left_factor, new_right, precision=HIGH, preferred_element_type=jn...]
    dot_general x0 -> x1, other arithmetic: none -> 3.91 us  [per_device(): lax.dot_general(left, combined, (((0,), (0,)), ((), ())), precision=HIGH,...]
    another operation x5 -> x8, other arithmetic: 6.68 us -> 6.82 us  [the longest x3 3.59 us: per_device(): lower = jnp.linalg.cholesky(gram)]
  transfers between devices with their start and end apart: 1 -> 15, of which waited for: 1 -> 10; matrix products, arithmetic and copies ran while one was open for 0% -> 25% of each run, Pallas kernels for 0% -> 0%
where the time goes in v1:
time: 79.6 us; the launch traced here: 79.1 us
  matrix products  23.5 us (30%)
  starting transfers between devices  17.7 us (22%)
  waiting for transfers between devices  15.4 us (19%)
  other arithmetic  10.9 us (14%)
  local copies, waits for them, and re-layouts  10.7 us (13%)
  between operations  0.84 us (1%)
    ppermute x15, starting transfers between devices, swap(): return lax.ppermute(x, axis, [(i, i ^ mask) for i in range(size)])  17.7 us
    ppermute x15, waiting for transfers between devices, swap(): return lax.ppermute(x, axis, [(i, i ^ mask) for i in range(size)])  15.4 us
    dot_general x1, local copies, waits for them, and re-layouts, per_device(): lax.dot_general(left, combined, (((0,), (0,)), ((), ())), precision=HIGH,...  8.39 us
    dot_general x1, matrix products, per_device(): jnp.dot(left_factor, new_right, precision=HIGH, preferred_element_type=jn...  8.37 us
    dot_general x1, matrix products, per_device(): jnp.dot(combined, right_factor, precision=HIGH, preferred_element_type=jn...  8.05 us
    dot_general x1, matrix products, per_device(): lax.dot_general(left, combined, (((0,), (0,)), ((), ())), precision=HIGH,...  6.31 us
    dot_general x1, other arithmetic, per_device(): lax.dot_general(left, combined, (((0,), (0,)), ((), ())), precision=HIGH,...  3.91 us
    another operation x3, other arithmetic, per_device(): lower = jnp.linalg.cholesky(gram)  3.59 us
  transfers between devices with their start and end apart: 15, of which 10 were waited for; matrix products, arithmetic and copies ran while one was open for 25% of the time, Pallas kernels for 0%

profile of v1, /device:TPU:1, one launch (start us, length us, event | category | flops | bytes accessed | tf_op | source)
XLA Modules:
  0.0 79.1 jit_solution(16425850994296995442)
XLA Ops:
  0.6 0.0 copy-start
  0.7 0.0 copy-start.1
  0.7 1.1 %copy-done = f32[7168,32]{0,1:T(8,128)S(1)} copy-done((f32[7168,32]{0,1:T(8,128)S(1)}, f32[7168,32]{0,1:T(8,128)}, u32[]{:S(2)}) %copy-start) | copy-done | bytes 917528
  1.8 8.0 %fusion.1 = f32[256,32]{0,1:T(8,128)S(1)} fusion(f32[7168,32]{0,1:T(8,128)S(1)} %copy-done, f32[1,256,7168]{2,1,0:T(8,128)} %param.4, bf16[1,256,7168]{2,1,0:T(8,128)(2,1)} %param.3), kind=kOutput, calls=%fused_computation.2 | convolution fusion | flops 355991552 | bytes 11960320 | tf_op jit(solution)/shard_map/dot_general | solution.py:48
  9.9 0.1 collective-permute-start
  10.0 1.1 %collective-permute-done = f32[256,32]{0,1:T(8,128)S(1)} collective-permute-done((f32[256,32]{0,1:T(8,128)S(1)}, f32[256,32]{0,1:T(8,128)S(1)}, u32[]{:S(2)}, u32[]{:S(2)}) %collective-permute-start) | collective-permute-done | bytes 32800 | tf_op jit(solution)/shard_map/ppermute | solution.py:12
  11.1 2.4 %collective-permute-start.1 = (f32[256,32]{0,1:T(8,128)S(1)}, f32[256,32]{0,1:T(8,128)S(1)}, u32[]{:S(2)}, u32[]{:S(2)}) collective-permute-start(f32[256,32]{0,1:T(8,128)S(1)} %add.82), channel_id=1, source_target_pairs={{0,8},{4,12},{8,0},{12,4},{16,24},{20,28},{24,16},{28,20},{1,9},{5... | collective-permute-start | bytes 98312 | tf_op jit(solution)/shard_map/ppermute | solution.py:12
  13.5 1.2 %collective-permute-start.2 = (f32[256,32]{0,1:T(8,128)S(1)}, f32[256,32]{0,1:T(8,128)S(1)}, u32[]{:S(2)}, u32[]{:S(2)}) collective-permute-start(f32[256,32]{0,1:T(8,128)S(1)} %add.82), channel_id=1, source_target_pairs={{0,16},{4,20},{8,24},{12,28},{16,0},{20,4},{24,8},{28,12},{1,17},{... | collective-permute-start | bytes 98312 | tf_op jit(solution)/shard_map/ppermute | solution.py:12
  14.8 0.0 collective-permute-start.3
  14.8 0.0 collective-permute-done.1
  14.8 1.5 %collective-permute-done.2 = f32[256,32]{0,1:T(8,128)S(1)} collective-permute-done((f32[256,32]{0,1:T(8,128)S(1)}, f32[256,32]{0,1:T(8,128)S(1)}, u32[]{:S(2)}, u32[]{:S(2)}) %collective-permute-start.2) | collective-permute-done | bytes 32800 | tf_op jit(solution)/shard_map/ppermute | solution.py:12
  16.3 2.1 %collective-permute-done.3 = f32[256,32]{0,1:T(8,128)S(1)} collective-permute-done((f32[256,32]{0,1:T(8,128)S(1)}, f32[256,32]{0,1:T(8,128)S(1)}, u32[]{:S(2)}, u32[]{:S(2)}) %collective-permute-start.3) | collective-permute-done | bytes 32800 | tf_op jit(solution)/shard_map/ppermute | solution.py:12
  18.4 1.4 %collective-permute-start.4 = (f32[256,32]{0,1:T(8,128)S(1)}, f32[256,32]{0,1:T(8,128)S(1)}, u32[]{:S(2)}, u32[]{:S(2)}) collective-permute-start(f32[256,32]{0,1:T(8,128)S(1)} %add_add_fusion), channel_id=1, source_target_pairs={{0,1},{1,0},{2,3},{3,2},{4,5},{5,4},{6,7},{7,6},{8,9},{9,8},{10,11... | collective-permute-start | bytes 98312 | tf_op jit(solution)/shard_map/ppermute | solution.py:12
  19.8 2.3 %collective-permute-start.5 = (f32[256,32]{0,1:T(8,128)S(1)}, f32[256,32]{0,1:T(8,128)S(1)}, u32[]{:S(2)}, u32[]{:S(2)}) collective-permute-start(f32[256,32]{0,1:T(8,128)S(1)} %add_add_fusion), channel_id=1, source_target_pairs={{0,2},{1,3},{2,0},{3,1},{4,6},{5,7},{6,4},{7,5},{8,10},{9,11},{10,... | collective-permute-start | bytes 98312 | tf_op jit(solution)/shard_map/ppermute | solution.py:12
  22.1 3.9 %fusion.3 = f32[7168,256]{0,1:T(8,128)} fusion(f32[1,256,7168]{2,1,0:T(8,128)S(1)} %copy-done.1, bf16[1,256,7168]{2,1,0:T(8,128)(2,1)S(1)} %copy-done.2), kind=kLoop, calls=%fused_computation.5 | loop fusion | flops 3670016 | bytes 18350080 | tf_op jit(solution)/shard_map/dot_general | solution.py:53
  26.0 8.4 %copy.12 = f32[7168,256]{1,0:T(8,128)} copy(f32[7168,256]{0,1:T(8,128)} %fusion.3) | data formatting | bytes 14680064 | tf_op jit(solution)/shard_map/dot_general | solution.py:53
  34.4 0.2 fusion.15
  34.6 6.3 %fusion.8 = f32[32,2,4,896]{3,0,2,1:T(8,128)S(1)} fusion(f32[2,4,896,256]{3,2,1,0:T(8,128)} %bitcast.63, f32[256,32]{0,1:T(8,128)S(1)} %add_multiply_fusion), kind=kOutput, calls=%fused_computation.21 | convolution fusion | flops 352321536 | bytes 8290304 | tf_op jit(solution)/shard_map/dot_general | solution.py:53
  41.0 2.9 %collective-permute-start.7 = (f32[4,32,896]{2,1,0:T(8,128)S(1)}, f32[4,32,896]{2,1,0:T(8,128)S(1)}, u32[]{:S(2)}, u32[]{:S(2)}) collective-permute-start(f32[4,32,896]{2,1,0:T(8,128)S(1)} %dynamic-slice_bitcast_fusion), channel_id=1, source_target_pairs={{0,4},{4,0},{8,12},{12,8},{16,20},{20,16},{24,28},{28,24},{1,5},{5... | collective-permute-start | bytes 1376264 | tf_op jit(solution)/shard_map/ppermute | solution.py:12
  43.9 0.1 copy.8
  44.0 2.9 %cholesky.17 = f32[32,32]{1,0:T(8,128)S(1)} custom-call(f32[32,32]{1,0:T(8,128)S(1)} %fusion.13), custom_call_target="Cholesky" | custom-call | tf_op jit(solution)/shard_map/jit(cholesky)/cholesky | solution.py:63
  46.9 0.6 compare_reduce_fusion
  47.6 0.7 fusion.10
  48.2 2.4 %custom-call.6 = f32[1,32,32]{1,2,0:T(8,128)S(1)} custom-call(f32[1,32,32]{2,1,0:T(8,128)S(1)} %fusion.10), custom_call_target="InvertDiagBlocksLowerTriangular" | custom-call | tf_op jit(solution)/shard_map/triangular_solve | solution.py:64
  50.7 0.1 bitcast_add_fusion
  50.8 0.1 collective-permute-start.10
  50.9 1.4 %collective-permute-start.8 = (f32[32,896]{1,0:T(8,128)S(1)}, f32[32,896]{1,0:T(8,128)S(1)}, u32[]{:S(2)}, u32[]{:S(2)}) collective-permute-start(f32[32,896]{1,0:T(8,128)S(1)} %get-tuple-element.11), channel_id=1, source_target_pairs={{0,8},{4,12},{8,0},{12,4},{16,24},{20,28},{24,16},{28,20},{1,9},{5... | collective-permute-start | bytes 344072 | tf_op jit(solution)/shard_map/ppermute | solution.py:12
  52.3 1.2 %collective-permute-start.9 = (f32[32,896]{1,0:T(8,128)S(1)}, f32[32,896]{1,0:T(8,128)S(1)}, u32[]{:S(2)}, u32[]{:S(2)}) collective-permute-start(f32[32,896]{1,0:T(8,128)S(1)} %get-tuple-element.10), channel_id=1, source_target_pairs={{0,16},{4,20},{8,24},{12,28},{16,0},{20,4},{24,8},{28,12},{1,17},{... | collective-permute-start | bytes 344072 | tf_op jit(solution)/shard_map/ppermute | solution.py:12
  53.5 0.2 fusion.11
  53.7 2.8 %collective-permute-done.10 = f32[32,896]{1,0:T(8,128)S(1)} collective-permute-done((f32[32,896]{1,0:T(8,128)S(1)}, f32[32,896]{1,0:T(8,128)S(1)}, u32[]{:S(2)}, u32[]{:S(2)}) %collective-permute-start.10) | collective-permute-done | bytes 114720 | tf_op jit(solution)/shard_map/ppermute | solution.py:12
  56.5 1.5 %collective-permute-done.8 = f32[32,896]{1,0:T(8,128)S(1)} collective-permute-done((f32[32,896]{1,0:T(8,128)S(1)}, f32[32,896]{1,0:T(8,128)S(1)}, u32[]{:S(2)}, u32[]{:S(2)}) %collective-permute-start.8) | collective-permute-done | bytes 114720 | tf_op jit(solution)/shard_map/ppermute | solution.py:12
  58.0 1.3 %collective-permute-done.9 = f32[32,896]{1,0:T(8,128)S(1)} collective-permute-done((f32[32,896]{1,0:T(8,128)S(1)}, f32[32,896]{1,0:T(8,128)S(1)}, u32[]{:S(2)}, u32[]{:S(2)}) %collective-permute-start.9) | collective-permute-done | bytes 114720 | tf_op jit(solution)/shard_map/ppermute | solution.py:12
  59.3 0.2 convolution_multiply_fusion
  59.5 0.3 collective-permute-start.11
  59.9 2.4 %collective-permute-start.13 = (f32[32,896]{1,0:T(8,128)S(1)}, f32[32,896]{1,0:T(8,128)S(1)}, u32[]{:S(2)}, u32[]{:S(2)}) collective-permute-start(f32[32,896]{1,0:T(8,128)S(1)} %convolution_multiply_fusion), channel_id=1, source_target_pairs={{0,24},{4,28},{8,16},{12,20},{16,8},{20,12},{24,0},{28,4},{1,25},{... | collective-permute-start | bytes 344072 | tf_op jit(solution)/shard_map/ppermute | solution.py:12
  62.2 1.6 %collective-permute-done.11 = f32[32,896]{1,0:T(8,128)S(1)} collective-permute-done((f32[32,896]{1,0:T(8,128)S(1)}, f32[32,896]{1,0:T(8,128)S(1)}, u32[]{:S(2)}, u32[]{:S(2)}) %collective-permute-start.11) | collective-permute-done | bytes 114720 | tf_op jit(solution)/shard_map/ppermute | solution.py:12
  63.8 0.5 collective-permute-done.12
  64.3 1.6 %collective-permute-done.13 = f32[32,896]{1,0:T(8,128)S(1)} collective-permute-done((f32[32,896]{1,0:T(8,128)S(1)}, f32[32,896]{1,0:T(8,128)S(1)}, u32[]{:S(2)}, u32[]{:S(2)}) %collective-permute-start.13) | collective-permute-done | bytes 114720 | tf_op jit(solution)/shard_map/ppermute | solution.py:12
  66.1 2.0 %collective-permute-start.14 = (f32[4,32,896]{2,1,0:T(8,128)S(1)}, f32[4,32,896]{2,1,0:T(8,128)S(1)}, u32[]{:S(2)}, u32[]{:S(2)}) collective-permute-start(f32[4,32,896]{2,1,0:T(8,128)S(1)} %pad_maximum_fusion.1), channel_id=1, source_target_pairs={{0,4},{4,0},{8,12},{12,8},{16,20},{20,16},{24,28},{28,24},{1,5},{5... | collective-permute-start | bytes 1376264 | tf_op jit(solution)/shard_map/ppermute | solution.py:12
  68.1 0.2 fusion.16
  68.2 0.0 copy-start.4
  68.3 1.3 %collective-permute-done.14 = f32[4,32,896]{2,1,0:T(8,128)S(1)} collective-permute-done((f32[4,32,896]{2,1,0:T(8,128)S(1)}, f32[4,32,896]{2,1,0:T(8,128)S(1)}, u32[]{:S(2)}, u32[]{:S(2)}) %collective-permute-start.14) | collective-permute-done | bytes 458784 | tf_op jit(solution)/shard_map/ppermute | solution.py:12
  69.5 0.1 select_bitcast_fusion.1
  69.6 0.1 maximum_bitcast_fusion
  69.7 0.6 copy.10
  70.3 0.4 reshape.22
  70.7 0.0 copy-start.3
  70.7 8.4 %fusion = f32[1,256,7168]{2,1,0:T(8,128)} fusion(f32[256,32]{0,1:T(8,128)S(1)} %fusion.16, f32[32,7168]{1,0:T(8,128)S(1)} %reshape.22, f32[1,256,7168]{2,1,0:T(8,128)} %param.4, bf16[1,256,7168]{2,1,0:T(8,128)(2,1)} %param.3), kind=kOutput, calls=%fused_computation.1 | convolution fusion | flops 357826560 | bytes 19300352 | tf_op jit(solution)/shard_map/dot_general | solution.py:75
  (21 shorter events, 0.3 us)
Async XLA Ops:
  0.6 1.2 %copy-start = (f32[7168,32]{0,1:T(8,128)S(1)}, f32[7168,32]{0,1:T(8,128)}, u32[]{:S(2)}) copy-start(f32[7168,32]{0,1:T(8,128)} %param.5) | copy-start | bytes 2752516
  0.6 21.5 %copy-start.2 = (bf16[1,256,7168]{2,1,0:T(8,128)(2,1)S(1)}, bf16[1,256,7168]{2,1,0:T(8,128)(2,1)}, u32[]{:S(2)}) copy-start(bf16[1,256,7168]{2,1,0:T(8,128)(2,1)} %param.3) | copy-start | bytes 11010052
  0.7 21.5 %copy-start.1 = (f32[1,256,7168]{2,1,0:T(8,128)S(1)}, f32[1,256,7168]{2,1,0:T(8,128)}, u32[]{:S(2)}) copy-start(f32[1,256,7168]{2,1,0:T(8,128)} %param.4) | copy-start | bytes 22020100
  9.9 1.3 %collective-permute-start = (f32[256,32]{0,1:T(8,128)S(1)}, f32[256,32]{0,1:T(8,128)S(1)}, u32[]{:S(2)}, u32[]{:S(2)}) collective-permute-start(f32[256,32]{0,1:T(8,128)S(1)} %fusion.1), channel_id=1, source_target_pairs={{0,4},{4,0},{8,12},{12,8},{16,20},{20,16},{24,28},{28,24},{1,5},{5... | collective-permute-start | bytes 98312 | tf_op jit(solution)/shard_map/ppermute | solution.py:12
  11.1 3.7 %collective-permute-start.1 = (f32[256,32]{0,1:T(8,128)S(1)}, f32[256,32]{0,1:T(8,128)S(1)}, u32[]{:S(2)}, u32[]{:S(2)}) collective-permute-start(f32[256,32]{0,1:T(8,128)S(1)} %add.82), channel_id=1, source_target_pairs={{0,8},{4,12},{8,0},{12,4},{16,24},{20,28},{24,16},{28,20},{1,9},{5... | collective-permute-start | bytes 98312 | tf_op jit(solution)/shard_map/ppermute | solution.py:12
  13.5 2.8 %collective-permute-start.2 = (f32[256,32]{0,1:T(8,128)S(1)}, f32[256,32]{0,1:T(8,128)S(1)}, u32[]{:S(2)}, u32[]{:S(2)}) collective-permute-start(f32[256,32]{0,1:T(8,128)S(1)} %add.82), channel_id=1, source_target_pairs={{0,16},{4,20},{8,24},{12,28},{16,0},{20,4},{24,8},{28,12},{1,17},{... | collective-permute-start | bytes 98312 | tf_op jit(solution)/shard_map/ppermute | solution.py:12
  14.8 3.7 %collective-permute-start.3 = (f32[256,32]{0,1:T(8,128)S(1)}, f32[256,32]{0,1:T(8,128)S(1)}, u32[]{:S(2)}, u32[]{:S(2)}) collective-permute-start(f32[256,32]{0,1:T(8,128)S(1)} %add.82), channel_id=1, source_target_pairs={{0,24},{4,28},{8,16},{12,20},{16,8},{20,12},{24,0},{28,4},{1,25},{... | collective-permute-start | bytes 98312 | tf_op jit(solution)/shard_map/ppermute | solution.py:12
  18.4 16.0 %collective-permute-start.4 = (f32[256,32]{0,1:T(8,128)S(1)}, f32[256,32]{0,1:T(8,128)S(1)}, u32[]{:S(2)}, u32[]{:S(2)}) collective-permute-start(f32[256,32]{0,1:T(8,128)S(1)} %add_add_fusion), channel_id=1, source_target_pairs={{0,1},{1,0},{2,3},{3,2},{4,5},{5,4},{6,7},{7,6},{8,9},{9,8},{10,11... | collective-permute-start | bytes 98312 | tf_op jit(solution)/shard_map/ppermute | solution.py:12
  19.8 14.6 %collective-permute-start.5 = (f32[256,32]{0,1:T(8,128)S(1)}, f32[256,32]{0,1:T(8,128)S(1)}, u32[]{:S(2)}, u32[]{:S(2)}) collective-permute-start(f32[256,32]{0,1:T(8,128)S(1)} %add_add_fusion), channel_id=1, source_target_pairs={{0,2},{1,3},{2,0},{3,1},{4,6},{5,7},{6,4},{7,5},{8,10},{9,11},{10,... | collective-permute-start | bytes 98312 | tf_op jit(solution)/shard_map/ppermute | solution.py:12
  22.1 12.3 %collective-permute-start.6 = (f32[256,32]{0,1:T(8,128)S(1)}, f32[256,32]{0,1:T(8,128)S(1)}, u32[]{:S(2)}, u32[]{:S(2)}) collective-permute-start(f32[256,32]{0,1:T(8,128)S(1)} %add_add_fusion), channel_id=1, source_target_pairs={{0,3},{1,2},{2,1},{3,0},{4,7},{5,6},{6,5},{7,4},{8,11},{9,10},{10,... | collective-permute-start | bytes 98312 | tf_op jit(solution)/shard_map/ppermute | solution.py:12
  41.0 9.7 %collective-permute-start.7 = (f32[4,32,896]{2,1,0:T(8,128)S(1)}, f32[4,32,896]{2,1,0:T(8,128)S(1)}, u32[]{:S(2)}, u32[]{:S(2)}) collective-permute-start(f32[4,32,896]{2,1,0:T(8,128)S(1)} %dynamic-slice_bitcast_fusion), channel_id=1, source_target_pairs={{0,4},{4,0},{8,12},{12,8},{16,20},{20,16},{24,28},{28,24},{1,5},{5... | collective-permute-start | bytes 1376264 | tf_op jit(solution)/shard_map/ppermute | solution.py:12
  50.8 5.7 %collective-permute-start.10 = (f32[32,896]{1,0:T(8,128)S(1)}, f32[32,896]{1,0:T(8,128)S(1)}, u32[]{:S(2)}, u32[]{:S(2)}) collective-permute-start(f32[32,896]{1,0:T(8,128)S(1)} %get-tuple-element.9), channel_id=1, source_target_pairs={{0,24},{4,28},{8,16},{12,20},{16,8},{20,12},{24,0},{28,4},{1,25},{... | collective-permute-start | bytes 344072 | tf_op jit(solution)/shard_map/ppermute | solution.py:12
  50.9 7.2 %collective-permute-start.8 = (f32[32,896]{1,0:T(8,128)S(1)}, f32[32,896]{1,0:T(8,128)S(1)}, u32[]{:S(2)}, u32[]{:S(2)}) collective-permute-start(f32[32,896]{1,0:T(8,128)S(1)} %get-tuple-element.11), channel_id=1, source_target_pairs={{0,8},{4,12},{8,0},{12,4},{16,24},{20,28},{24,16},{28,20},{1,9},{5... | collective-permute-start | bytes 344072 | tf_op jit(solution)/shard_map/ppermute | solution.py:12
  52.3 7.0 %collective-permute-start.9 = (f32[32,896]{1,0:T(8,128)S(1)}, f32[32,896]{1,0:T(8,128)S(1)}, u32[]{:S(2)}, u32[]{:S(2)}) collective-permute-start(f32[32,896]{1,0:T(8,128)S(1)} %get-tuple-element.10), channel_id=1, source_target_pairs={{0,16},{4,20},{8,24},{12,28},{16,0},{20,4},{24,8},{28,12},{1,17},{... | collective-permute-start | bytes 344072 | tf_op jit(solution)/shard_map/ppermute | solution.py:12
  59.5 4.3 %collective-permute-start.11 = (f32[32,896]{1,0:T(8,128)S(1)}, f32[32,896]{1,0:T(8,128)S(1)}, u32[]{:S(2)}, u32[]{:S(2)}) collective-permute-start(f32[32,896]{1,0:T(8,128)S(1)} %convolution_multiply_fusion), channel_id=1, source_target_pairs={{0,8},{4,12},{8,0},{12,4},{16,24},{20,28},{24,16},{28,20},{1,9},{5... | collective-permute-start | bytes 344072 | tf_op jit(solution)/shard_map/ppermute | solution.py:12
  59.9 4.5 %collective-permute-start.12 = (f32[32,896]{1,0:T(8,128)S(1)}, f32[32,896]{1,0:T(8,128)S(1)}, u32[]{:S(2)}, u32[]{:S(2)}) collective-permute-start(f32[32,896]{1,0:T(8,128)S(1)} %convolution_multiply_fusion), channel_id=1, source_target_pairs={{0,16},{4,20},{8,24},{12,28},{16,0},{20,4},{24,8},{28,12},{1,17},{... | collective-permute-start | bytes 344072 | tf_op jit(solution)/shard_map/ppermute | solution.py:12
  59.9 6.1 %collective-permute-start.13 = (f32[32,896]{1,0:T(8,128)S(1)}, f32[32,896]{1,0:T(8,128)S(1)}, u32[]{:S(2)}, u32[]{:S(2)}) collective-permute-start(f32[32,896]{1,0:T(8,128)S(1)} %convolution_multiply_fusion), channel_id=1, source_target_pairs={{0,24},{4,28},{8,16},{12,20},{16,8},{20,12},{24,0},{28,4},{1,25},{... | collective-permute-start | bytes 344072 | tf_op jit(solution)/shard_map/ppermute | solution.py:12
  66.1 3.4 %collective-permute-start.14 = (f32[4,32,896]{2,1,0:T(8,128)S(1)}, f32[4,32,896]{2,1,0:T(8,128)S(1)}, u32[]{:S(2)}, u32[]{:S(2)}) collective-permute-start(f32[4,32,896]{2,1,0:T(8,128)S(1)} %pad_maximum_fusion.1), channel_id=1, source_target_pairs={{0,4},{4,0},{8,12},{12,8},{16,20},{20,16},{24,28},{28,24},{1,5},{5... | collective-permute-start | bytes 1376264 | tf_op jit(solution)/shard_map/ppermute | solution.py:12
  68.2 10.8 %copy-start.4 = (f32[256,32]{0,1:T(8,128)}, f32[256,32]{0,1:T(8,128)S(1)}, u32[]{:S(2)}) copy-start(f32[256,32]{0,1:T(8,128)S(1)} %fusion.16) | copy-start | bytes 98308
  70.7 8.4 %copy-start.3 = (f32[32,7168]{1,0:T(8,128)}, f32[32,7168]{1,0:T(8,128)S(1)}, u32[]{:S(2)}) copy-start(f32[32,7168]{1,0:T(8,128)S(1)} %reshape.22) | copy-start | bytes 2752516

commit v2 on v1

v2 whole, which is shorter than its diff:
```python
import functools

import jax
import jax.numpy as jnp
from jax import lax
from jax.experimental import pallas as pl
from jax.experimental.pallas import tpu as pltpu
from jax.sharding import PartitionSpec as P

F32, BF16 = jnp.float32, jnp.bfloat16
HIGHEST = lax.Precision.HIGHEST
ANY = pl.BlockSpec(memory_space=pl.ANY)
VMEM = pl.BlockSpec(memory_space=pltpu.VMEM)


def split(x):
    high = x.astype(BF16)
    return high, (x - high.astype(F32)).astype(BF16)


def dot(a, b, a_dim, b_dim, precision=None):
    return lax.dot_general(a, b, (((a_dim,), (b_dim,)), ((), ())), precision=precision, preferred_element_type=F32)


def params(mebibytes):
    return pltpu.CompilerParams(vmem_limit_bytes=mebibytes << 20)


def cost(flops, bytes_accessed):
    return pl.CostEstimate(flops=int(flops), bytes_accessed=int(bytes_accessed), transcendentals=0)


def left_kernel(chunk, gradient, feedback, right, combined, high, low, left, gradient_buf, right_buf, sems):
    rows, columns = gradient.shape
    rank = right.shape[0]
    blocks = [pl.ds(i * chunk, chunk) for i in range(columns // chunk)]
    copies = []
    for i, at in enumerate(blocks):
        group = [
            pltpu.make_async_copy(gradient.at[:, at], gradient_buf.at[:, at], sems.at[0, i]),
            pltpu.make_async_copy(feedback.at[:, at], combined.at[:, at], sems.at[1, i]),
            pltpu.make_async_copy(right.at[:, at], right_buf.at[:, at], sems.at[2, i]),
        ]
        for copy in group:
            copy.start()
        copies.append(group)
    padded = combined.shape[1]
    if padded > columns:
        rest = pl.ds(columns, padded - columns)
        combined[:, rest] = jnp.zeros((rows, padded - columns), F32)
        high[:, rest] = jnp.zeros((rows, padded - columns), BF16)
        low[:, rest] = jnp.zeros((rows, padded - columns), BF16)
    total = jnp.zeros((rows, 2 * rank), F32)
    for at, group in zip(blocks, copies):
        for copy in group:
            copy.wait()
        both = jnp.concatenate(split(right_buf[:, at]), axis=0)
        c = combined[:, at] + gradient_buf[:, at].astype(F32)
        c_high, c_low = split(c)
        combined[:, at] = c
        high[:, at] = c_high
        low[:, at] = c_low
        total += dot(c_high, both, 1, 1) + dot(c_low, both, 1, 1)
    left[...] = (total[:, :rank] + total[:, rank:]).T


def left_product(gradient, feedback, right, padded):
    rows, columns = gradient.shape
    rank = right.shape[0]
    chunk = 512 if columns % 512 == 0 else 128
    return pl.pallas_call(
        functools.partial(left_kernel, chunk),
        in_specs=[ANY] * 3,
        out_specs=[VMEM] * 4,
        out_shape=[
            pltpu.VMEM((rows, padded), F32),
            pltpu.VMEM((rows, padded), BF16),
            pltpu.VMEM((rows, padded), BF16),
            pltpu.VMEM((rank, rows), F32),
        ],
        scratch_shapes=[
            pltpu.VMEM((rows, columns), BF16),
            pltpu.VMEM((rank, columns), F32),
            pltpu.SemaphoreType.DMA((3, columns // chunk)),
        ],
        compiler_params=params(16),
        cost_estimate=cost(8 * rows * columns * rank, 6 * rows * columns),
        name="left",
    )(gradient, feedback, right)


def right_kernel(index, left, high, low, pieces):
    chips, rank, width = pieces.shape
    half = chips * width
    block = 512 if half % 512 == 0 else 128
    both = jnp.concatenate(split(left[...]), axis=0)
    for i in range(half // block):
        at = pl.ds(pl.multiple_of(index[0] * half + i * block, block), block)
        total = dot(both, high[:, at], 1, 0) + dot(both, low[:, at], 1, 0)
        total = total[:rank] + total[rank:]
        start = i * block
        while start < (i + 1) * block:
            piece = start // width
            stop = min((i + 1) * block, (piece + 1) * width)
            pieces[piece, :, start - piece * width : stop - piece * width] = total[:, start - i * block : stop - i * block]
            start = stop


def right_product(index, left, high, low, chips, width):
    rank, rows = left.shape
    return pl.pallas_call(
        right_kernel,
        in_specs=[pl.BlockSpec(memory_space=pltpu.SMEM)] + [VMEM] * 3,
        out_specs=VMEM,
        out_shape=pltpu.VMEM((chips, rank, width), F32),
        compiler_params=params(8),
        cost_estimate=cost(8 * rows * chips * width * rank, 4 * rows * chips * width),
        name="right",
    )(index.reshape(1), left, high, low)


def factor_kernel(left, inverse, factor, stacked):
    rank, rows = left.shape
    values = left[...]
    gram = dot(values, values, 1, 1, HIGHEST)
    row = lax.broadcasted_iota(jnp.int32, (rank, rank), 0)
    column = lax.broadcasted_iota(jnp.int32, (rank, rank), 1)
    unit = (row == column).astype(F32)
    wide = jnp.concatenate([gram, unit], axis=1)
    row_of = lax.broadcasted_iota(jnp.int32, (rank, 1), 0)
    for j in range(rank - 1):
        pivot = wide[j : j + 1, :]
        scaled = pivot * (1.0 / pivot[:, j : j + 1])
        wide = wide - jnp.where(row_of > j, wide[:, j : j + 1], 0.0) * scaled
    diagonal = jnp.sum(wide[:, :rank] * unit, axis=1, keepdims=True)
    inv = wide[:, rank:] * (1.0 / jnp.sqrt(diagonal))
    inverse[...] = inv
    q = dot(inv, values, 1, 0, HIGHEST)
    factor[...] = q
    q_high, q_low = (part.astype(F32) for part in split(q))
    stacked[...] = jnp.concatenate([q_high, q_low, q_high, q_low], axis=0).T.astype(BF16)


def factors(left):
    rank, rows = left.shape
    return pl.pallas_call(
        factor_kernel,
        in_specs=[VMEM],
        out_specs=[VMEM] * 3,
        out_shape=[
            pltpu.VMEM((rank, rank), F32),
            pltpu.VMEM((rank, rows), F32),
            pltpu.VMEM((rows, 4 * rank), BF16),
        ],
        compiler_params=params(8),
        cost_estimate=cost(2e9, 1e6),
        name="factor",
    )(left)


def feedback_kernel(aliased, columns, index, stacked, pieces, combined, *refs):
    feedback, right, feedback_buf, sems = refs[2 * aliased :]
    rank = pieces[0].shape[-2]
    chips, rows, width = feedback_buf.shape
    whole = combined.shape[1] == columns
    copies = []
    for k in range(chips):
        place = index[0] * chips + (index[1] ^ k)
        at = pl.ds(pl.multiple_of(place * width, 128), width)
        piece = pieces[k]
        piece_high, piece_low = split(piece[...])
        four = jnp.concatenate([piece_high, piece_high, piece_low, piece_low], axis=0)
        feedback_buf[k] = combined[:, at] - dot(stacked[...], four, 1, 0)
        copies.append(
            (
                place * width < columns,
                pltpu.make_async_copy(feedback_buf.at[k], feedback.at[:, at], sems.at[0, k]),
                pltpu.make_async_copy(piece, right.at[:, at], sems.at[1, k]),
            )
        )
        start_or_wait(copies[-1], whole, "start")
    for copy in copies:
        start_or_wait(copy, whole, "wait")


def start_or_wait(copy, whole, action):
    inside, *both = copy

    def run():
        for one in both:
            getattr(one, action)()

    if whole:
        run()
    else:
        pl.when(inside)(run)


def new_feedback(index, stacked, pieces, combined, columns, before=()):
    rows = combined.shape[0]
    separate = isinstance(pieces, list)
    chips = len(pieces) if separate else pieces.shape[0]
    rank, width = (pieces[0] if separate else pieces).shape[-2:]
    given = pieces if separate else [pieces]

    def kernel(index, stacked, *refs):
        mine = refs[: len(given)]
        parts = list(mine) if separate else [mine[0].at[k] for k in range(chips)]
        feedback_kernel(len(before) // 2, columns, index, stacked, parts, *refs[len(given) :])

    return pl.pallas_call(
        kernel,
        in_specs=[pl.BlockSpec(memory_space=pltpu.SMEM)] + [VMEM] * (2 + len(given)) + [ANY] * len(before),
        out_specs=[ANY] * 2,
        out_shape=[jax.ShapeDtypeStruct((rows, columns), F32), jax.ShapeDtypeStruct((rank, columns), F32)],
        input_output_aliases={3 + len(given) + i: i for i in range(len(before))},
        scratch_shapes=[
            pltpu.VMEM((chips, rows, width), F32),
            pltpu.SemaphoreType.DMA((2, chips)),
        ],
        compiler_params=params(16),
        cost_estimate=cost(8 * rows * chips * width * rank, 4 * rows * chips * width),
        name="feedback",
    )(index, stacked, *given, combined, *before)


def swap(x, axis, mask):
    size = lax.axis_size(axis)
    return lax.ppermute(x, axis, [(i, i ^ mask) for i in range(size)])


def tree(terms):
    while len(terms) > 1:
        terms = [a + b for a, b in zip(terms[::2], terms[1::2])]
    return terms[0]


def sum_over(x, axis, low, high):
    while low < high:
        step = min(2, high - low)
        x = tree([x] + [swap(x, axis, k << low) for k in range(1, 1 << step)])
        low += step
    return x


def bits(axis):
    size = lax.axis_size(axis)
    assert size & (size - 1) == 0
    return size.bit_length() - 1


def pick(x, index):
    return lax.dynamic_index_in_dim(x, index, 0, keepdims=False)


def per_device(gradient, feedback, right_factor):
    gradient, feedback = gradient[0], feedback[0]
    columns = gradient.shape[1]
    replicas = lax.axis_size("dp")
    me = lax.axis_index("dp")
    core, chip = me % 2, me // 2
    chips = replicas // 2
    width = -(-columns // (replicas * 128)) * 128
    assert columns % width == 0

    combined, high, low, left = left_product(gradient, feedback, right_factor.T, replicas * width)
    left = sum_over(left, "dp", 0, 1)
    left = sum_over(left, "dp", 1, bits("dp"))
    left = sum_over(left, "tensor", 0, bits("tensor")) / replicas

    theirs = swap(right_product(1 - core, left, high, low, chips, width), "dp", 1)
    half = right_product(core, left, high, low, chips, width) + theirs
    own = tree([pick(half, chip)] + [swap(pick(half, chip ^ k), "dp", 2 * k) for k in range(1, chips)])

    inverse, factor, stacked = factors(left)
    own = jnp.dot(inverse, own, precision=HIGHEST, preferred_element_type=F32) / replicas

    got = [own] + [swap(own, "dp", 2 * k) for k in range(1, chips)]
    other = swap(jnp.stack(got), "dp", 1)
    place = jnp.stack([core, chip])
    outs = new_feedback(place, stacked, got, combined, columns)
    place = jnp.stack([1 - core, chip])
    outs = new_feedback(place, stacked, other, combined, columns, tuple(outs))
    return (outs[0][None], factor.T, outs[1].T)


def solution(mesh):
    return jax.shard_map(
        per_device,
        mesh=mesh,
        in_specs=(P("dp", None, "tensor"), P("dp", None, "tensor"), P("tensor", None)),
        out_specs=(P("dp", None, "tensor"), P(), P("tensor", None)),
        check_vma=False,
    )
```

time: 79.6 us -> 72.6 us (0.912)
  matrix products: 23.5 us -> 0.25 us
  Pallas kernels: 0 us -> 16.6 us
  local copies, waits for them, and re-layouts: 10.7 us -> 21.8 us
  other arithmetic: 10.9 us -> 0.29 us
  starting transfers between devices: 17.7 us -> 16.6 us
    dot_general x6 -> x1, matrix products: 23.3 us -> 0.25 us  [per_device(): jnp.dot(inverse, own, precision=HIGHEST, preferred_element_type=F32)]
    unnamed x10 -> x25, local copies, waits for them, and re-layouts: 1.18 us -> 21.7 us
    pallas_call x0 -> x6, Pallas kernels: none -> 16.6 us  [the longest x1 6.31 us: left_product(): pl.pallas_call(functools.partial(left_kernel, chunk), in_specs=[ANY] * 3,...]
    dot_general x2 -> x0, local copies, waits for them, and re-layouts: 8.46 us -> none  [the longest x1 8.39 us: per_device(): lax.dot_general(left, combined, (((0,), (0,)), ((), ())), precision=HIGH,...]
    another operation x8 -> x3, other arithmetic: 6.82 us -> 0.18 us  [the longest x1 0.07 us: per_device(): place = jnp.stack([1 - core, chip])]
    dot_general x1 -> x0, other arithmetic: 3.91 us -> none  [per_device(): lax.dot_general(left, combined, (((0,), (0,)), ((), ())), precision=HIGH,...]
    ppermute x15, starting transfers between devices: 17.7 us -> 16.6 us  [swap(): return lax.ppermute(x, axis, [(i, i ^ mask) for i in range(size)])]
  transfers between devices with their start and end apart: 15 -> 15, of which waited for: 10 -> 9; matrix products, arithmetic and copies ran while one was open for 25% -> 1% of each run, Pallas kernels for 0% -> 9%
where the time goes in v2:
time: 72.6 us; the launch traced here: 72.2 us
  local copies, waits for them, and re-layouts  21.8 us (30%)
  Pallas kernels  16.6 us (23%)
  starting transfers between devices  16.6 us (23%)
  waiting for transfers between devices  15.9 us (22%)
  between operations  0.76 us (1%)
    unnamed x25, local copies, waits for them, and re-layouts  21.7 us
    ppermute x15, starting transfers between devices, swap(): return lax.ppermute(x, axis, [(i, i ^ mask) for i in range(size)])  16.6 us
    ppermute x15, waiting for transfers between devices, swap(): return lax.ppermute(x, axis, [(i, i ^ mask) for i in range(size)])  15.9 us
    pallas_call x1, Pallas kernels, left_product(): pl.pallas_call(functools.partial(left_kernel, chunk), in_specs=[ANY] * 3,...  6.31 us
    pallas_call x2, Pallas kernels, new_feedback(): pl.pallas_call(kernel, in_specs=[pl.BlockSpec(memory_space=pltpu.SMEM)] +...  5.73 us
    pallas_call x1, Pallas kernels, factors(): pl.pallas_call(factor_kernel, in_specs=[VMEM], out_specs=[VMEM] * 3, out_...  3.12 us
    pallas_call x2, Pallas kernels, right_product(): pl.pallas_call(right_kernel, in_specs=[pl.BlockSpec(memory_space=pltpu.SM...  1.47 us
  transfers between devices with their start and end apart: 15, of which 9 were waited for; matrix products, arithmetic and copies ran while one was open for 1% of the time, Pallas kernels for 9%

profile of v2, /device:TPU:1, one launch (start us, length us, event | category | flops | bytes accessed | tf_op | source)
XLA Modules:
  0.0 72.2 jit_solution(14013703885701160006)
XLA Ops:
  0.6 3.1 %copy-done.7 = f32[1,256,7168]{2,1,0:T(8,128)S(1)} copy-done((f32[1,256,7168]{2,1,0:T(8,128)S(1)}, f32[1,256,7168]{2,1,0:T(8,128)}, u32[]{:S(2)}) %copy-start.7) | copy-done | bytes 7340056
  3.7 2.0 %copy-done.8 = bf16[1,256,7168]{2,1,0:T(8,128)(2,1)S(1)} copy-done((bf16[1,256,7168]{2,1,0:T(8,128)(2,1)S(1)}, bf16[1,256,7168]{2,1,0:T(8,128)(2,1)}, u32[]{:S(2)}) %copy-start.8) | copy-done | bytes 3670040
  5.8 1.2 %copy-done.9 = f32[7168,32]{0,1:T(8,128)S(1)} copy-done((f32[7168,32]{0,1:T(8,128)S(1)}, f32[7168,32]{0,1:T(8,128)}, u32[]{:S(2)}) %copy-start.9) | copy-done | bytes 917528
  7.0 6.3 %left.1 = (f32[256,7168]{1,0:T(8,128)S(1)}, bf16[256,7168]{1,0:T(8,128)(2,1)S(1)}, bf16[256,7168]{1,0:T(8,128)(2,1)S(1)}, f32[32,256]{1,0:T(8,128)S(1)}) custom-call(bf16[256,7168]{1,0:T(8,128)(2,1)S(1)} %bitcast.29, f32[256,7168]{1,0:T(8,128)S(1)} %bitcast.28, f32[32,7168]{1,0:T(8,128)S(1)} %bitcast.31), custom_call_target="tpu_custom_call" | custom-call | flops 469762048 | bytes 11010048 | tf_op jit(solution)/shard_map/left/pallas_call | solution.py:71
  13.3 0.0 copy-start
  13.3 3.0 %copy-done = f32[256,7168]{1,0:T(8,128)} copy-done((f32[256,7168]{1,0:T(8,128)}, f32[256,7168]{1,0:T(8,128)S(1)}, u32[]{:S(2)}) %copy-start) | copy-done | bytes 7340056
  16.3 1.8 %copy-done.1 = bf16[256,7168]{1,0:T(8,128)(2,1)} copy-done((bf16[256,7168]{1,0:T(8,128)(2,1)}, bf16[256,7168]{1,0:T(8,128)(2,1)S(1)}, u32[]{:S(2)}) %copy-start.1) | copy-done | bytes 3670040
  18.1 1.8 %copy-done.4 = bf16[256,7168]{1,0:T(8,128)(2,1)} copy-done((bf16[256,7168]{1,0:T(8,128)(2,1)}, bf16[256,7168]{1,0:T(8,128)(2,1)S(1)}, u32[]{:S(2)}) %copy-start.4) | copy-done | bytes 3670040
  19.9 0.1 collective-permute-start
  20.0 1.2 %collective-permute-done = f32[32,256]{1,0:T(8,128)S(1)} collective-permute-done((f32[32,256]{1,0:T(8,128)S(1)}, f32[32,256]{1,0:T(8,128)S(1)}, u32[]{:S(2)}, u32[]{:S(2)}) %collective-permute-start) | collective-permute-done | bytes 32800 | tf_op jit(solution)/shard_map/ppermute | solution.py:229
  21.2 3.3 %collective-permute-start.3 = (f32[32,256]{1,0:T(8,128)S(1)}, f32[32,256]{1,0:T(8,128)S(1)}, u32[]{:S(2)}, u32[]{:S(2)}) collective-permute-start(f32[32,256]{1,0:T(8,128)S(1)} %add.52), channel_id=1, source_target_pairs={{0,24},{4,28},{8,16},{12,20},{16,8},{20,12},{24,0},{28,4},{1,25},{... | collective-permute-start | bytes 98312 | tf_op jit(solution)/shard_map/ppermute | solution.py:229
  24.5 0.2 collective-permute-start.2
  24.7 0.1 collective-permute-start.1
  24.8 0.9 %collective-permute-done.3 = f32[32,256]{1,0:T(8,128)S(1)} collective-permute-done((f32[32,256]{1,0:T(8,128)S(1)}, f32[32,256]{1,0:T(8,128)S(1)}, u32[]{:S(2)}, u32[]{:S(2)}) %collective-permute-start.3) | collective-permute-done | bytes 32800 | tf_op jit(solution)/shard_map/ppermute | solution.py:229
  25.8 1.5 %collective-permute-done.2 = f32[32,256]{1,0:T(8,128)S(1)} collective-permute-done((f32[32,256]{1,0:T(8,128)S(1)}, f32[32,256]{1,0:T(8,128)S(1)}, u32[]{:S(2)}, u32[]{:S(2)}) %collective-permute-start.2) | collective-permute-done | bytes 32800 | tf_op jit(solution)/shard_map/ppermute | solution.py:229
  27.2 0.2 collective-permute-done.1
  27.5 3.4 %collective-permute-start.6 = (f32[32,256]{1,0:T(8,128)S(1)}, f32[32,256]{1,0:T(8,128)S(1)}, u32[]{:S(2)}, u32[]{:S(2)}) collective-permute-start(f32[32,256]{1,0:T(8,128)S(1)} %add_add_fusion), channel_id=1, source_target_pairs={{0,3},{1,2},{2,1},{3,0},{4,7},{5,6},{6,5},{7,4},{8,11},{9,10},{10,... | collective-permute-start | bytes 98312 | tf_op jit(solution)/shard_map/ppermute | solution.py:229
  30.9 0.0 collective-permute-start.5
  30.9 0.4 collective-permute-start.4
  31.2 0.9 %collective-permute-done.6 = f32[32,256]{1,0:T(8,128)S(1)} collective-permute-done((f32[32,256]{1,0:T(8,128)S(1)}, f32[32,256]{1,0:T(8,128)S(1)}, u32[]{:S(2)}, u32[]{:S(2)}) %collective-permute-start.6) | collective-permute-done | bytes 32800 | tf_op jit(solution)/shard_map/ppermute | solution.py:229
  32.2 2.7 %collective-permute-done.5 = f32[32,256]{1,0:T(8,128)S(1)} collective-permute-done((f32[32,256]{1,0:T(8,128)S(1)}, f32[32,256]{1,0:T(8,128)S(1)}, u32[]{:S(2)}, u32[]{:S(2)}) %collective-permute-start.5) | collective-permute-done | bytes 32800 | tf_op jit(solution)/shard_map/ppermute | solution.py:229
  34.9 0.0 collective-permute-done.4
  34.9 2.0 %copy-done.2 = bf16[256,7168]{1,0:T(8,128)(2,1)S(1)} copy-done((bf16[256,7168]{1,0:T(8,128)(2,1)S(1)}, bf16[256,7168]{1,0:T(8,128)(2,1)}, u32[]{:S(2)}) %copy-start.2) | copy-done | bytes 3670040
  37.0 2.0 %copy-done.5 = bf16[256,7168]{1,0:T(8,128)(2,1)S(1)} copy-done((bf16[256,7168]{1,0:T(8,128)(2,1)S(1)}, bf16[256,7168]{1,0:T(8,128)(2,1)}, u32[]{:S(2)}) %copy-start.5) | copy-done | bytes 3670040
  39.0 0.7 %right.3 = f32[4,32,896]{2,1,0:T(8,128)S(1)} custom-call(s32[1]{0:T(128)} %bitcast.index, f32[32,256]{1,0:T(8,128)S(1)} %add_multiply_fusion.left, bf16[256,7168]{1,0:T(8,128)(2,1)S(1)} %copy-done.2, bf16[256,7168]{1,0:T(8,128)(2,1)S(1)} %copy-done.5), custom_call_target="tpu_custom_call" | custom-call | flops 234881024 | bytes 3670016 | tf_op jit(solution)/shard_map/right/pallas_call | solution.py:111
  39.8 3.1 %collective-permute-start.7 = (f32[4,32,896]{2,1,0:T(8,128)S(1)}, f32[4,32,896]{2,1,0:T(8,128)S(1)}, u32[]{:S(2)}, u32[]{:S(2)}) collective-permute-start(f32[4,32,896]{2,1,0:T(8,128)S(1)} %right.3), channel_id=1, source_target_pairs={{0,4},{4,0},{8,12},{12,8},{16,20},{20,16},{24,28},{28,24},{1,5},{5... | collective-permute-start | bytes 1376264 | tf_op jit(solution)/shard_map/ppermute | solution.py:229
  42.9 2.0 %copy-done.3 = bf16[256,7168]{1,0:T(8,128)(2,1)S(1)} copy-done((bf16[256,7168]{1,0:T(8,128)(2,1)S(1)}, bf16[256,7168]{1,0:T(8,128)(2,1)}, u32[]{:S(2)}) %copy-start.3) | copy-done | bytes 3670040
  44.9 2.0 %copy-done.6 = bf16[256,7168]{1,0:T(8,128)(2,1)S(1)} copy-done((bf16[256,7168]{1,0:T(8,128)(2,1)S(1)}, bf16[256,7168]{1,0:T(8,128)(2,1)}, u32[]{:S(2)}) %copy-start.6) | copy-done | bytes 3670040
  46.9 0.7 %right.2 = f32[4,32,896]{2,1,0:T(8,128)S(1)} custom-call(s32[1]{0:T(128)} %bitcast.5.index, f32[32,256]{1,0:T(8,128)S(1)} %add_multiply_fusion.left, bf16[256,7168]{1,0:T(8,128)(2,1)S(1)} %copy-done.3, bf16[256,7168]{1,0:T(8,128)(2,1)S(1)} %copy-done.6), custom_call_target="tpu_custom_call" | custom-call | flops 234881024 | bytes 3670016 | tf_op jit(solution)/shard_map/right/pallas_call | solution.py:111
  47.7 0.1 add.59
  47.8 0.0 slice-start.1
  47.8 1.3 %collective-permute-start.10 = (f32[32,896]{1,0:T(8,128)S(1)}, f32[32,896]{1,0:T(8,128)S(1)}, u32[]{:S(2)}, u32[]{:S(2)}) collective-permute-start(f32[32,896]{1,0:T(8,128)S(1)} %get-tuple-element.25), channel_id=1, source_target_pairs={{0,24},{4,28},{8,16},{12,20},{16,8},{20,12},{24,0},{28,4},{1,25},{... | collective-permute-start | bytes 344072 | tf_op jit(solution)/shard_map/ppermute | solution.py:229
  49.1 0.2 collective-permute-start.9
  49.3 1.2 %collective-permute-start.8 = (f32[32,896]{1,0:T(8,128)S(1)}, f32[32,896]{1,0:T(8,128)S(1)}, u32[]{:S(2)}, u32[]{:S(2)}) collective-permute-start(f32[32,896]{1,0:T(8,128)S(1)} %get-tuple-element.27), channel_id=1, source_target_pairs={{0,8},{4,12},{8,0},{12,4},{16,24},{20,28},{24,16},{28,20},{1,9},{5... | collective-permute-start | bytes 344072 | tf_op jit(solution)/shard_map/ppermute | solution.py:229
  50.5 3.1 %factor.1 = (f32[32,32]{1,0:T(8,128)S(1)}, f32[32,256]{1,0:T(8,128)S(1)}, bf16[256,128]{1,0:T(8,128)(2,1)S(1)}) custom-call(f32[32,256]{1,0:T(8,128)S(1)} %add_multiply_fusion.left), custom_call_target="tpu_custom_call" | custom-call | flops 2000000000 | bytes 1000000 | tf_op jit(solution)/shard_map/factor/pallas_call | solution.py:146
  53.7 2.7 %collective-permute-done.9 = f32[32,896]{1,0:T(8,128)S(1)} collective-permute-done((f32[32,896]{1,0:T(8,128)S(1)}, f32[32,896]{1,0:T(8,128)S(1)}, u32[]{:S(2)}, u32[]{:S(2)}) %collective-permute-start.9) | collective-permute-done | bytes 114720 | tf_op jit(solution)/shard_map/ppermute | solution.py:229
  56.4 0.2 convolution_multiply_fusion.refs_0_
  56.6 1.3 %collective-permute-start.13 = (f32[32,896]{1,0:T(8,128)S(1)}, f32[32,896]{1,0:T(8,128)S(1)}, u32[]{:S(2)}, u32[]{:S(2)}) collective-permute-start(f32[32,896]{1,0:T(8,128)S(1)} %convolution_multiply_fusion.refs_0_), channel_id=1, source_target_pairs={{0,24},{4,28},{8,16},{12,20},{16,8},{20,12},{24,0},{28,4},{1,25},{... | collective-permute-start | bytes 344072 | tf_op jit(solution)/shard_map/ppermute | solution.py:229
  57.9 0.2 collective-permute-start.12
  58.1 1.2 %collective-permute-start.11 = (f32[32,896]{1,0:T(8,128)S(1)}, f32[32,896]{1,0:T(8,128)S(1)}, u32[]{:S(2)}, u32[]{:S(2)}) collective-permute-start(f32[32,896]{1,0:T(8,128)S(1)} %convolution_multiply_fusion.refs_0_), channel_id=1, source_target_pairs={{0,8},{4,12},{8,0},{12,4},{16,24},{20,28},{24,16},{28,20},{1,9},{5... | collective-permute-start | bytes 344072 | tf_op jit(solution)/shard_map/ppermute | solution.py:229
  59.3 2.4 %collective-permute-done.13.refs_3_ = f32[32,896]{1,0:T(8,128)S(1)} collective-permute-done((f32[32,896]{1,0:T(8,128)S(1)}, f32[32,896]{1,0:T(8,128)S(1)}, u32[]{:S(2)}, u32[]{:S(2)}) %collective-permute-start.13) | collective-permute-done | bytes 114720 | tf_op jit(solution)/shard_map/ppermute | solution.py:229
  61.7 3.4 %collective-permute-done.12.refs_2_ = f32[32,896]{1,0:T(8,128)S(1)} collective-permute-done((f32[32,896]{1,0:T(8,128)S(1)}, f32[32,896]{1,0:T(8,128)S(1)}, u32[]{:S(2)}, u32[]{:S(2)}) %collective-permute-start.12) | collective-permute-done | bytes 114720 | tf_op jit(solution)/shard_map/ppermute | solution.py:229
  65.1 0.6 collective-permute-start.14
  65.7 0.1 pad_add_fusion.index
  65.8 0.1 pad_add_fusion.1.index
  65.8 0.6 copy.10
  66.5 2.9 %feedback.2 = (f32[256,7168]{1,0:T(8,128)}, f32[32,7168]{1,0:T(8,128)}) custom-call(s32[2]{0:T(128)S(1)} %pad_add_fusion.1.index, bf16[256,128]{1,0:T(8,128)(2,1)S(1)} %get-tuple-element.15.stacked, f32[32,896]{1,0:T(8,128)S(1)} %convolution_multiply_fusion.refs_0_, f32[32,896]{1,0:T(8,128)S(1)} %collective-permute-done.11.refs_1_, ...), custom_call_target="tpu_custom_call" | custom-call | flops 234881024 | bytes 3670016 | tf_op jit(solution)/shard_map/feedback/pallas_call | solution.py:211
  69.4 2.9 %feedback.3 = (f32[256,7168]{1,0:T(8,128)}, f32[32,7168]{1,0:T(8,128)}) custom-call(s32[2]{0:T(128)S(1)} %pad_add_fusion.index, bf16[256,128]{1,0:T(8,128)(2,1)S(1)} %get-tuple-element.15.stacked, f32[4,32,896]{2,1,0:T(8,128)S(1)} %collective-permute-done.14.refs_0_, f32[256,7168]{1,0:T(8,128)S(1)} %bitcast.27, ...), custom_call_target="tpu_custom_call", output_to_operand_aliasing={{0}: (4, {}), {1}: (5, {})} | custom-call | flops 234881024 | bytes 3670016 | tf_op jit(solution)/shard_map/feedback/pallas_call | solution.py:211
  (23 shorter events, 0.1 us)
Async XLA Ops:
  0.6 3.1 %copy-start.7 = (f32[1,256,7168]{2,1,0:T(8,128)S(1)}, f32[1,256,7168]{2,1,0:T(8,128)}, u32[]{:S(2)}) copy-start(f32[1,256,7168]{2,1,0:T(8,128)} %param.4) | copy-start | bytes 22020100
  3.7 2.0 %copy-start.8 = (bf16[1,256,7168]{2,1,0:T(8,128)(2,1)S(1)}, bf16[1,256,7168]{2,1,0:T(8,128)(2,1)}, u32[]{:S(2)}) copy-start(bf16[1,256,7168]{2,1,0:T(8,128)(2,1)} %param.3) | copy-start | bytes 11010052
  5.8 1.2 %copy-start.9 = (f32[7168,32]{0,1:T(8,128)S(1)}, f32[7168,32]{0,1:T(8,128)}, u32[]{:S(2)}) copy-start(f32[7168,32]{0,1:T(8,128)} %param.5) | copy-start | bytes 2752516
  13.3 3.1 %copy-start = (f32[256,7168]{1,0:T(8,128)}, f32[256,7168]{1,0:T(8,128)S(1)}, u32[]{:S(2)}) copy-start(f32[256,7168]{1,0:T(8,128)S(1)} %get-tuple-element.19.refs_4_.refs_1_) | copy-start | bytes 22020100
  16.3 1.8 %copy-start.1 = (bf16[256,7168]{1,0:T(8,128)(2,1)}, bf16[256,7168]{1,0:T(8,128)(2,1)S(1)}, u32[]{:S(2)}) copy-start(bf16[256,7168]{1,0:T(8,128)(2,1)S(1)} %get-tuple-element.17.high) | copy-start | bytes 11010052
  18.1 1.8 %copy-start.4 = (bf16[256,7168]{1,0:T(8,128)(2,1)}, bf16[256,7168]{1,0:T(8,128)(2,1)S(1)}, u32[]{:S(2)}) copy-start(bf16[256,7168]{1,0:T(8,128)(2,1)S(1)} %get-tuple-element.18.low) | copy-start | bytes 11010052
  19.9 1.2 %collective-permute-start = (f32[32,256]{1,0:T(8,128)S(1)}, f32[32,256]{1,0:T(8,128)S(1)}, u32[]{:S(2)}, u32[]{:S(2)}) collective-permute-start(f32[32,256]{1,0:T(8,128)S(1)} %get-tuple-element.14), channel_id=1, source_target_pairs={{0,4},{4,0},{8,12},{12,8},{16,20},{20,16},{24,28},{28,24},{1,5},{5... | collective-permute-start | bytes 98312 | tf_op jit(solution)/shard_map/ppermute | solution.py:229
  21.2 4.6 %collective-permute-start.3 = (f32[32,256]{1,0:T(8,128)S(1)}, f32[32,256]{1,0:T(8,128)S(1)}, u32[]{:S(2)}, u32[]{:S(2)}) collective-permute-start(f32[32,256]{1,0:T(8,128)S(1)} %add.52), channel_id=1, source_target_pairs={{0,24},{4,28},{8,16},{12,20},{16,8},{20,12},{24,0},{28,4},{1,25},{... | collective-permute-start | bytes 98312 | tf_op jit(solution)/shard_map/ppermute | solution.py:229
  24.5 2.8 %collective-permute-start.2 = (f32[32,256]{1,0:T(8,128)S(1)}, f32[32,256]{1,0:T(8,128)S(1)}, u32[]{:S(2)}, u32[]{:S(2)}) collective-permute-start(f32[32,256]{1,0:T(8,128)S(1)} %add.52), channel_id=1, source_target_pairs={{0,16},{4,20},{8,24},{12,28},{16,0},{20,4},{24,8},{28,12},{1,17},{... | collective-permute-start | bytes 98312 | tf_op jit(solution)/shard_map/ppermute | solution.py:229
  24.7 2.8 %collective-permute-start.1 = (f32[32,256]{1,0:T(8,128)S(1)}, f32[32,256]{1,0:T(8,128)S(1)}, u32[]{:S(2)}, u32[]{:S(2)}) collective-permute-start(f32[32,256]{1,0:T(8,128)S(1)} %add.52), channel_id=1, source_target_pairs={{0,8},{4,12},{8,0},{12,4},{16,24},{20,28},{24,16},{28,20},{1,9},{5... | collective-permute-start | bytes 98312 | tf_op jit(solution)/shard_map/ppermute | solution.py:229
  27.5 4.7 %collective-permute-start.6 = (f32[32,256]{1,0:T(8,128)S(1)}, f32[32,256]{1,0:T(8,128)S(1)}, u32[]{:S(2)}, u32[]{:S(2)}) collective-permute-start(f32[32,256]{1,0:T(8,128)S(1)} %add_add_fusion), channel_id=1, source_target_pairs={{0,3},{1,2},{2,1},{3,0},{4,7},{5,6},{6,5},{7,4},{8,11},{9,10},{10,... | collective-permute-start | bytes 98312 | tf_op jit(solution)/shard_map/ppermute | solution.py:229
  30.9 4.1 %collective-permute-start.5 = (f32[32,256]{1,0:T(8,128)S(1)}, f32[32,256]{1,0:T(8,128)S(1)}, u32[]{:S(2)}, u32[]{:S(2)}) collective-permute-start(f32[32,256]{1,0:T(8,128)S(1)} %add_add_fusion), channel_id=1, source_target_pairs={{0,2},{1,3},{2,0},{3,1},{4,6},{5,7},{6,4},{7,5},{8,10},{9,11},{10,... | collective-permute-start | bytes 98312 | tf_op jit(solution)/shard_map/ppermute | solution.py:229
  30.9 4.1 %collective-permute-start.4 = (f32[32,256]{1,0:T(8,128)S(1)}, f32[32,256]{1,0:T(8,128)S(1)}, u32[]{:S(2)}, u32[]{:S(2)}) collective-permute-start(f32[32,256]{1,0:T(8,128)S(1)} %add_add_fusion), channel_id=1, source_target_pairs={{0,1},{1,0},{2,3},{3,2},{4,5},{5,4},{6,7},{7,6},{8,9},{9,8},{10,11... | collective-permute-start | bytes 98312 | tf_op jit(solution)/shard_map/ppermute | solution.py:229
  34.9 2.0 %copy-start.2 = (bf16[256,7168]{1,0:T(8,128)(2,1)S(1)}, bf16[256,7168]{1,0:T(8,128)(2,1)}, u32[]{:S(2)}) copy-start(bf16[256,7168]{1,0:T(8,128)(2,1)} %copy-done.1) | copy-start | bytes 11010052
  37.0 2.0 %copy-start.5 = (bf16[256,7168]{1,0:T(8,128)(2,1)S(1)}, bf16[256,7168]{1,0:T(8,128)(2,1)}, u32[]{:S(2)}) copy-start(bf16[256,7168]{1,0:T(8,128)(2,1)} %copy-done.4) | copy-start | bytes 11010052
  39.8 7.9 %collective-permute-start.7 = (f32[4,32,896]{2,1,0:T(8,128)S(1)}, f32[4,32,896]{2,1,0:T(8,128)S(1)}, u32[]{:S(2)}, u32[]{:S(2)}) collective-permute-start(f32[4,32,896]{2,1,0:T(8,128)S(1)} %right.3), channel_id=1, source_target_pairs={{0,4},{4,0},{8,12},{12,8},{16,20},{20,16},{24,28},{28,24},{1,5},{5... | collective-permute-start | bytes 1376264 | tf_op jit(solution)/shard_map/ppermute | solution.py:229
  42.9 2.0 %copy-start.3 = (bf16[256,7168]{1,0:T(8,128)(2,1)S(1)}, bf16[256,7168]{1,0:T(8,128)(2,1)}, u32[]{:S(2)}) copy-start(bf16[256,7168]{1,0:T(8,128)(2,1)} %copy-done.1) | copy-start | bytes 11010052
  44.9 2.0 %copy-start.6 = (bf16[256,7168]{1,0:T(8,128)(2,1)S(1)}, bf16[256,7168]{1,0:T(8,128)(2,1)}, u32[]{:S(2)}) copy-start(bf16[256,7168]{1,0:T(8,128)(2,1)} %copy-done.4) | copy-start | bytes 11010052
  46.9 19.5 %slice-start = ((s8[7340032]{0:T(1024)(128)(4,1)}), s8[4194304]{0:T(1024)(128)(4,1)S(1)}, s32[]{:S(2)}) async-start(s8[7340032]{0:T(1024)(128)(4,1)} %bitcast.26), calls=%async_computation | async-start | bytes 8388608
  47.8 18.7 %slice-start.1 = ((s8[7340032]{0:T(1024)(128)(4,1)}), s8[3145728]{0:T(1024)(128)(4,1)S(1)}, s32[]{:S(2)}) async-start(s8[7340032]{0:T(1024)(128)(4,1)} %bitcast.26), calls=%async_computation.1 | async-start | bytes 6291456
  47.8 5.8 %collective-permute-start.10 = (f32[32,896]{1,0:T(8,128)S(1)}, f32[32,896]{1,0:T(8,128)S(1)}, u32[]{:S(2)}, u32[]{:S(2)}) collective-permute-start(f32[32,896]{1,0:T(8,128)S(1)} %get-tuple-element.25), channel_id=1, source_target_pairs={{0,24},{4,28},{8,16},{12,20},{16,8},{20,12},{24,0},{28,4},{1,25},{... | collective-permute-start | bytes 344072 | tf_op jit(solution)/shard_map/ppermute | solution.py:229
  49.1 7.2 %collective-permute-start.9 = (f32[32,896]{1,0:T(8,128)S(1)}, f32[32,896]{1,0:T(8,128)S(1)}, u32[]{:S(2)}, u32[]{:S(2)}) collective-permute-start(f32[32,896]{1,0:T(8,128)S(1)} %get-tuple-element.26), channel_id=1, source_target_pairs={{0,16},{4,20},{8,24},{12,28},{16,0},{20,4},{24,8},{28,12},{1,17},{... | collective-permute-start | bytes 344072 | tf_op jit(solution)/shard_map/ppermute | solution.py:229
  49.3 7.0 %collective-permute-start.8 = (f32[32,896]{1,0:T(8,128)S(1)}, f32[32,896]{1,0:T(8,128)S(1)}, u32[]{:S(2)}, u32[]{:S(2)}) collective-permute-start(f32[32,896]{1,0:T(8,128)S(1)} %get-tuple-element.27), channel_id=1, source_target_pairs={{0,8},{4,12},{8,0},{12,4},{16,24},{20,28},{24,16},{28,20},{1,9},{5... | collective-permute-start | bytes 344072 | tf_op jit(solution)/shard_map/ppermute | solution.py:229
  56.6 5.1 %collective-permute-start.13 = (f32[32,896]{1,0:T(8,128)S(1)}, f32[32,896]{1,0:T(8,128)S(1)}, u32[]{:S(2)}, u32[]{:S(2)}) collective-permute-start(f32[32,896]{1,0:T(8,128)S(1)} %convolution_multiply_fusion.refs_0_), channel_id=1, source_target_pairs={{0,24},{4,28},{8,16},{12,20},{16,8},{20,12},{24,0},{28,4},{1,25},{... | collective-permute-start | bytes 344072 | tf_op jit(solution)/shard_map/ppermute | solution.py:229
  57.9 7.2 %collective-permute-start.12 = (f32[32,896]{1,0:T(8,128)S(1)}, f32[32,896]{1,0:T(8,128)S(1)}, u32[]{:S(2)}, u32[]{:S(2)}) collective-permute-start(f32[32,896]{1,0:T(8,128)S(1)} %convolution_multiply_fusion.refs_0_), channel_id=1, source_target_pairs={{0,16},{4,20},{8,24},{12,28},{16,0},{20,4},{24,8},{28,12},{1,17},{... | collective-permute-start | bytes 344072 | tf_op jit(solution)/shard_map/ppermute | solution.py:229
  58.1 7.0 %collective-permute-start.11 = (f32[32,896]{1,0:T(8,128)S(1)}, f32[32,896]{1,0:T(8,128)S(1)}, u32[]{:S(2)}, u32[]{:S(2)}) collective-permute-start(f32[32,896]{1,0:T(8,128)S(1)} %convolution_multiply_fusion.refs_0_), channel_id=1, source_target_pairs={{0,8},{4,12},{8,0},{12,4},{16,24},{20,28},{24,16},{28,20},{1,9},{5... | collective-permute-start | bytes 344072 | tf_op jit(solution)/shard_map/ppermute | solution.py:229
  65.1 4.2 %collective-permute-start.14 = (f32[4,32,896]{2,1,0:T(8,128)S(1)}, f32[4,32,896]{2,1,0:T(8,128)S(1)}, u32[]{:S(2)}, u32[]{:S(2)}) collective-permute-start(f32[4,32,896]{2,1,0:T(8,128)S(1)} %pad_maximum_fusion), channel_id=1, source_target_pairs={{0,4},{4,0},{8,12},{12,8},{16,20},{20,16},{24,28},{28,24},{1,5},{5... | collective-permute-start | bytes 1376264 | tf_op jit(solution)/shard_map/ppermute | solution.py:229

commit v3 on v2

--- a/solution.py
+++ b/solution.py
@@ -20,6 +20,15 @@
 
 def dot(a, b, a_dim, b_dim, precision=None):
     return lax.dot_general(a, b, (((a_dim,), (b_dim,)), ((), ())), precision=precision, preferred_element_type=F32)
+
+
+def keep(x, space):
+    return pltpu.with_memory_space_constraint(x, space)
+
+
+def position():
+    me = lax.axis_index("dp")
+    return lax.rem(me, 2), lax.div(me, 2)
 
 
 def params(mebibytes):
@@ -89,13 +98,15 @@
     )(gradient, feedback, right)
 
 
-def right_kernel(index, left, high, low, pieces):
+def right_kernel(own, left, high, low, pieces):
     chips, rank, width = pieces.shape
     half = chips * width
+    core, _ = position()
+    side = core if own else 1 - core
     block = 512 if half % 512 == 0 else 128
     both = jnp.concatenate(split(left[...]), axis=0)
     for i in range(half // block):
-        at = pl.ds(pl.multiple_of(index[0] * half + i * block, block), block)
+        at = pl.ds(pl.multiple_of(side * half + i * block, block), block)
         total = dot(both, high[:, at], 1, 0) + dot(both, low[:, at], 1, 0)
         total = total[:rank] + total[rank:]
         start = i * block
@@ -106,17 +117,36 @@
             start = stop
 
 
-def right_product(index, left, high, low, chips, width):
+def right_product(own, left, high, low, chips, width):
     rank, rows = left.shape
     return pl.pallas_call(
-        right_kernel,
-        in_specs=[pl.BlockSpec(memory_space=pltpu.SMEM)] + [VMEM] * 3,
+        functools.partial(right_kernel, own),
+        in_specs=[VMEM] * 3,
         out_specs=VMEM,
         out_shape=pltpu.VMEM((chips, rank, width), F32),
         compiler_params=params(8),
         cost_estimate=cost(8 * rows * chips * width * rank, 4 * rows * chips * width),
         name="right",
-    )(index.reshape(1), left, high, low)
+    )(left, high, low)
+
+
+def share_kernel(a, b, *outs):
+    _, chip = position()
+    for k, out in enumerate(outs):
+        out[...] = a[chip ^ k] + b[chip ^ k]
+
+
+def share(a, b):
+    chips, rank, width = a.shape
+    return pl.pallas_call(
+        share_kernel,
+        in_specs=[VMEM] * 2,
+        out_specs=[VMEM] * chips,
+        out_shape=[pltpu.VMEM((rank, width), F32)] * chips,
+        compiler_params=params(8),
+        cost_estimate=cost(chips * rank * width, 12 * chips * rank * width),
+        name="share",
+    )(a, b)
 
 
 def factor_kernel(left, inverse, factor, stacked):
@@ -158,14 +188,16 @@
     )(left)
 
 
-def feedback_kernel(aliased, columns, index, stacked, pieces, combined, *refs):
+def feedback_kernel(own, aliased, columns, stacked, pieces, combined, *refs):
     feedback, right, feedback_buf, sems = refs[2 * aliased :]
     rank = pieces[0].shape[-2]
     chips, rows, width = feedback_buf.shape
     whole = combined.shape[1] == columns
+    core, chip = position()
+    side = core if own else 1 - core
     copies = []
     for k in range(chips):
-        place = index[0] * chips + (index[1] ^ k)
+        place = side * chips + (chip ^ k)
         at = pl.ds(pl.multiple_of(place * width, 128), width)
         piece = pieces[k]
         piece_high, piece_low = split(piece[...])
@@ -196,24 +228,24 @@
         pl.when(inside)(run)
 
 
-def new_feedback(index, stacked, pieces, combined, columns, before=()):
+def new_feedback(own, stacked, pieces, combined, columns, before=()):
     rows = combined.shape[0]
     separate = isinstance(pieces, list)
     chips = len(pieces) if separate else pieces.shape[0]
     rank, width = (pieces[0] if separate else pieces).shape[-2:]
     given = pieces if separate else [pieces]
 
-    def kernel(index, stacked, *refs):
+    def kernel(stacked, *refs):
         mine = refs[: len(given)]
         parts = list(mine) if separate else [mine[0].at[k] for k in range(chips)]
-        feedback_kernel(len(before) // 2, columns, index, stacked, parts, *refs[len(given) :])
+        feedback_kernel(own, len(before) // 2, columns, stacked, parts, *refs[len(given) :])
 
     return pl.pallas_call(
         kernel,
-        in_specs=[pl.BlockSpec(memory_space=pltpu.SMEM)] + [VMEM] * (2 + len(given)) + [ANY] * len(before),
+        in_specs=[VMEM] * (2 + len(given)) + [ANY] * len(before),
         out_specs=[ANY] * 2,
         out_shape=[jax.ShapeDtypeStruct((rows, columns), F32), jax.ShapeDtypeStruct((rank, columns), F32)],
-        input_output_aliases={3 + len(given) + i: i for i in range(len(before))},
+        input_output_aliases={2 + len(given) + i: i for i in range(len(before))},
         scratch_shapes=[
             pltpu.VMEM((chips, rows, width), F32),
             pltpu.SemaphoreType.DMA((2, chips)),
@@ -221,7 +253,7 @@
         compiler_params=params(16),
         cost_estimate=cost(8 * rows * chips * width * rank, 4 * rows * chips * width),
         name="feedback",
-    )(index, stacked, *given, combined, *before)
+    )(stacked, *given, combined, *before)
 
 
 def swap(x, axis, mask):
@@ -249,38 +281,32 @@
     return size.bit_length() - 1
 
 
-def pick(x, index):
-    return lax.dynamic_index_in_dim(x, index, 0, keepdims=False)
-
-
 def per_device(gradient, feedback, right_factor):
     gradient, feedback = gradient[0], feedback[0]
     columns = gradient.shape[1]
     replicas = lax.axis_size("dp")
-    me = lax.axis_index("dp")
-    core, chip = me % 2, me // 2
     chips = replicas // 2
     width = -(-columns // (replicas * 128)) * 128
     assert columns % width == 0
 
-    combined, high, low, left = left_product(gradient, feedback, right_factor.T, replicas * width)
+    given = [keep(x, pltpu.HBM) for x in (gradient, feedback, right_factor.T)]
+    combined, high, low, left = left_product(*given, replicas * width)
+    combined, high, low = (keep(x, pltpu.VMEM) for x in (combined, high, low))
     left = sum_over(left, "dp", 0, 1)
     left = sum_over(left, "dp", 1, bits("dp"))
     left = sum_over(left, "tensor", 0, bits("tensor")) / replicas
 
-    theirs = swap(right_product(1 - core, left, high, low, chips, width), "dp", 1)
-    half = right_product(core, left, high, low, chips, width) + theirs
-    own = tree([pick(half, chip)] + [swap(pick(half, chip ^ k), "dp", 2 * k) for k in range(1, chips)])
+    theirs = swap(right_product(False, left, high, low, chips, width), "dp", 1)
+    own, *away = share(right_product(True, left, high, low, chips, width), theirs)
+    own = tree([own] + [swap(x, "dp", 2 * k) for k, x in enumerate(away, 1)])
 
     inverse, factor, stacked = factors(left)
     own = jnp.dot(inverse, own, precision=HIGHEST, preferred_element_type=F32) / replicas
 
     got = [own] + [swap(own, "dp", 2 * k) for k in range(1, chips)]
     other = swap(jnp.stack(got), "dp", 1)
-    place = jnp.stack([core, chip])
-    outs = new_feedback(place, stacked, got, combined, columns)
-    place = jnp.stack([1 - core, chip])
-    outs = new_feedback(place, stacked, other, combined, columns, tuple(outs))
+    outs = new_feedback(True, stacked, got, combined, columns)
+    outs = new_feedback(False, stacked, other, combined, columns, tuple(outs))
     return (outs[0][None], factor.T, outs[1].T)
 
 

time: 72.6 us -> 49.5 us (0.68)
  local copies, waits for them, and re-layouts: 21.8 us -> 0.61 us
  waiting for transfers between devices: 15.9 us -> 13.1 us
  starting transfers between devices: 16.6 us -> 19.1 us
  Pallas kernels: 16.6 us -> 15.5 us
    unnamed x25 -> x1, local copies, waits for them, and re-layouts: 21.7 us -> 0.61 us
    ppermute x15, waiting for transfers between devices: 15.9 us -> 13.1 us  [swap(): return lax.ppermute(x, axis, [(i, i ^ mask) for i in range(size)])]
    ppermute x15, starting transfers between devices: 16.6 us -> 19.1 us  [swap(): return lax.ppermute(x, axis, [(i, i ^ mask) for i in range(size)])]
    pallas_call x4 -> x5, Pallas kernels: 7.2 us -> 6.18 us  [the longest x2 4.65 us: new_feedback(): pl.pallas_call(kernel, in_specs=[VMEM] * (2 + len(given)) + [ANY] * len(b...]
  transfers between devices with their start and end apart: 15 -> 15, of which waited for: 9 -> 11; matrix products, arithmetic and copies ran while one was open for 1% -> 1% of each run, Pallas kernels for 9% -> 12%
where the time goes in v3:
time: 49.5 us; the launch traced here: 49.4 us
  starting transfers between devices  19.1 us (39%)
  Pallas kernels  15.5 us (31%)
  waiting for transfers between devices  13.1 us (26%)
  between operations  0.72 us (1%)
  local copies, waits for them, and re-layouts  0.61 us (1%)
    ppermute x15, starting transfers between devices, swap(): return lax.ppermute(x, axis, [(i, i ^ mask) for i in range(size)])  19.1 us
    ppermute x15, waiting for transfers between devices, swap(): return lax.ppermute(x, axis, [(i, i ^ mask) for i in range(size)])  13.1 us
    pallas_call x1, Pallas kernels, left_product(): pl.pallas_call(functools.partial(left_kernel, chunk), in_specs=[ANY] * 3,...  6.19 us
    pallas_call x2, Pallas kernels, new_feedback(): pl.pallas_call(kernel, in_specs=[VMEM] * (2 + len(given)) + [ANY] * len(b...  4.65 us
    pallas_call x1, Pallas kernels, factors(): pl.pallas_call(factor_kernel, in_specs=[VMEM], out_specs=[VMEM] * 3, out_...  3.12 us
    pallas_call x2, Pallas kernels, right_product(): pl.pallas_call(functools.partial(right_kernel, own), in_specs=[VMEM] * 3,...  1.48 us
  transfers between devices with their start and end apart: 15, of which 11 were waited for; matrix products, arithmetic and copies ran while one was open for 1% of the time, Pallas kernels for 12%

profile of v3, /device:TPU:1, one launch (start us, length us, event | category | flops | bytes accessed | tf_op | source)
XLA Modules:
  0.0 49.4 jit_solution(1966355166901917045)
XLA Ops:
  0.6 6.2 %left.1 = (f32[256,7168]{1,0:T(8,128)S(1)}, bf16[256,7168]{1,0:T(8,128)(2,1)S(1)}, bf16[256,7168]{1,0:T(8,128)(2,1)S(1)}, f32[32,256]{1,0:T(8,128)S(1)}) custom-call(bf16[256,7168]{1,0:T(8,128)(2,1)} %bitcast.18, f32[256,7168]{1,0:T(8,128)} %bitcast.16, f32[32,7168]{1,0:T(8,128)} %bitcast.19), custom_call_target="tpu_custom_call" | custom-call | flops 469762048 | bytes 11010048 | tf_op jit(solution)/shard_map/left/pallas_call | solution.py:80
  6.8 0.1 collective-permute-start
  7.0 1.1 %collective-permute-done = f32[32,256]{1,0:T(8,128)S(1)} collective-permute-done((f32[32,256]{1,0:T(8,128)S(1)}, f32[32,256]{1,0:T(8,128)S(1)}, u32[]{:S(2)}, u32[]{:S(2)}) %collective-permute-start) | collective-permute-done | bytes 32800 | tf_op jit(solution)/shard_map/ppermute | solution.py:261
  8.1 3.3 %collective-permute-start.3 = (f32[32,256]{1,0:T(8,128)S(1)}, f32[32,256]{1,0:T(8,128)S(1)}, u32[]{:S(2)}, u32[]{:S(2)}) collective-permute-start(f32[32,256]{1,0:T(8,128)S(1)} %add.30), channel_id=1, source_target_pairs={{0,24},{4,28},{8,16},{12,20},{16,8},{20,12},{24,0},{28,4},{1,25},{... | collective-permute-start | bytes 98312 | tf_op jit(solution)/shard_map/ppermute | solution.py:261
  11.4 0.2 collective-permute-start.2
  11.7 0.1 collective-permute-start.1
  11.8 0.9 %collective-permute-done.3 = f32[32,256]{1,0:T(8,128)S(1)} collective-permute-done((f32[32,256]{1,0:T(8,128)S(1)}, f32[32,256]{1,0:T(8,128)S(1)}, u32[]{:S(2)}, u32[]{:S(2)}) %collective-permute-start.3) | collective-permute-done | bytes 32800 | tf_op jit(solution)/shard_map/ppermute | solution.py:261
  12.7 1.5 %collective-permute-done.2 = f32[32,256]{1,0:T(8,128)S(1)} collective-permute-done((f32[32,256]{1,0:T(8,128)S(1)}, f32[32,256]{1,0:T(8,128)S(1)}, u32[]{:S(2)}, u32[]{:S(2)}) %collective-permute-start.2) | collective-permute-done | bytes 32800 | tf_op jit(solution)/shard_map/ppermute | solution.py:261
  14.2 0.2 collective-permute-done.1
  14.4 3.4 %collective-permute-start.6 = (f32[32,256]{1,0:T(8,128)S(1)}, f32[32,256]{1,0:T(8,128)S(1)}, u32[]{:S(2)}, u32[]{:S(2)}) collective-permute-start(f32[32,256]{1,0:T(8,128)S(1)} %add_add_fusion), channel_id=1, source_target_pairs={{0,3},{1,2},{2,1},{3,0},{4,7},{5,6},{6,5},{7,4},{8,11},{9,10},{10,... | collective-permute-start | bytes 98312 | tf_op jit(solution)/shard_map/ppermute | solution.py:261
  17.8 0.0 collective-permute-start.5
  17.8 0.4 collective-permute-start.4
  18.2 0.9 %collective-permute-done.6 = f32[32,256]{1,0:T(8,128)S(1)} collective-permute-done((f32[32,256]{1,0:T(8,128)S(1)}, f32[32,256]{1,0:T(8,128)S(1)}, u32[]{:S(2)}, u32[]{:S(2)}) %collective-permute-start.6) | collective-permute-done | bytes 32800 | tf_op jit(solution)/shard_map/ppermute | solution.py:261
  19.1 2.7 %collective-permute-done.5 = f32[32,256]{1,0:T(8,128)S(1)} collective-permute-done((f32[32,256]{1,0:T(8,128)S(1)}, f32[32,256]{1,0:T(8,128)S(1)}, u32[]{:S(2)}, u32[]{:S(2)}) %collective-permute-start.5) | collective-permute-done | bytes 32800 | tf_op jit(solution)/shard_map/ppermute | solution.py:261
  21.9 0.0 collective-permute-done.4
  21.9 0.7 %right.3 = f32[4,32,896]{2,1,0:T(8,128)S(1)} custom-call(f32[32,256]{1,0:T(8,128)S(1)} %add_multiply_fusion.left, bf16[256,7168]{1,0:T(8,128)(2,1)S(1)} %get-tuple-element.21.high, bf16[256,7168]{1,0:T(8,128)(2,1)S(1)} %get-tuple-element.22.low), custom_call_target="tpu_custom_call" | custom-call | flops 234881024 | bytes 3670016 | tf_op jit(solution)/shard_map/right/pallas_call | solution.py:122
  22.6 3.1 %collective-permute-start.7 = (f32[4,32,896]{2,1,0:T(8,128)S(1)}, f32[4,32,896]{2,1,0:T(8,128)S(1)}, u32[]{:S(2)}, u32[]{:S(2)}) collective-permute-start(f32[4,32,896]{2,1,0:T(8,128)S(1)} %right.3), channel_id=1, source_target_pairs={{0,4},{4,0},{8,12},{12,8},{16,20},{20,16},{24,28},{28,24},{1,5},{5... | collective-permute-start | bytes 1376264 | tf_op jit(solution)/shard_map/ppermute | solution.py:261
  25.8 0.7 %right.2.a = f32[4,32,896]{2,1,0:T(8,128)S(1)} custom-call(f32[32,256]{1,0:T(8,128)S(1)} %add_multiply_fusion.left, bf16[256,7168]{1,0:T(8,128)(2,1)S(1)} %get-tuple-element.21.high, bf16[256,7168]{1,0:T(8,128)(2,1)S(1)} %get-tuple-element.22.low), custom_call_target="tpu_custom_call" | custom-call | flops 234881024 | bytes 3670016 | tf_op jit(solution)/shard_map/right/pallas_call | solution.py:122
  26.5 0.7 %collective-permute-done.7.b = f32[4,32,896]{2,1,0:T(8,128)S(1)} collective-permute-done((f32[4,32,896]{2,1,0:T(8,128)S(1)}, f32[4,32,896]{2,1,0:T(8,128)S(1)}, u32[]{:S(2)}, u32[]{:S(2)}) %collective-permute-start.7) | collective-permute-done | bytes 458784 | tf_op jit(solution)/shard_map/ppermute | solution.py:261
  27.3 0.3 collective-permute-start.8
  27.6 1.2 %collective-permute-start.9 = (f32[32,896]{1,0:T(8,128)S(1)}, f32[32,896]{1,0:T(8,128)S(1)}, u32[]{:S(2)}, u32[]{:S(2)}) collective-permute-start(f32[32,896]{1,0:T(8,128)S(1)} %get-tuple-element.25), channel_id=1, source_target_pairs={{0,16},{4,20},{8,24},{12,28},{16,0},{20,4},{24,8},{28,12},{1,17},{... | collective-permute-start | bytes 344072 | tf_op jit(solution)/shard_map/ppermute | solution.py:261
  28.8 1.2 %collective-permute-start.10 = (f32[32,896]{1,0:T(8,128)S(1)}, f32[32,896]{1,0:T(8,128)S(1)}, u32[]{:S(2)}, u32[]{:S(2)}) collective-permute-start(f32[32,896]{1,0:T(8,128)S(1)} %get-tuple-element.26), channel_id=1, source_target_pairs={{0,24},{4,28},{8,16},{12,20},{16,8},{20,12},{24,0},{28,4},{1,25},{... | collective-permute-start | bytes 344072 | tf_op jit(solution)/shard_map/ppermute | solution.py:261
  30.0 3.1 %factor.1 = (f32[32,32]{1,0:T(8,128)S(1)}, f32[32,256]{1,0:T(8,128)S(1)}, bf16[256,128]{1,0:T(8,128)(2,1)S(1)}) custom-call(f32[32,256]{1,0:T(8,128)S(1)} %add_multiply_fusion.left), custom_call_target="tpu_custom_call" | custom-call | flops 2000000000 | bytes 1000000 | tf_op jit(solution)/shard_map/factor/pallas_call | solution.py:176
  33.1 0.0 collective-permute-done.8
  33.1 0.0 collective-permute-done.9
  33.1 2.0 %collective-permute-done.10 = f32[32,896]{1,0:T(8,128)S(1)} collective-permute-done((f32[32,896]{1,0:T(8,128)S(1)}, f32[32,896]{1,0:T(8,128)S(1)}, u32[]{:S(2)}, u32[]{:S(2)}) %collective-permute-start.10) | collective-permute-done | bytes 114720 | tf_op jit(solution)/shard_map/ppermute | solution.py:261
  35.1 0.2 convolution_multiply_fusion.refs_0_
  35.4 0.2 collective-permute-start.13
  35.6 0.7 %collective-permute-start.12 = (f32[32,896]{1,0:T(8,128)S(1)}, f32[32,896]{1,0:T(8,128)S(1)}, u32[]{:S(2)}, u32[]{:S(2)}) collective-permute-start(f32[32,896]{1,0:T(8,128)S(1)} %convolution_multiply_fusion.refs_0_), channel_id=1, source_target_pairs={{0,16},{4,20},{8,24},{12,28},{16,0},{20,4},{24,8},{28,12},{1,17},{... | collective-permute-start | bytes 344072 | tf_op jit(solution)/shard_map/ppermute | solution.py:261
  36.3 1.8 %collective-permute-start.11 = (f32[32,896]{1,0:T(8,128)S(1)}, f32[32,896]{1,0:T(8,128)S(1)}, u32[]{:S(2)}, u32[]{:S(2)}) collective-permute-start(f32[32,896]{1,0:T(8,128)S(1)} %convolution_multiply_fusion.refs_0_), channel_id=1, source_target_pairs={{0,8},{4,12},{8,0},{12,4},{16,24},{20,28},{24,16},{28,20},{1,9},{5... | collective-permute-start | bytes 344072 | tf_op jit(solution)/shard_map/ppermute | solution.py:261
  38.1 2.0 %collective-permute-done.13.refs_3_ = f32[32,896]{1,0:T(8,128)S(1)} collective-permute-done((f32[32,896]{1,0:T(8,128)S(1)}, f32[32,896]{1,0:T(8,128)S(1)}, u32[]{:S(2)}, u32[]{:S(2)}) %collective-permute-start.13) | collective-permute-done | bytes 114720 | tf_op jit(solution)/shard_map/ppermute | solution.py:261
  40.1 0.4 collective-permute-done.12.refs_2_
  40.4 0.6 %collective-permute-done.11.refs_1_ = f32[32,896]{1,0:T(8,128)S(1)} collective-permute-done((f32[32,896]{1,0:T(8,128)S(1)}, f32[32,896]{1,0:T(8,128)S(1)}, u32[]{:S(2)}, u32[]{:S(2)}) %collective-permute-start.11) | collective-permute-done | bytes 114720 | tf_op jit(solution)/shard_map/ppermute | solution.py:261
  41.1 3.0 %collective-permute-start.14 = (f32[4,32,896]{2,1,0:T(8,128)S(1)}, f32[4,32,896]{2,1,0:T(8,128)S(1)}, u32[]{:S(2)}, u32[]{:S(2)}) collective-permute-start(f32[4,32,896]{2,1,0:T(8,128)S(1)} %pad_maximum_fusion), channel_id=1, source_target_pairs={{0,4},{4,0},{8,12},{12,8},{16,20},{20,16},{24,28},{28,24},{1,5},{5... | collective-permute-start | bytes 1376264 | tf_op jit(solution)/shard_map/ppermute | solution.py:261
  44.1 0.6 %copy.10 = f32[256,32]{0,1:T(8,128)} copy(f32[256,32]{0,1:T(8,128)S(1)} %bitcast.11) | data formatting | bytes 65536
  44.7 2.3 %feedback.2 = (f32[256,7168]{1,0:T(8,128)}, f32[32,7168]{1,0:T(8,128)}) custom-call(bf16[256,128]{1,0:T(8,128)(2,1)S(1)} %get-tuple-element.19.stacked, f32[32,896]{1,0:T(8,128)S(1)} %convolution_multiply_fusion.refs_0_, f32[32,896]{1,0:T(8,128)S(1)} %collective-permute-done.11.refs_1_, f32[32,896]{1,0:T(8,128)S(1)} %collective-permute-done.12.refs_2_, ...), custom_call_target="tpu_custom_call" | custom-call | flops 234881024 | bytes 3670016 | tf_op jit(solution)/shard_map/feedback/pallas_call | solution.py:243
  47.0 0.0 collective-permute-done.14.refs_0_
  47.1 2.3 %feedback.3 = (f32[256,7168]{1,0:T(8,128)}, f32[32,7168]{1,0:T(8,128)}) custom-call(bf16[256,128]{1,0:T(8,128)(2,1)S(1)} %get-tuple-element.19.stacked, f32[4,32,896]{2,1,0:T(8,128)S(1)} %collective-permute-done.14.refs_0_, f32[256,7168]{1,0:T(8,128)S(1)} %get-tuple-element.27.refs_4_.refs_1_, ...), custom_call_target="tpu_custom_call", output_to_operand_aliasing={{0}: (3, {}), {1}: (4, {})} | custom-call | flops 234881024 | bytes 3670016 | tf_op jit(solution)/shard_map/feedback/pallas_call | solution.py:243
  (5 shorter events, 0.1 us)
Async XLA Ops:
  6.8 1.3 %collective-permute-start = (f32[32,256]{1,0:T(8,128)S(1)}, f32[32,256]{1,0:T(8,128)S(1)}, u32[]{:S(2)}, u32[]{:S(2)}) collective-permute-start(f32[32,256]{1,0:T(8,128)S(1)} %get-tuple-element.18), channel_id=1, source_target_pairs={{0,4},{4,0},{8,12},{12,8},{16,20},{20,16},{24,28},{28,24},{1,5},{5... | collective-permute-start | bytes 98312 | tf_op jit(solution)/shard_map/ppermute | solution.py:261
  8.1 4.6 %collective-permute-start.3 = (f32[32,256]{1,0:T(8,128)S(1)}, f32[32,256]{1,0:T(8,128)S(1)}, u32[]{:S(2)}, u32[]{:S(2)}) collective-permute-start(f32[32,256]{1,0:T(8,128)S(1)} %add.30), channel_id=1, source_target_pairs={{0,24},{4,28},{8,16},{12,20},{16,8},{20,12},{24,0},{28,4},{1,25},{... | collective-permute-start | bytes 98312 | tf_op jit(solution)/shard_map/ppermute | solution.py:261
  11.4 2.8 %collective-permute-start.2 = (f32[32,256]{1,0:T(8,128)S(1)}, f32[32,256]{1,0:T(8,128)S(1)}, u32[]{:S(2)}, u32[]{:S(2)}) collective-permute-start(f32[32,256]{1,0:T(8,128)S(1)} %add.30), channel_id=1, source_target_pairs={{0,16},{4,20},{8,24},{12,28},{16,0},{20,4},{24,8},{28,12},{1,17},{... | collective-permute-start | bytes 98312 | tf_op jit(solution)/shard_map/ppermute | solution.py:261
  11.7 2.8 %collective-permute-start.1 = (f32[32,256]{1,0:T(8,128)S(1)}, f32[32,256]{1,0:T(8,128)S(1)}, u32[]{:S(2)}, u32[]{:S(2)}) collective-permute-start(f32[32,256]{1,0:T(8,128)S(1)} %add.30), channel_id=1, source_target_pairs={{0,8},{4,12},{8,0},{12,4},{16,24},{20,28},{24,16},{28,20},{1,9},{5... | collective-permute-start | bytes 98312 | tf_op jit(solution)/shard_map/ppermute | solution.py:261
  14.4 4.7 %collective-permute-start.6 = (f32[32,256]{1,0:T(8,128)S(1)}, f32[32,256]{1,0:T(8,128)S(1)}, u32[]{:S(2)}, u32[]{:S(2)}) collective-permute-start(f32[32,256]{1,0:T(8,128)S(1)} %add_add_fusion), channel_id=1, source_target_pairs={{0,3},{1,2},{2,1},{3,0},{4,7},{5,6},{6,5},{7,4},{8,11},{9,10},{10,... | collective-permute-start | bytes 98312 | tf_op jit(solution)/shard_map/ppermute | solution.py:261
  17.8 4.1 %collective-permute-start.5 = (f32[32,256]{1,0:T(8,128)S(1)}, f32[32,256]{1,0:T(8,128)S(1)}, u32[]{:S(2)}, u32[]{:S(2)}) collective-permute-start(f32[32,256]{1,0:T(8,128)S(1)} %add_add_fusion), channel_id=1, source_target_pairs={{0,2},{1,3},{2,0},{3,1},{4,6},{5,7},{6,4},{7,5},{8,10},{9,11},{10,... | collective-permute-start | bytes 98312 | tf_op jit(solution)/shard_map/ppermute | solution.py:261
  17.8 4.1 %collective-permute-start.4 = (f32[32,256]{1,0:T(8,128)S(1)}, f32[32,256]{1,0:T(8,128)S(1)}, u32[]{:S(2)}, u32[]{:S(2)}) collective-permute-start(f32[32,256]{1,0:T(8,128)S(1)} %add_add_fusion), channel_id=1, source_target_pairs={{0,1},{1,0},{2,3},{3,2},{4,5},{5,4},{6,7},{7,6},{8,9},{9,8},{10,11... | collective-permute-start | bytes 98312 | tf_op jit(solution)/shard_map/ppermute | solution.py:261
  22.6 4.6 %collective-permute-start.7 = (f32[4,32,896]{2,1,0:T(8,128)S(1)}, f32[4,32,896]{2,1,0:T(8,128)S(1)}, u32[]{:S(2)}, u32[]{:S(2)}) collective-permute-start(f32[4,32,896]{2,1,0:T(8,128)S(1)} %right.3), channel_id=1, source_target_pairs={{0,4},{4,0},{8,12},{12,8},{16,20},{20,16},{24,28},{28,24},{1,5},{5... | collective-permute-start | bytes 1376264 | tf_op jit(solution)/shard_map/ppermute | solution.py:261
  27.3 5.8 %collective-permute-start.8 = (f32[32,896]{1,0:T(8,128)S(1)}, f32[32,896]{1,0:T(8,128)S(1)}, u32[]{:S(2)}, u32[]{:S(2)}) collective-permute-start(f32[32,896]{1,0:T(8,128)S(1)} %get-tuple-element.24), channel_id=1, source_target_pairs={{0,8},{4,12},{8,0},{12,4},{16,24},{20,28},{24,16},{28,20},{1,9},{5... | collective-permute-start | bytes 344072 | tf_op jit(solution)/shard_map/ppermute | solution.py:261
  27.6 5.5 %collective-permute-start.9 = (f32[32,896]{1,0:T(8,128)S(1)}, f32[32,896]{1,0:T(8,128)S(1)}, u32[]{:S(2)}, u32[]{:S(2)}) collective-permute-start(f32[32,896]{1,0:T(8,128)S(1)} %get-tuple-element.25), channel_id=1, source_target_pairs={{0,16},{4,20},{8,24},{12,28},{16,0},{20,4},{24,8},{28,12},{1,17},{... | collective-permute-start | bytes 344072 | tf_op jit(solution)/shard_map/ppermute | solution.py:261
  28.8 6.3 %collective-permute-start.10 = (f32[32,896]{1,0:T(8,128)S(1)}, f32[32,896]{1,0:T(8,128)S(1)}, u32[]{:S(2)}, u32[]{:S(2)}) collective-permute-start(f32[32,896]{1,0:T(8,128)S(1)} %get-tuple-element.26), channel_id=1, source_target_pairs={{0,24},{4,28},{8,16},{12,20},{16,8},{20,12},{24,0},{28,4},{1,25},{... | collective-permute-start | bytes 344072 | tf_op jit(solution)/shard_map/ppermute | solution.py:261
  35.4 4.7 %collective-permute-start.13 = (f32[32,896]{1,0:T(8,128)S(1)}, f32[32,896]{1,0:T(8,128)S(1)}, u32[]{:S(2)}, u32[]{:S(2)}) collective-permute-start(f32[32,896]{1,0:T(8,128)S(1)} %convolution_multiply_fusion.refs_0_), channel_id=1, source_target_pairs={{0,24},{4,28},{8,16},{12,20},{16,8},{20,12},{24,0},{28,4},{1,25},{... | collective-permute-start | bytes 344072 | tf_op jit(solution)/shard_map/ppermute | solution.py:261
  35.6 4.9 %collective-permute-start.12 = (f32[32,896]{1,0:T(8,128)S(1)}, f32[32,896]{1,0:T(8,128)S(1)}, u32[]{:S(2)}, u32[]{:S(2)}) collective-permute-start(f32[32,896]{1,0:T(8,128)S(1)} %convolution_multiply_fusion.refs_0_), channel_id=1, source_target_pairs={{0,16},{4,20},{8,24},{12,28},{16,0},{20,4},{24,8},{28,12},{1,17},{... | collective-permute-start | bytes 344072 | tf_op jit(solution)/shard_map/ppermute | solution.py:261
  36.3 4.8 %collective-permute-start.11 = (f32[32,896]{1,0:T(8,128)S(1)}, f32[32,896]{1,0:T(8,128)S(1)}, u32[]{:S(2)}, u32[]{:S(2)}) collective-permute-start(f32[32,896]{1,0:T(8,128)S(1)} %convolution_multiply_fusion.refs_0_), channel_id=1, source_target_pairs={{0,8},{4,12},{8,0},{12,4},{16,24},{20,28},{24,16},{28,20},{1,9},{5... | collective-permute-start | bytes 344072 | tf_op jit(solution)/shard_map/ppermute | solution.py:261
  41.1 6.0 %collective-permute-start.14 = (f32[4,32,896]{2,1,0:T(8,128)S(1)}, f32[4,32,896]{2,1,0:T(8,128)S(1)}, u32[]{:S(2)}, u32[]{:S(2)}) collective-permute-start(f32[4,32,896]{2,1,0:T(8,128)S(1)} %pad_maximum_fusion), channel_id=1, source_target_pairs={{0,4},{4,0},{8,12},{12,8},{16,20},{20,16},{24,28},{28,24},{1,5},{5... | collective-permute-start | bytes 1376264 | tf_op jit(solution)/shard_map/ppermute | solution.py:261

commit v4 on v3

--- a/solution.py
+++ b/solution.py
@@ -76,7 +76,7 @@
 def left_product(gradient, feedback, right, padded):
     rows, columns = gradient.shape
     rank = right.shape[0]
-    chunk = 512 if columns % 512 == 0 else 128
+    chunk = next(c for c in (1024, 512, 128) if columns % c == 0)
     return pl.pallas_call(
         functools.partial(left_kernel, chunk),
         in_specs=[ANY] * 3,
@@ -188,29 +188,26 @@
     )(left)
 
 
-def feedback_kernel(own, aliased, columns, stacked, pieces, combined, *refs):
-    feedback, right, feedback_buf, sems = refs[2 * aliased :]
-    rank = pieces[0].shape[-2]
-    chips, rows, width = feedback_buf.shape
+def feedback_kernel(order, columns, stacked, pieces, combined, feedback, right, token, feedback_buf, sems):
+    chips, width = combined.shape[1] // (2 * feedback_buf.shape[2]), feedback_buf.shape[2]
+    core, chip = position()
     whole = combined.shape[1] == columns
-    core, chip = position()
-    side = core if own else 1 - core
     copies = []
-    for k in range(chips):
-        place = side * chips + (chip ^ k)
+    for i, (other, k) in enumerate(order):
+        place = (1 - core if other else core) * chips + (chip ^ k)
         at = pl.ds(pl.multiple_of(place * width, 128), width)
-        piece = pieces[k]
-        piece_high, piece_low = split(piece[...])
+        piece_high, piece_low = split(pieces[i][...])
         four = jnp.concatenate([piece_high, piece_high, piece_low, piece_low], axis=0)
-        feedback_buf[k] = combined[:, at] - dot(stacked[...], four, 1, 0)
+        feedback_buf[i] = combined[:, at] - dot(stacked[...], four, 1, 0)
         copies.append(
             (
                 place * width < columns,
-                pltpu.make_async_copy(feedback_buf.at[k], feedback.at[:, at], sems.at[0, k]),
-                pltpu.make_async_copy(piece, right.at[:, at], sems.at[1, k]),
+                pltpu.make_async_copy(feedback_buf.at[i], feedback.at[:, at], sems.at[0, i]),
+                pltpu.make_async_copy(pieces[i], right.at[:, at], sems.at[1, i]),
             )
         )
         start_or_wait(copies[-1], whole, "start")
+    token[...] = jnp.zeros_like(token)
     for copy in copies:
         start_or_wait(copy, whole, "wait")
 
@@ -228,30 +225,35 @@
         pl.when(inside)(run)
 
 
-def new_feedback(own, stacked, pieces, combined, columns, before=()):
+def new_feedback(order, stacked, pieces, combined, columns, before):
     rows = combined.shape[0]
     separate = isinstance(pieces, list)
-    chips = len(pieces) if separate else pieces.shape[0]
-    rank, width = (pieces[0] if separate else pieces).shape[-2:]
     given = pieces if separate else [pieces]
+    count = len(order)
+    rank, width = given[0].shape[-2:]
 
     def kernel(stacked, *refs):
         mine = refs[: len(given)]
-        parts = list(mine) if separate else [mine[0].at[k] for k in range(chips)]
-        feedback_kernel(own, len(before) // 2, columns, stacked, parts, *refs[len(given) :])
+        parts = list(mine) if separate else [mine[0].at[i] for i in range(count)]
+        combined, *rest = refs[len(given) :]
+        feedback_kernel(order, columns, stacked, parts, combined, *rest[len(before) :])
 
     return pl.pallas_call(
         kernel,
         in_specs=[VMEM] * (2 + len(given)) + [ANY] * len(before),
-        out_specs=[ANY] * 2,
-        out_shape=[jax.ShapeDtypeStruct((rows, columns), F32), jax.ShapeDtypeStruct((rank, columns), F32)],
+        out_specs=[ANY] * 2 + [VMEM],
+        out_shape=[
+            jax.ShapeDtypeStruct((rows, columns), F32),
+            jax.ShapeDtypeStruct((rank, columns), F32),
+            pltpu.VMEM((8, 128), F32),
+        ],
         input_output_aliases={2 + len(given) + i: i for i in range(len(before))},
         scratch_shapes=[
-            pltpu.VMEM((chips, rows, width), F32),
-            pltpu.SemaphoreType.DMA((2, chips)),
+            pltpu.VMEM((count, rows, width), F32),
+            pltpu.SemaphoreType.DMA((2, count)),
         ],
         compiler_params=params(16),
-        cost_estimate=cost(8 * rows * chips * width * rank, 4 * rows * chips * width),
+        cost_estimate=cost(8 * rows * count * width * rank, 4 * rows * count * width),
         name="feedback",
     )(stacked, *given, combined, *before)
 
@@ -259,6 +261,10 @@
 def swap(x, axis, mask):
     size = lax.axis_size(axis)
     return lax.ppermute(x, axis, [(i, i ^ mask) for i in range(size)])
+
+
+def after(x, token):
+    return lax.optimization_barrier((x, token))[0]
 
 
 def tree(terms):
@@ -270,7 +276,8 @@
 def sum_over(x, axis, low, high):
     while low < high:
         step = min(2, high - low)
-        x = tree([x] + [swap(x, axis, k << low) for k in range(1, 1 << step)])
+        came = [swap(x, axis, k << low) for k in reversed(range(1, 1 << step))]
+        x = tree([x] + came[::-1])
         low += step
     return x
 
@@ -298,15 +305,23 @@
 
     theirs = swap(right_product(False, left, high, low, chips, width), "dp", 1)
     own, *away = share(right_product(True, left, high, low, chips, width), theirs)
-    own = tree([own] + [swap(x, "dp", 2 * k) for k, x in enumerate(away, 1)])
+    came = [swap(x, "dp", 2 * k) for k, x in reversed(list(enumerate(away, 1)))]
+    own = tree([own] + came[::-1])
 
     inverse, factor, stacked = factors(left)
     own = jnp.dot(inverse, own, precision=HIGHEST, preferred_element_type=F32) / replicas
 
-    got = [own] + [swap(own, "dp", 2 * k) for k in range(1, chips)]
-    other = swap(jnp.stack(got), "dp", 1)
-    outs = new_feedback(True, stacked, got, combined, columns)
-    outs = new_feedback(False, stacked, other, combined, columns, tuple(outs))
+    beside = swap(own, "dp", 1)
+    far, near = [chips - 1], list(range(1, chips - 1))
+    got = {k: swap(own, "dp", 2 * k) for k in far + near}
+    update = functools.partial(new_feedback, stacked=stacked, combined=combined, columns=columns)
+    *outs, token = update([(0, 0), (1, 0)], pieces=[own, beside], before=())
+    got |= {k: after(got[k], token) for k in far}
+    *outs, token = update([(0, k) for k in far], pieces=[got[k] for k in far], before=outs)
+    got |= {k: after(got[k], token) for k in near}
+    others = swap(jnp.stack([got[k] for k in far + near]), "dp", 1)
+    *outs, _ = update([(0, k) for k in near], pieces=[got[k] for k in near], before=outs)
+    *outs, _ = update([(1, k) for k in far + near], pieces=others, before=outs)
     return (outs[0][None], factor.T, outs[1].T)
 
 

time: 49.5 us -> 51.9 us (1.048)
  Pallas kernels: 15.5 us -> 19.4 us
  waiting for transfers between devices: 13.1 us -> 10.9 us
  starting transfers between devices: 19.1 us -> 19.8 us
    pallas_call x2 -> x4, Pallas kernels: 4.65 us -> 8.78 us  [new_feedback(): pl.pallas_call(kernel, in_specs=[VMEM] * (2 + len(given)) + [ANY] * len(b...]
    ppermute x15 -> x16, waiting for transfers between devices: 13.1 us -> 10.9 us  [swap(): return lax.ppermute(x, axis, [(i, i ^ mask) for i in range(size)])]
    ppermute x15 -> x16, starting transfers between devices: 19.1 us -> 19.8 us  [swap(): return lax.ppermute(x, axis, [(i, i ^ mask) for i in range(size)])]
  transfers between devices with their start and end apart: 15 -> 16, of which waited for: 11 -> 10; matrix products, arithmetic and copies ran while one was open for 1% -> 1% of each run, Pallas kernels for 12% -> 19%
where the time goes in v4:
time: 51.9 us; the launch traced here: 51.7 us
  starting transfers between devices  19.8 us (38%)
  Pallas kernels  19.4 us (37%)
  waiting for transfers between devices  10.9 us (21%)
  between operations  0.73 us (1%)
  local copies, waits for them, and re-layouts  0.61 us (1%)
    ppermute x16, starting transfers between devices, swap(): return lax.ppermute(x, axis, [(i, i ^ mask) for i in range(size)])  19.8 us
    ppermute x16, waiting for transfers between devices, swap(): return lax.ppermute(x, axis, [(i, i ^ mask) for i in range(size)])  10.9 us
    pallas_call x4, Pallas kernels, new_feedback(): pl.pallas_call(kernel, in_specs=[VMEM] * (2 + len(given)) + [ANY] * len(b...  8.78 us
    pallas_call x1, Pallas kernels, left_product(): pl.pallas_call(functools.partial(left_kernel, chunk), in_specs=[ANY] * 3,...  5.94 us
    pallas_call x1, Pallas kernels, factors(): pl.pallas_call(factor_kernel, in_specs=[VMEM], out_specs=[VMEM] * 3, out_...  3.12 us
    pallas_call x2, Pallas kernels, right_product(): pl.pallas_call(functools.partial(right_kernel, own), in_specs=[VMEM] * 3,...  1.48 us
  transfers between devices with their start and end apart: 16, of which 10 were waited for; matrix products, arithmetic and copies ran while one was open for 1% of the time, Pallas kernels for 19%

profile of v4, /device:TPU:1, one launch (start us, length us, event | category | flops | bytes accessed | tf_op | source)
XLA Modules:
  0.0 51.7 jit_solution(9184858413171511197)
XLA Ops:
  0.6 5.9 %left.1 = (f32[256,7168]{1,0:T(8,128)S(1)}, bf16[256,7168]{1,0:T(8,128)(2,1)S(1)}, bf16[256,7168]{1,0:T(8,128)(2,1)S(1)}, f32[32,256]{1,0:T(8,128)S(1)}) custom-call(bf16[256,7168]{1,0:T(8,128)(2,1)} %bitcast.17, f32[256,7168]{1,0:T(8,128)} %bitcast.16, f32[32,7168]{1,0:T(8,128)} %bitcast.18), custom_call_target="tpu_custom_call" | custom-call | flops 469762048 | bytes 11010048 | tf_op jit(solution)/shard_map/left/pallas_call | solution.py:80
  6.6 0.1 collective-permute-start
  6.7 1.2 %collective-permute-done = f32[32,256]{1,0:T(8,128)S(1)} collective-permute-done((f32[32,256]{1,0:T(8,128)S(1)}, f32[32,256]{1,0:T(8,128)S(1)}, u32[]{:S(2)}, u32[]{:S(2)}) %collective-permute-start) | collective-permute-done | bytes 32800 | tf_op jit(solution)/shard_map/ppermute | solution.py:263
  7.9 3.3 %collective-permute-start.3 = (f32[32,256]{1,0:T(8,128)S(1)}, f32[32,256]{1,0:T(8,128)S(1)}, u32[]{:S(2)}, u32[]{:S(2)}) collective-permute-start(f32[32,256]{1,0:T(8,128)S(1)} %add.30), channel_id=1, source_target_pairs={{0,24},{4,28},{8,16},{12,20},{16,8},{20,12},{24,0},{28,4},{1,25},{... | collective-permute-start | bytes 98312 | tf_op jit(solution)/shard_map/ppermute | solution.py:263
  11.2 0.2 collective-permute-start.2
  11.4 0.1 collective-permute-start.1
  11.5 0.9 %collective-permute-done.3 = f32[32,256]{1,0:T(8,128)S(1)} collective-permute-done((f32[32,256]{1,0:T(8,128)S(1)}, f32[32,256]{1,0:T(8,128)S(1)}, u32[]{:S(2)}, u32[]{:S(2)}) %collective-permute-start.3) | collective-permute-done | bytes 32800 | tf_op jit(solution)/shard_map/ppermute | solution.py:263
  12.5 1.5 %collective-permute-done.2 = f32[32,256]{1,0:T(8,128)S(1)} collective-permute-done((f32[32,256]{1,0:T(8,128)S(1)}, f32[32,256]{1,0:T(8,128)S(1)}, u32[]{:S(2)}, u32[]{:S(2)}) %collective-permute-start.2) | collective-permute-done | bytes 32800 | tf_op jit(solution)/shard_map/ppermute | solution.py:263
  13.9 0.2 collective-permute-done.1
  14.2 3.4 %collective-permute-start.6 = (f32[32,256]{1,0:T(8,128)S(1)}, f32[32,256]{1,0:T(8,128)S(1)}, u32[]{:S(2)}, u32[]{:S(2)}) collective-permute-start(f32[32,256]{1,0:T(8,128)S(1)} %add_add_fusion), channel_id=1, source_target_pairs={{0,3},{1,2},{2,1},{3,0},{4,7},{5,6},{6,5},{7,4},{8,11},{9,10},{10,... | collective-permute-start | bytes 98312 | tf_op jit(solution)/shard_map/ppermute | solution.py:263
  17.6 0.0 collective-permute-start.5
  17.6 0.4 collective-permute-start.4
  17.9 0.9 %collective-permute-done.6 = f32[32,256]{1,0:T(8,128)S(1)} collective-permute-done((f32[32,256]{1,0:T(8,128)S(1)}, f32[32,256]{1,0:T(8,128)S(1)}, u32[]{:S(2)}, u32[]{:S(2)}) %collective-permute-start.6) | collective-permute-done | bytes 32800 | tf_op jit(solution)/shard_map/ppermute | solution.py:263
  18.9 2.7 %collective-permute-done.5 = f32[32,256]{1,0:T(8,128)S(1)} collective-permute-done((f32[32,256]{1,0:T(8,128)S(1)}, f32[32,256]{1,0:T(8,128)S(1)}, u32[]{:S(2)}, u32[]{:S(2)}) %collective-permute-start.5) | collective-permute-done | bytes 32800 | tf_op jit(solution)/shard_map/ppermute | solution.py:263
  21.6 0.0 collective-permute-done.4
  21.6 0.7 %right.3 = f32[4,32,896]{2,1,0:T(8,128)S(1)} custom-call(f32[32,256]{1,0:T(8,128)S(1)} %add_multiply_fusion.left, bf16[256,7168]{1,0:T(8,128)(2,1)S(1)} %get-tuple-element.28.high, bf16[256,7168]{1,0:T(8,128)(2,1)S(1)} %get-tuple-element.29.low), custom_call_target="tpu_custom_call" | custom-call | flops 234881024 | bytes 3670016 | tf_op jit(solution)/shard_map/right/pallas_call | solution.py:122
  22.4 3.1 %collective-permute-start.7 = (f32[4,32,896]{2,1,0:T(8,128)S(1)}, f32[4,32,896]{2,1,0:T(8,128)S(1)}, u32[]{:S(2)}, u32[]{:S(2)}) collective-permute-start(f32[4,32,896]{2,1,0:T(8,128)S(1)} %right.3), channel_id=1, source_target_pairs={{0,4},{4,0},{8,12},{12,8},{16,20},{20,16},{24,28},{28,24},{1,5},{5... | collective-permute-start | bytes 1376264 | tf_op jit(solution)/shard_map/ppermute | solution.py:263
  25.5 0.7 %right.2.a = f32[4,32,896]{2,1,0:T(8,128)S(1)} custom-call(f32[32,256]{1,0:T(8,128)S(1)} %add_multiply_fusion.left, bf16[256,7168]{1,0:T(8,128)(2,1)S(1)} %get-tuple-element.28.high, bf16[256,7168]{1,0:T(8,128)(2,1)S(1)} %get-tuple-element.29.low), custom_call_target="tpu_custom_call" | custom-call | flops 234881024 | bytes 3670016 | tf_op jit(solution)/shard_map/right/pallas_call | solution.py:122
  26.2 0.7 %collective-permute-done.7.b = f32[4,32,896]{2,1,0:T(8,128)S(1)} collective-permute-done((f32[4,32,896]{2,1,0:T(8,128)S(1)}, f32[4,32,896]{2,1,0:T(8,128)S(1)}, u32[]{:S(2)}, u32[]{:S(2)}) %collective-permute-start.7) | collective-permute-done | bytes 458784 | tf_op jit(solution)/shard_map/ppermute | solution.py:263
  27.0 0.3 collective-permute-start.8
  27.3 1.2 %collective-permute-start.9 = (f32[32,896]{1,0:T(8,128)S(1)}, f32[32,896]{1,0:T(8,128)S(1)}, u32[]{:S(2)}, u32[]{:S(2)}) collective-permute-start(f32[32,896]{1,0:T(8,128)S(1)} %get-tuple-element.32), channel_id=1, source_target_pairs={{0,16},{4,20},{8,24},{12,28},{16,0},{20,4},{24,8},{28,12},{1,17},{... | collective-permute-start | bytes 344072 | tf_op jit(solution)/shard_map/ppermute | solution.py:263
  28.6 1.2 %collective-permute-start.10 = (f32[32,896]{1,0:T(8,128)S(1)}, f32[32,896]{1,0:T(8,128)S(1)}, u32[]{:S(2)}, u32[]{:S(2)}) collective-permute-start(f32[32,896]{1,0:T(8,128)S(1)} %get-tuple-element.33), channel_id=1, source_target_pairs={{0,24},{4,28},{8,16},{12,20},{16,8},{20,12},{24,0},{28,4},{1,25},{... | collective-permute-start | bytes 344072 | tf_op jit(solution)/shard_map/ppermute | solution.py:263
  29.7 3.1 %factor.1 = (f32[32,32]{1,0:T(8,128)S(1)}, f32[32,256]{1,0:T(8,128)S(1)}, bf16[256,128]{1,0:T(8,128)(2,1)S(1)}) custom-call(f32[32,256]{1,0:T(8,128)S(1)} %add_multiply_fusion.left), custom_call_target="tpu_custom_call" | custom-call | flops 2000000000 | bytes 1000000 | tf_op jit(solution)/shard_map/factor/pallas_call | solution.py:176
  32.8 0.0 collective-permute-done.8
  32.9 0.0 collective-permute-done.9
  32.9 2.0 %collective-permute-done.10 = f32[32,896]{1,0:T(8,128)S(1)} collective-permute-done((f32[32,896]{1,0:T(8,128)S(1)}, f32[32,896]{1,0:T(8,128)S(1)}, u32[]{:S(2)}, u32[]{:S(2)}) %collective-permute-start.10) | collective-permute-done | bytes 114720 | tf_op jit(solution)/shard_map/ppermute | solution.py:263
  34.8 0.2 convolution_multiply_fusion.refs_0_
  35.1 0.3 collective-permute-start.11
  35.4 2.7 %collective-permute-start.13 = (f32[32,896]{1,0:T(8,128)S(1)}, f32[32,896]{1,0:T(8,128)S(1)}, u32[]{:S(2)}, u32[]{:S(2)}) collective-permute-start(f32[32,896]{1,0:T(8,128)S(1)} %convolution_multiply_fusion.refs_0_), channel_id=1, source_target_pairs={{0,4},{4,0},{8,12},{12,8},{16,20},{20,16},{24,28},{28,24},{1,5},{5... | collective-permute-start | bytes 344072 | tf_op jit(solution)/shard_map/ppermute | solution.py:263
  38.1 0.2 collective-permute-start.14
  38.3 0.9 %collective-permute-start.12 = (f32[32,896]{1,0:T(8,128)S(1)}, f32[32,896]{1,0:T(8,128)S(1)}, u32[]{:S(2)}, u32[]{:S(2)}) collective-permute-start(f32[32,896]{1,0:T(8,128)S(1)} %convolution_multiply_fusion.refs_0_), channel_id=1, source_target_pairs={{0,8},{4,12},{8,0},{12,4},{16,24},{20,28},{24,16},{28,20},{1,9},{5... | collective-permute-start | bytes 344072 | tf_op jit(solution)/shard_map/ppermute | solution.py:263
  39.3 0.4 collective-permute-done.11.refs_0_
  39.7 0.0 collective-permute-done.13.refs_1_
  39.7 2.2 %feedback.4 = (f32[256,7168]{1,0:T(8,128)}, f32[32,7168]{1,0:T(8,128)}, f32[8,128]{1,0:T(8,128)}) custom-call(bf16[256,128]{1,0:T(8,128)(2,1)S(1)} %get-tuple-element.26.stacked, f32[32,896]{1,0:T(8,128)S(1)} %convolution_multiply_fusion.refs_0_, f32[32,896]{1,0:T(8,128)S(1)} %collective-permute-done.13.refs_1_, ...), custom_call_target="tpu_custom_call" | custom-call | flops 117440512 | bytes 1835008 | tf_op jit(solution)/shard_map/feedback/pallas_call | solution.py:241
  41.9 1.8 %feedback.5 = (f32[256,7168]{1,0:T(8,128)}, f32[32,7168]{1,0:T(8,128)}, f32[8,128]{1,0:T(8,128)}) custom-call(bf16[256,128]{1,0:T(8,128)(2,1)S(1)} %get-tuple-element.26.stacked, f32[32,896]{1,0:T(8,128)S(1)} %collective-permute-done.11.refs_0_, f32[256,7168]{1,0:T(8,128)S(1)} %get-tuple-element.34.refs_2_.refs_1_, ...), custom_call_target="tpu_custom_call", output_to_operand_aliasing={{0}: (3, {}), {1}: (4, {})} | custom-call | flops 58720256 | bytes 917504 | tf_op jit(solution)/shard_map/feedback/pallas_call | solution.py:241
  43.8 0.3 collective-permute-done.14.refs_1_
  44.1 0.0 collective-permute-done.12.refs_0_
  44.1 2.2 %collective-permute-start.15 = (f32[3,32,896]{2,1,0:T(8,128)S(1)}, f32[3,32,896]{2,1,0:T(8,128)S(1)}, u32[]{:S(2)}, u32[]{:S(2)}) collective-permute-start(f32[3,32,896]{2,1,0:T(8,128)S(1)} %pad_maximum_fusion), channel_id=1, source_target_pairs={{0,4},{4,0},{8,12},{12,8},{16,20},{20,16},{24,28},{28,24},{1,5},{5... | collective-permute-start | bytes 1032200 | tf_op jit(solution)/shard_map/ppermute | solution.py:263
  46.3 0.6 %copy.18 = f32[256,32]{0,1:T(8,128)} copy(f32[256,32]{0,1:T(8,128)S(1)} %bitcast.10) | data formatting | bytes 65536
  46.9 2.2 %feedback.6 = (f32[256,7168]{1,0:T(8,128)}, f32[32,7168]{1,0:T(8,128)}, f32[8,128]{1,0:T(8,128)}) custom-call(bf16[256,128]{1,0:T(8,128)(2,1)S(1)} %get-tuple-element.26.stacked, f32[32,896]{1,0:T(8,128)S(1)} %collective-permute-done.12.refs_0_, f32[32,896]{1,0:T(8,128)S(1)} %collective-permute-done.14.refs_1_, ...), custom_call_target="tpu_custom_call", output_to_operand_aliasing={{0}: (4, {}), {1}: (5, {})} | custom-call | flops 117440512 | bytes 1835008 | tf_op jit(solution)/shard_map/feedback/pallas_call | solution.py:241
  49.1 0.0 collective-permute-done.15.refs_0_
  49.1 2.6 %feedback.7 = (f32[256,7168]{1,0:T(8,128)}, f32[32,7168]{1,0:T(8,128)}, f32[8,128]{1,0:T(8,128)}) custom-call(bf16[256,128]{1,0:T(8,128)(2,1)S(1)} %get-tuple-element.26.stacked, f32[3,32,896]{2,1,0:T(8,128)S(1)} %collective-permute-done.15.refs_0_, f32[256,7168]{1,0:T(8,128)S(1)} %get-tuple-element.34.refs_2_.refs_1_, ...), custom_call_target="tpu_custom_call", output_to_operand_aliasing={{0}: (3, {}), {1}: (4, {})} | custom-call | flops 176160768 | bytes 2752512 | tf_op jit(solution)/shard_map/feedback/pallas_call | solution.py:241
  (5 shorter events, 0.1 us)
Async XLA Ops:
  6.6 1.3 %collective-permute-start = (f32[32,256]{1,0:T(8,128)S(1)}, f32[32,256]{1,0:T(8,128)S(1)}, u32[]{:S(2)}, u32[]{:S(2)}) collective-permute-start(f32[32,256]{1,0:T(8,128)S(1)} %get-tuple-element.25), channel_id=1, source_target_pairs={{0,4},{4,0},{8,12},{12,8},{16,20},{20,16},{24,28},{28,24},{1,5},{5... | collective-permute-start | bytes 98312 | tf_op jit(solution)/shard_map/ppermute | solution.py:263
  7.9 4.6 %collective-permute-start.3 = (f32[32,256]{1,0:T(8,128)S(1)}, f32[32,256]{1,0:T(8,128)S(1)}, u32[]{:S(2)}, u32[]{:S(2)}) collective-permute-start(f32[32,256]{1,0:T(8,128)S(1)} %add.30), channel_id=1, source_target_pairs={{0,24},{4,28},{8,16},{12,20},{16,8},{20,12},{24,0},{28,4},{1,25},{... | collective-permute-start | bytes 98312 | tf_op jit(solution)/shard_map/ppermute | solution.py:263
  11.2 2.8 %collective-permute-start.2 = (f32[32,256]{1,0:T(8,128)S(1)}, f32[32,256]{1,0:T(8,128)S(1)}, u32[]{:S(2)}, u32[]{:S(2)}) collective-permute-start(f32[32,256]{1,0:T(8,128)S(1)} %add.30), channel_id=1, source_target_pairs={{0,16},{4,20},{8,24},{12,28},{16,0},{20,4},{24,8},{28,12},{1,17},{... | collective-permute-start | bytes 98312 | tf_op jit(solution)/shard_map/ppermute | solution.py:263
  11.4 2.8 %collective-permute-start.1 = (f32[32,256]{1,0:T(8,128)S(1)}, f32[32,256]{1,0:T(8,128)S(1)}, u32[]{:S(2)}, u32[]{:S(2)}) collective-permute-start(f32[32,256]{1,0:T(8,128)S(1)} %add.30), channel_id=1, source_target_pairs={{0,8},{4,12},{8,0},{12,4},{16,24},{20,28},{24,16},{28,20},{1,9},{5... | collective-permute-start | bytes 98312 | tf_op jit(solution)/shard_map/ppermute | solution.py:263
  14.2 4.7 %collective-permute-start.6 = (f32[32,256]{1,0:T(8,128)S(1)}, f32[32,256]{1,0:T(8,128)S(1)}, u32[]{:S(2)}, u32[]{:S(2)}) collective-permute-start(f32[32,256]{1,0:T(8,128)S(1)} %add_add_fusion), channel_id=1, source_target_pairs={{0,3},{1,2},{2,1},{3,0},{4,7},{5,6},{6,5},{7,4},{8,11},{9,10},{10,... | collective-permute-start | bytes 98312 | tf_op jit(solution)/shard_map/ppermute | solution.py:263
  17.6 4.1 %collective-permute-start.5 = (f32[32,256]{1,0:T(8,128)S(1)}, f32[32,256]{1,0:T(8,128)S(1)}, u32[]{:S(2)}, u32[]{:S(2)}) collective-permute-start(f32[32,256]{1,0:T(8,128)S(1)} %add_add_fusion), channel_id=1, source_target_pairs={{0,2},{1,3},{2,0},{3,1},{4,6},{5,7},{6,4},{7,5},{8,10},{9,11},{10,... | collective-permute-start | bytes 98312 | tf_op jit(solution)/shard_map/ppermute | solution.py:263
  17.6 4.1 %collective-permute-start.4 = (f32[32,256]{1,0:T(8,128)S(1)}, f32[32,256]{1,0:T(8,128)S(1)}, u32[]{:S(2)}, u32[]{:S(2)}) collective-permute-start(f32[32,256]{1,0:T(8,128)S(1)} %add_add_fusion), channel_id=1, source_target_pairs={{0,1},{1,0},{2,3},{3,2},{4,5},{5,4},{6,7},{7,6},{8,9},{9,8},{10,11... | collective-permute-start | bytes 98312 | tf_op jit(solution)/shard_map/ppermute | solution.py:263
  22.4 4.6 %collective-permute-start.7 = (f32[4,32,896]{2,1,0:T(8,128)S(1)}, f32[4,32,896]{2,1,0:T(8,128)S(1)}, u32[]{:S(2)}, u32[]{:S(2)}) collective-permute-start(f32[4,32,896]{2,1,0:T(8,128)S(1)} %right.3), channel_id=1, source_target_pairs={{0,4},{4,0},{8,12},{12,8},{16,20},{20,16},{24,28},{28,24},{1,5},{5... | collective-permute-start | bytes 1376264 | tf_op jit(solution)/shard_map/ppermute | solution.py:263
  27.0 5.8 %collective-permute-start.8 = (f32[32,896]{1,0:T(8,128)S(1)}, f32[32,896]{1,0:T(8,128)S(1)}, u32[]{:S(2)}, u32[]{:S(2)}) collective-permute-start(f32[32,896]{1,0:T(8,128)S(1)} %get-tuple-element.31), channel_id=1, source_target_pairs={{0,8},{4,12},{8,0},{12,4},{16,24},{20,28},{24,16},{28,20},{1,9},{5... | collective-permute-start | bytes 344072 | tf_op jit(solution)/shard_map/ppermute | solution.py:263
  27.3 5.5 %collective-permute-start.9 = (f32[32,896]{1,0:T(8,128)S(1)}, f32[32,896]{1,0:T(8,128)S(1)}, u32[]{:S(2)}, u32[]{:S(2)}) collective-permute-start(f32[32,896]{1,0:T(8,128)S(1)} %get-tuple-element.32), channel_id=1, source_target_pairs={{0,16},{4,20},{8,24},{12,28},{16,0},{20,4},{24,8},{28,12},{1,17},{... | collective-permute-start | bytes 344072 | tf_op jit(solution)/shard_map/ppermute | solution.py:263
  28.6 6.3 %collective-permute-start.10 = (f32[32,896]{1,0:T(8,128)S(1)}, f32[32,896]{1,0:T(8,128)S(1)}, u32[]{:S(2)}, u32[]{:S(2)}) collective-permute-start(f32[32,896]{1,0:T(8,128)S(1)} %get-tuple-element.33), channel_id=1, source_target_pairs={{0,24},{4,28},{8,16},{12,20},{16,8},{20,12},{24,0},{28,4},{1,25},{... | collective-permute-start | bytes 344072 | tf_op jit(solution)/shard_map/ppermute | solution.py:263
  35.1 4.6 %collective-permute-start.11 = (f32[32,896]{1,0:T(8,128)S(1)}, f32[32,896]{1,0:T(8,128)S(1)}, u32[]{:S(2)}, u32[]{:S(2)}) collective-permute-start(f32[32,896]{1,0:T(8,128)S(1)} %convolution_multiply_fusion.refs_0_), channel_id=1, source_target_pairs={{0,24},{4,28},{8,16},{12,20},{16,8},{20,12},{24,0},{28,4},{1,25},{... | collective-permute-start | bytes 344072 | tf_op jit(solution)/shard_map/ppermute | solution.py:263
  35.4 4.3 %collective-permute-start.13 = (f32[32,896]{1,0:T(8,128)S(1)}, f32[32,896]{1,0:T(8,128)S(1)}, u32[]{:S(2)}, u32[]{:S(2)}) collective-permute-start(f32[32,896]{1,0:T(8,128)S(1)} %convolution_multiply_fusion.refs_0_), channel_id=1, source_target_pairs={{0,4},{4,0},{8,12},{12,8},{16,20},{20,16},{24,28},{28,24},{1,5},{5... | collective-permute-start | bytes 344072 | tf_op jit(solution)/shard_map/ppermute | solution.py:263
  38.1 6.0 %collective-permute-start.14 = (f32[32,896]{1,0:T(8,128)S(1)}, f32[32,896]{1,0:T(8,128)S(1)}, u32[]{:S(2)}, u32[]{:S(2)}) collective-permute-start(f32[32,896]{1,0:T(8,128)S(1)} %convolution_multiply_fusion.refs_0_), channel_id=1, source_target_pairs={{0,16},{4,20},{8,24},{12,28},{16,0},{20,4},{24,8},{28,12},{1,17},{... | collective-permute-start | bytes 344072 | tf_op jit(solution)/shard_map/ppermute | solution.py:263
  38.3 5.7 %collective-permute-start.12 = (f32[32,896]{1,0:T(8,128)S(1)}, f32[32,896]{1,0:T(8,128)S(1)}, u32[]{:S(2)}, u32[]{:S(2)}) collective-permute-start(f32[32,896]{1,0:T(8,128)S(1)} %convolution_multiply_fusion.refs_0_), channel_id=1, source_target_pairs={{0,8},{4,12},{8,0},{12,4},{16,24},{20,28},{24,16},{28,20},{1,9},{5... | collective-permute-start | bytes 344072 | tf_op jit(solution)/shard_map/ppermute | solution.py:263
  44.1 5.0 %collective-permute-start.15 = (f32[3,32,896]{2,1,0:T(8,128)S(1)}, f32[3,32,896]{2,1,0:T(8,128)S(1)}, u32[]{:S(2)}, u32[]{:S(2)}) collective-permute-start(f32[3,32,896]{2,1,0:T(8,128)S(1)} %pad_maximum_fusion), channel_id=1, source_target_pairs={{0,4},{4,0},{8,12},{12,8},{16,20},{20,16},{24,28},{28,24},{1,5},{5... | collective-permute-start | bytes 1032200 | tf_op jit(solution)/shard_map/ppermute | solution.py:263

commit v5 on v3

--- a/solution.py
+++ b/solution.py
@@ -76,7 +76,7 @@
 def left_product(gradient, feedback, right, padded):
     rows, columns = gradient.shape
     rank = right.shape[0]
-    chunk = 512 if columns % 512 == 0 else 128
+    chunk = next(c for c in (1024, 512, 128) if columns % c == 0)
     return pl.pallas_call(
         functools.partial(left_kernel, chunk),
         in_specs=[ANY] * 3,
@@ -98,7 +98,8 @@
     )(gradient, feedback, right)
 
 
-def right_kernel(own, left, high, low, pieces):
+def right_kernel(own, left, high, low, *refs):
+    *before, pieces = refs
     chips, rank, width = pieces.shape
     half = chips * width
     core, _ = position()
@@ -113,21 +114,23 @@
         while start < (i + 1) * block:
             piece = start // width
             stop = min((i + 1) * block, (piece + 1) * width)
-            pieces[piece, :, start - piece * width : stop - piece * width] = total[:, start - i * block : stop - i * block]
+            there = (piece, slice(None), slice(start - piece * width, stop - piece * width))
+            part = total[:, start - i * block : stop - i * block]
+            pieces[there] = before[0][there] + part if before else part
             start = stop
 
 
-def right_product(own, left, high, low, chips, width):
+def right_product(own, left, high, low, chips, width, *before):
     rank, rows = left.shape
     return pl.pallas_call(
         functools.partial(right_kernel, own),
-        in_specs=[VMEM] * 3,
+        in_specs=[VMEM] * (3 + len(before)),
         out_specs=VMEM,
         out_shape=pltpu.VMEM((chips, rank, width), F32),
         compiler_params=params(8),
         cost_estimate=cost(8 * rows * chips * width * rank, 4 * rows * chips * width),
         name="right",
-    )(left, high, low)
+    )(left, high, low, *before)
 
 
 def share_kernel(a, b, *outs):
@@ -188,14 +191,16 @@
     )(left)
 
 
-def feedback_kernel(own, aliased, columns, stacked, pieces, combined, *refs):
-    feedback, right, feedback_buf, sems = refs[2 * aliased :]
+def feedback_kernel(own, columns, stacked, pieces, combined, factor, feedback, right, factor_out, feedback_buf, sems, factor_sem):
     rank = pieces[0].shape[-2]
     chips, rows, width = feedback_buf.shape
     whole = combined.shape[1] == columns
     core, chip = position()
     side = core if own else 1 - core
     copies = []
+    if own:
+        factor_copy = pltpu.make_async_copy(factor, factor_out, factor_sem)
+        factor_copy.start()
     for k in range(chips):
         place = side * chips + (chip ^ k)
         at = pl.ds(pl.multiple_of(place * width, 128), width)
@@ -213,6 +218,8 @@
         start_or_wait(copies[-1], whole, "start")
     for copy in copies:
         start_or_wait(copy, whole, "wait")
+    if own:
+        factor_copy.wait()
 
 
 def start_or_wait(copy, whole, action):
@@ -228,32 +235,42 @@
         pl.when(inside)(run)
 
 
-def new_feedback(own, stacked, pieces, combined, columns, before=()):
+def new_feedback(own, stacked, pieces, combined, columns, last):
     rows = combined.shape[0]
-    separate = isinstance(pieces, list)
-    chips = len(pieces) if separate else pieces.shape[0]
-    rank, width = (pieces[0] if separate else pieces).shape[-2:]
-    given = pieces if separate else [pieces]
+    given = pieces if own else [pieces]
+    chips = len(pieces) if own else pieces.shape[0]
+    rank, width = given[0].shape[-2:]
+    outs = 3 if own else 2
 
     def kernel(stacked, *refs):
-        mine = refs[: len(given)]
-        parts = list(mine) if separate else [mine[0].at[k] for k in range(chips)]
-        feedback_kernel(own, len(before) // 2, columns, stacked, parts, *refs[len(given) :])
+        parts, rest = refs[: len(given)], refs[len(given) :]
+        if own:
+            combined, factor, feedback, right, factor_out, *scratch = rest
+        else:
+            parts = [parts[0].at[k] for k in range(chips)]
+            combined, _, _, feedback, right, *scratch = rest
+            factor = factor_out = None
+        feedback_kernel(own, columns, stacked, parts, combined, factor, feedback, right, factor_out, *scratch)
 
     return pl.pallas_call(
         kernel,
-        in_specs=[VMEM] * (2 + len(given)) + [ANY] * len(before),
-        out_specs=[ANY] * 2,
-        out_shape=[jax.ShapeDtypeStruct((rows, columns), F32), jax.ShapeDtypeStruct((rank, columns), F32)],
-        input_output_aliases={2 + len(given) + i: i for i in range(len(before))},
+        in_specs=[VMEM] * (2 + len(given)) + ([VMEM] if own else [ANY] * 2),
+        out_specs=[ANY] * outs,
+        out_shape=[
+            pltpu.HBM((rows, columns), F32),
+            pltpu.HBM((rank, columns), F32),
+            pltpu.HBM((rank, rows), F32),
+        ][:outs],
+        input_output_aliases={} if own else {3: 0, 4: 1},
         scratch_shapes=[
             pltpu.VMEM((chips, rows, width), F32),
             pltpu.SemaphoreType.DMA((2, chips)),
+            pltpu.SemaphoreType.DMA,
         ],
         compiler_params=params(16),
         cost_estimate=cost(8 * rows * chips * width * rank, 4 * rows * chips * width),
         name="feedback",
-    )(stacked, *given, combined, *before)
+    )(stacked, *given, combined, *last)
 
 
 def swap(x, axis, mask):
@@ -292,21 +309,24 @@
     given = [keep(x, pltpu.HBM) for x in (gradient, feedback, right_factor.T)]
     combined, high, low, left = left_product(*given, replicas * width)
     combined, high, low = (keep(x, pltpu.VMEM) for x in (combined, high, low))
-    left = sum_over(left, "dp", 0, 1)
     left = sum_over(left, "dp", 1, bits("dp"))
-    left = sum_over(left, "tensor", 0, bits("tensor")) / replicas
-
-    theirs = swap(right_product(False, left, high, low, chips, width), "dp", 1)
-    own, *away = share(right_product(True, left, high, low, chips, width), theirs)
+    left = sum_over(left, "tensor", 0, bits("tensor"))
+
+    beside = swap(left, "dp", 1)
+    theirs, half = (right_product(side, left, high, low, chips, width) for side in (False, True))
+    theirs = swap(right_product(False, beside, high, low, chips, width, theirs), "dp", 1)
+    half = right_product(True, beside, high, low, chips, width, half)
+    left = (left + beside) / replicas
+    own, *away = share(half, theirs)
     own = tree([own] + [swap(x, "dp", 2 * k) for k, x in enumerate(away, 1)])
 
     inverse, factor, stacked = factors(left)
-    own = jnp.dot(inverse, own, precision=HIGHEST, preferred_element_type=F32) / replicas
+    own = jnp.dot(inverse, own, precision=HIGHEST, preferred_element_type=F32) / replicas**2
 
     got = [own] + [swap(own, "dp", 2 * k) for k in range(1, chips)]
     other = swap(jnp.stack(got), "dp", 1)
-    outs = new_feedback(True, stacked, got, combined, columns)
-    outs = new_feedback(False, stacked, other, combined, columns, tuple(outs))
+    *outs, factor = new_feedback(True, stacked, got, combined, columns, [factor])
+    outs = new_feedback(False, stacked, other, combined, columns, outs)
     return (outs[0][None], factor.T, outs[1].T)
 
 

time: 49.5 us -> 49.3 us (level)
  starting transfers between devices: 19.1 us -> 17.8 us
  Pallas kernels: 15.5 us -> 16.7 us
  local copies, waits for them, and re-layouts: 0.61 us -> 0 us
  waiting for transfers between devices: 13.1 us -> 13.6 us
    pallas_call x4 -> x6, Pallas kernels: 6.13 us -> 7.63 us  [the longest x2 4.67 us: new_feedback(): pl.pallas_call(kernel, in_specs=[VMEM] * (2 + len(given)) + ([VMEM] if ow...]
    ppermute x15, starting transfers between devices: 19.1 us -> 17.8 us  [swap(): return lax.ppermute(x, axis, [(i, i ^ mask) for i in range(size)])]
    unnamed x1 -> x0, local copies, waits for them, and re-layouts: 0.61 us -> none
  transfers between devices with their start and end apart: 15 -> 15, of which waited for: 11 -> 9; matrix products, arithmetic and copies ran while one was open for 1% -> 0% of each run, Pallas kernels for 12% -> 16%
where the time goes in v5:
time: 49.3 us; the launch traced here: 49.1 us
  starting transfers between devices  17.8 us (36%)
  Pallas kernels  16.7 us (34%)
  waiting for transfers between devices  13.6 us (28%)
  between operations  0.74 us (2%)
    ppermute x15, starting transfers between devices, swap(): return lax.ppermute(x, axis, [(i, i ^ mask) for i in range(size)])  17.8 us
    ppermute x15, waiting for transfers between devices, swap(): return lax.ppermute(x, axis, [(i, i ^ mask) for i in range(size)])  13.6 us
    pallas_call x1, Pallas kernels, left_product(): pl.pallas_call(functools.partial(left_kernel, chunk), in_specs=[ANY] * 3,...  5.94 us
    pallas_call x2, Pallas kernels, new_feedback(): pl.pallas_call(kernel, in_specs=[VMEM] * (2 + len(given)) + ([VMEM] if ow...  4.67 us
    pallas_call x1, Pallas kernels, factors(): pl.pallas_call(factor_kernel, in_specs=[VMEM], out_specs=[VMEM] * 3, out_...  3.12 us
    pallas_call x4, Pallas kernels, right_product(): pl.pallas_call(functools.partial(right_kernel, own), in_specs=[VMEM] * (3...  2.96 us
  transfers between devices with their start and end apart: 15, of which 9 were waited for; matrix products, arithmetic and copies ran while one was open for 0% of the time, Pallas kernels for 16%

profile of v5, /device:TPU:1, one launch (start us, length us, event | category | flops | bytes accessed | tf_op | source)
XLA Modules:
  0.0 49.1 jit_solution(7671709917567143804)
XLA Ops:
  0.6 5.9 %left.1 = (f32[256,7168]{1,0:T(8,128)S(1)}, bf16[256,7168]{1,0:T(8,128)(2,1)S(1)}, bf16[256,7168]{1,0:T(8,128)(2,1)S(1)}, f32[32,256]{1,0:T(8,128)S(1)}) custom-call(bf16[256,7168]{1,0:T(8,128)(2,1)} %bitcast.17, f32[256,7168]{1,0:T(8,128)} %bitcast.15, f32[32,7168]{1,0:T(8,128)} %bitcast.18), custom_call_target="tpu_custom_call" | custom-call | flops 469762048 | bytes 11010048 | tf_op jit(solution)/shard_map/left/pallas_call | solution.py:80
  6.6 3.1 %collective-permute-start.2 = (f32[32,256]{1,0:T(8,128)S(1)}, f32[32,256]{1,0:T(8,128)S(1)}, u32[]{:S(2)}, u32[]{:S(2)}) collective-permute-start(f32[32,256]{1,0:T(8,128)S(1)} %get-tuple-element.19), channel_id=1, source_target_pairs={{0,24},{4,28},{8,16},{12,20},{16,8},{20,12},{24,0},{28,4},{1,25},{... | collective-permute-start | bytes 98312 | tf_op jit(solution)/shard_map/ppermute | solution.py:278
  9.6 0.2 collective-permute-start.1
  9.9 0.1 collective-permute-start
  10.0 0.9 %collective-permute-done.2 = f32[32,256]{1,0:T(8,128)S(1)} collective-permute-done((f32[32,256]{1,0:T(8,128)S(1)}, f32[32,256]{1,0:T(8,128)S(1)}, u32[]{:S(2)}, u32[]{:S(2)}) %collective-permute-start.2) | collective-permute-done | bytes 32800 | tf_op jit(solution)/shard_map/ppermute | solution.py:278
  10.9 1.5 %collective-permute-done.1 = f32[32,256]{1,0:T(8,128)S(1)} collective-permute-done((f32[32,256]{1,0:T(8,128)S(1)}, f32[32,256]{1,0:T(8,128)S(1)}, u32[]{:S(2)}, u32[]{:S(2)}) %collective-permute-start.1) | collective-permute-done | bytes 32800 | tf_op jit(solution)/shard_map/ppermute | solution.py:278
  12.4 0.3 collective-permute-done
  12.7 3.4 %collective-permute-start.5 = (f32[32,256]{1,0:T(8,128)S(1)}, f32[32,256]{1,0:T(8,128)S(1)}, u32[]{:S(2)}, u32[]{:S(2)}) collective-permute-start(f32[32,256]{1,0:T(8,128)S(1)} %add_add_fusion.1), channel_id=1, source_target_pairs={{0,3},{1,2},{2,1},{3,0},{4,7},{5,6},{6,5},{7,4},{8,11},{9,10},{10,... | collective-permute-start | bytes 98312 | tf_op jit(solution)/shard_map/ppermute | solution.py:278
  16.1 0.0 collective-permute-start.4
  16.1 0.4 collective-permute-start.3
  16.4 0.9 %collective-permute-done.5 = f32[32,256]{1,0:T(8,128)S(1)} collective-permute-done((f32[32,256]{1,0:T(8,128)S(1)}, f32[32,256]{1,0:T(8,128)S(1)}, u32[]{:S(2)}, u32[]{:S(2)}) %collective-permute-start.5) | collective-permute-done | bytes 32800 | tf_op jit(solution)/shard_map/ppermute | solution.py:278
  17.4 2.7 %collective-permute-done.4 = f32[32,256]{1,0:T(8,128)S(1)} collective-permute-done((f32[32,256]{1,0:T(8,128)S(1)}, f32[32,256]{1,0:T(8,128)S(1)}, u32[]{:S(2)}, u32[]{:S(2)}) %collective-permute-start.4) | collective-permute-done | bytes 32800 | tf_op jit(solution)/shard_map/ppermute | solution.py:278
  20.0 0.0 collective-permute-done.3
  20.1 3.5 %collective-permute-start.6 = (f32[32,256]{1,0:T(8,128)S(1)}, f32[32,256]{1,0:T(8,128)S(1)}, u32[]{:S(2)}, u32[]{:S(2)}) collective-permute-start(f32[32,256]{1,0:T(8,128)S(1)} %add_add_fusion.left), channel_id=1, source_target_pairs={{0,4},{4,0},{8,12},{12,8},{16,20},{20,16},{24,28},{28,24},{1,5},{5... | collective-permute-start | bytes 98312 | tf_op jit(solution)/shard_map/ppermute | solution.py:278
  23.6 0.7 %right.6.refs_0_ = f32[4,32,896]{2,1,0:T(8,128)S(1)} custom-call(f32[32,256]{1,0:T(8,128)S(1)} %add_add_fusion.left, bf16[256,7168]{1,0:T(8,128)(2,1)S(1)} %get-tuple-element.22.high, bf16[256,7168]{1,0:T(8,128)(2,1)S(1)} %get-tuple-element.23.low), custom_call_target="tpu_custom_call" | custom-call | flops 234881024 | bytes 3670016 | tf_op jit(solution)/shard_map/right/pallas_call | solution.py:125
  24.3 0.1 collective-permute-done.6.left
  24.5 0.7 %right.7 = f32[4,32,896]{2,1,0:T(8,128)S(1)} custom-call(f32[32,256]{1,0:T(8,128)S(1)} %collective-permute-done.6.left, bf16[256,7168]{1,0:T(8,128)(2,1)S(1)} %get-tuple-element.22.high, bf16[256,7168]{1,0:T(8,128)(2,1)S(1)} %get-tuple-element.23.low, f32[4,32,896]{2,1,0:T(8,128)S(1)} %right.6.refs_0_), custom_call_target="tpu_custom_call" | custom-call | flops 234881024 | bytes 3670016 | tf_op jit(solution)/shard_map/right/pallas_call | solution.py:125
  25.2 0.4 collective-permute-start.7
  25.6 0.7 %right.4.refs_0_ = f32[4,32,896]{2,1,0:T(8,128)S(1)} custom-call(f32[32,256]{1,0:T(8,128)S(1)} %add_add_fusion.left, bf16[256,7168]{1,0:T(8,128)(2,1)S(1)} %get-tuple-element.22.high, bf16[256,7168]{1,0:T(8,128)(2,1)S(1)} %get-tuple-element.23.low), custom_call_target="tpu_custom_call" | custom-call | flops 234881024 | bytes 3670016 | tf_op jit(solution)/shard_map/right/pallas_call | solution.py:125
  26.3 0.8 %right.5.a = f32[4,32,896]{2,1,0:T(8,128)S(1)} custom-call(f32[32,256]{1,0:T(8,128)S(1)} %collective-permute-done.6.left, bf16[256,7168]{1,0:T(8,128)(2,1)S(1)} %get-tuple-element.22.high, bf16[256,7168]{1,0:T(8,128)(2,1)S(1)} %get-tuple-element.23.low, f32[4,32,896]{2,1,0:T(8,128)S(1)} %right.4.refs_0_), custom_call_target="tpu_custom_call" | custom-call | flops 234881024 | bytes 3670016 | tf_op jit(solution)/shard_map/right/pallas_call | solution.py:125
  27.1 0.0 collective-permute-done.7.b
  27.1 0.1 share.1
  27.2 0.3 collective-permute-start.8
  27.5 1.2 %collective-permute-start.9 = (f32[32,896]{1,0:T(8,128)S(1)}, f32[32,896]{1,0:T(8,128)S(1)}, u32[]{:S(2)}, u32[]{:S(2)}) collective-permute-start(f32[32,896]{1,0:T(8,128)S(1)} %get-tuple-element.26), channel_id=1, source_target_pairs={{0,16},{4,20},{8,24},{12,28},{16,0},{20,4},{24,8},{28,12},{1,17},{... | collective-permute-start | bytes 344072 | tf_op jit(solution)/shard_map/ppermute | solution.py:278
  28.7 1.2 %collective-permute-start.10 = (f32[32,896]{1,0:T(8,128)S(1)}, f32[32,896]{1,0:T(8,128)S(1)}, u32[]{:S(2)}, u32[]{:S(2)}) collective-permute-start(f32[32,896]{1,0:T(8,128)S(1)} %get-tuple-element.27), channel_id=1, source_target_pairs={{0,24},{4,28},{8,16},{12,20},{16,8},{20,12},{24,0},{28,4},{1,25},{... | collective-permute-start | bytes 344072 | tf_op jit(solution)/shard_map/ppermute | solution.py:278
  29.9 3.1 %factor.1 = (f32[32,32]{1,0:T(8,128)S(1)}, f32[32,256]{1,0:T(8,128)S(1)}, bf16[256,128]{1,0:T(8,128)(2,1)S(1)}) custom-call(f32[32,256]{1,0:T(8,128)S(1)} %add_multiply_fusion.left), custom_call_target="tpu_custom_call" | custom-call | flops 2000000000 | bytes 1000000 | tf_op jit(solution)/shard_map/factor/pallas_call | solution.py:179
  33.0 0.0 collective-permute-done.8
  33.0 0.0 collective-permute-done.9
  33.0 2.1 %collective-permute-done.10 = f32[32,896]{1,0:T(8,128)S(1)} collective-permute-done((f32[32,896]{1,0:T(8,128)S(1)}, f32[32,896]{1,0:T(8,128)S(1)}, u32[]{:S(2)}, u32[]{:S(2)}) %collective-permute-start.10) | collective-permute-done | bytes 114720 | tf_op jit(solution)/shard_map/ppermute | solution.py:278
  35.1 0.2 convolution_multiply_fusion.refs_0_
  35.4 1.2 %collective-permute-start.13 = (f32[32,896]{1,0:T(8,128)S(1)}, f32[32,896]{1,0:T(8,128)S(1)}, u32[]{:S(2)}, u32[]{:S(2)}) collective-permute-start(f32[32,896]{1,0:T(8,128)S(1)} %convolution_multiply_fusion.refs_0_), channel_id=1, source_target_pairs={{0,24},{4,28},{8,16},{12,20},{16,8},{20,12},{24,0},{28,4},{1,25},{... | collective-permute-start | bytes 344072 | tf_op jit(solution)/shard_map/ppermute | solution.py:278
  36.6 0.0 collective-permute-start.12
  36.6 1.5 %collective-permute-start.11 = (f32[32,896]{1,0:T(8,128)S(1)}, f32[32,896]{1,0:T(8,128)S(1)}, u32[]{:S(2)}, u32[]{:S(2)}) collective-permute-start(f32[32,896]{1,0:T(8,128)S(1)} %convolution_multiply_fusion.refs_0_), channel_id=1, source_target_pairs={{0,8},{4,12},{8,0},{12,4},{16,24},{20,28},{24,16},{28,20},{1,9},{5... | collective-permute-start | bytes 344072 | tf_op jit(solution)/shard_map/ppermute | solution.py:278
  38.1 2.0 %collective-permute-done.13.refs_3_ = f32[32,896]{1,0:T(8,128)S(1)} collective-permute-done((f32[32,896]{1,0:T(8,128)S(1)}, f32[32,896]{1,0:T(8,128)S(1)}, u32[]{:S(2)}, u32[]{:S(2)}) %collective-permute-start.13) | collective-permute-done | bytes 114720 | tf_op jit(solution)/shard_map/ppermute | solution.py:278
  40.1 3.1 %collective-permute-done.12.refs_2_ = f32[32,896]{1,0:T(8,128)S(1)} collective-permute-done((f32[32,896]{1,0:T(8,128)S(1)}, f32[32,896]{1,0:T(8,128)S(1)}, u32[]{:S(2)}, u32[]{:S(2)}) %collective-permute-start.12) | collective-permute-done | bytes 114720 | tf_op jit(solution)/shard_map/ppermute | solution.py:278
  43.1 0.0 collective-permute-done.11.refs_1_
  43.2 1.3 %collective-permute-start.14 = (f32[4,32,896]{2,1,0:T(8,128)S(1)}, f32[4,32,896]{2,1,0:T(8,128)S(1)}, u32[]{:S(2)}, u32[]{:S(2)}) collective-permute-start(f32[4,32,896]{2,1,0:T(8,128)S(1)} %pad_maximum_fusion), channel_id=1, source_target_pairs={{0,4},{4,0},{8,12},{12,8},{16,20},{20,16},{24,28},{28,24},{1,5},{5... | collective-permute-start | bytes 1376264 | tf_op jit(solution)/shard_map/ppermute | solution.py:278
  44.5 2.3 %feedback.2 = (f32[256,7168]{1,0:T(8,128)}, f32[32,7168]{1,0:T(8,128)}, f32[32,256]{1,0:T(8,128)}) custom-call(bf16[256,128]{1,0:T(8,128)(2,1)S(1)} %get-tuple-element.20.stacked, f32[32,896]{1,0:T(8,128)S(1)} %convolution_multiply_fusion.refs_0_, f32[32,896]{1,0:T(8,128)S(1)} %collective-permute-done.11.refs_1_, ...), custom_call_target="tpu_custom_call" | custom-call | flops 234881024 | bytes 3670016 | tf_op jit(solution)/shard_map/feedback/pallas_call | solution.py:255
  46.8 0.0 collective-permute-done.14.refs_0_
  46.8 2.3 %feedback.3 = (f32[256,7168]{1,0:T(8,128)}, f32[32,7168]{1,0:T(8,128)}) custom-call(bf16[256,128]{1,0:T(8,128)(2,1)S(1)} %get-tuple-element.20.stacked, f32[4,32,896]{2,1,0:T(8,128)S(1)} %collective-permute-done.14.refs_0_, f32[256,7168]{1,0:T(8,128)S(1)} %get-tuple-element.28.refs_4_.refs_1_, ...), custom_call_target="tpu_custom_call", output_to_operand_aliasing={{0}: (3, {}), {1}: (4, {})} | custom-call | flops 234881024 | bytes 3670016 | tf_op jit(solution)/shard_map/feedback/pallas_call | solution.py:255
  (4 shorter events, 0.1 us)
Async XLA Ops:
  6.6 4.4 %collective-permute-start.2 = (f32[32,256]{1,0:T(8,128)S(1)}, f32[32,256]{1,0:T(8,128)S(1)}, u32[]{:S(2)}, u32[]{:S(2)}) collective-permute-start(f32[32,256]{1,0:T(8,128)S(1)} %get-tuple-element.19), channel_id=1, source_target_pairs={{0,24},{4,28},{8,16},{12,20},{16,8},{20,12},{24,0},{28,4},{1,25},{... | collective-permute-start | bytes 98312 | tf_op jit(solution)/shard_map/ppermute | solution.py:278
  9.6 2.8 %collective-permute-start.1 = (f32[32,256]{1,0:T(8,128)S(1)}, f32[32,256]{1,0:T(8,128)S(1)}, u32[]{:S(2)}, u32[]{:S(2)}) collective-permute-start(f32[32,256]{1,0:T(8,128)S(1)} %get-tuple-element.19), channel_id=1, source_target_pairs={{0,16},{4,20},{8,24},{12,28},{16,0},{20,4},{24,8},{28,12},{1,17},{... | collective-permute-start | bytes 98312 | tf_op jit(solution)/shard_map/ppermute | solution.py:278
  9.9 2.8 %collective-permute-start = (f32[32,256]{1,0:T(8,128)S(1)}, f32[32,256]{1,0:T(8,128)S(1)}, u32[]{:S(2)}, u32[]{:S(2)}) collective-permute-start(f32[32,256]{1,0:T(8,128)S(1)} %get-tuple-element.19), channel_id=1, source_target_pairs={{0,8},{4,12},{8,0},{12,4},{16,24},{20,28},{24,16},{28,20},{1,9},{5... | collective-permute-start | bytes 98312 | tf_op jit(solution)/shard_map/ppermute | solution.py:278
  12.7 4.7 %collective-permute-start.5 = (f32[32,256]{1,0:T(8,128)S(1)}, f32[32,256]{1,0:T(8,128)S(1)}, u32[]{:S(2)}, u32[]{:S(2)}) collective-permute-start(f32[32,256]{1,0:T(8,128)S(1)} %add_add_fusion.1), channel_id=1, source_target_pairs={{0,3},{1,2},{2,1},{3,0},{4,7},{5,6},{6,5},{7,4},{8,11},{9,10},{10,... | collective-permute-start | bytes 98312 | tf_op jit(solution)/shard_map/ppermute | solution.py:278
  16.1 4.0 %collective-permute-start.4 = (f32[32,256]{1,0:T(8,128)S(1)}, f32[32,256]{1,0:T(8,128)S(1)}, u32[]{:S(2)}, u32[]{:S(2)}) collective-permute-start(f32[32,256]{1,0:T(8,128)S(1)} %add_add_fusion.1), channel_id=1, source_target_pairs={{0,2},{1,3},{2,0},{3,1},{4,6},{5,7},{6,4},{7,5},{8,10},{9,11},{10,... | collective-permute-start | bytes 98312 | tf_op jit(solution)/shard_map/ppermute | solution.py:278
  16.1 4.0 %collective-permute-start.3 = (f32[32,256]{1,0:T(8,128)S(1)}, f32[32,256]{1,0:T(8,128)S(1)}, u32[]{:S(2)}, u32[]{:S(2)}) collective-permute-start(f32[32,256]{1,0:T(8,128)S(1)} %add_add_fusion.1), channel_id=1, source_target_pairs={{0,1},{1,0},{2,3},{3,2},{4,5},{5,4},{6,7},{7,6},{8,9},{9,8},{10,11... | collective-permute-start | bytes 98312 | tf_op jit(solution)/shard_map/ppermute | solution.py:278
  20.1 4.4 %collective-permute-start.6 = (f32[32,256]{1,0:T(8,128)S(1)}, f32[32,256]{1,0:T(8,128)S(1)}, u32[]{:S(2)}, u32[]{:S(2)}) collective-permute-start(f32[32,256]{1,0:T(8,128)S(1)} %add_add_fusion.left), channel_id=1, source_target_pairs={{0,4},{4,0},{8,12},{12,8},{16,20},{20,16},{24,28},{28,24},{1,5},{5... | collective-permute-start | bytes 98312 | tf_op jit(solution)/shard_map/ppermute | solution.py:278
  25.2 1.9 %collective-permute-start.7 = (f32[4,32,896]{2,1,0:T(8,128)S(1)}, f32[4,32,896]{2,1,0:T(8,128)S(1)}, u32[]{:S(2)}, u32[]{:S(2)}) collective-permute-start(f32[4,32,896]{2,1,0:T(8,128)S(1)} %right.7), channel_id=1, source_target_pairs={{0,4},{4,0},{8,12},{12,8},{16,20},{20,16},{24,28},{28,24},{1,5},{5... | collective-permute-start | bytes 1376264 | tf_op jit(solution)/shard_map/ppermute | solution.py:278
  27.2 5.8 %collective-permute-start.8 = (f32[32,896]{1,0:T(8,128)S(1)}, f32[32,896]{1,0:T(8,128)S(1)}, u32[]{:S(2)}, u32[]{:S(2)}) collective-permute-start(f32[32,896]{1,0:T(8,128)S(1)} %get-tuple-element.25), channel_id=1, source_target_pairs={{0,8},{4,12},{8,0},{12,4},{16,24},{20,28},{24,16},{28,20},{1,9},{5... | collective-permute-start | bytes 344072 | tf_op jit(solution)/shard_map/ppermute | solution.py:278
  27.5 5.5 %collective-permute-start.9 = (f32[32,896]{1,0:T(8,128)S(1)}, f32[32,896]{1,0:T(8,128)S(1)}, u32[]{:S(2)}, u32[]{:S(2)}) collective-permute-start(f32[32,896]{1,0:T(8,128)S(1)} %get-tuple-element.26), channel_id=1, source_target_pairs={{0,16},{4,20},{8,24},{12,28},{16,0},{20,4},{24,8},{28,12},{1,17},{... | collective-permute-start | bytes 344072 | tf_op jit(solution)/shard_map/ppermute | solution.py:278
  28.7 6.4 %collective-permute-start.10 = (f32[32,896]{1,0:T(8,128)S(1)}, f32[32,896]{1,0:T(8,128)S(1)}, u32[]{:S(2)}, u32[]{:S(2)}) collective-permute-start(f32[32,896]{1,0:T(8,128)S(1)} %get-tuple-element.27), channel_id=1, source_target_pairs={{0,24},{4,28},{8,16},{12,20},{16,8},{20,12},{24,0},{28,4},{1,25},{... | collective-permute-start | bytes 344072 | tf_op jit(solution)/shard_map/ppermute | solution.py:278
  35.4 4.7 %collective-permute-start.13 = (f32[32,896]{1,0:T(8,128)S(1)}, f32[32,896]{1,0:T(8,128)S(1)}, u32[]{:S(2)}, u32[]{:S(2)}) collective-permute-start(f32[32,896]{1,0:T(8,128)S(1)} %convolution_multiply_fusion.refs_0_), channel_id=1, source_target_pairs={{0,24},{4,28},{8,16},{12,20},{16,8},{20,12},{24,0},{28,4},{1,25},{... | collective-permute-start | bytes 344072 | tf_op jit(solution)/shard_map/ppermute | solution.py:278
  36.6 6.6 %collective-permute-start.12 = (f32[32,896]{1,0:T(8,128)S(1)}, f32[32,896]{1,0:T(8,128)S(1)}, u32[]{:S(2)}, u32[]{:S(2)}) collective-permute-start(f32[32,896]{1,0:T(8,128)S(1)} %convolution_multiply_fusion.refs_0_), channel_id=1, source_target_pairs={{0,16},{4,20},{8,24},{12,28},{16,0},{20,4},{24,8},{28,12},{1,17},{... | collective-permute-start | bytes 344072 | tf_op jit(solution)/shard_map/ppermute | solution.py:278
  36.6 6.6 %collective-permute-start.11 = (f32[32,896]{1,0:T(8,128)S(1)}, f32[32,896]{1,0:T(8,128)S(1)}, u32[]{:S(2)}, u32[]{:S(2)}) collective-permute-start(f32[32,896]{1,0:T(8,128)S(1)} %convolution_multiply_fusion.refs_0_), channel_id=1, source_target_pairs={{0,8},{4,12},{8,0},{12,4},{16,24},{20,28},{24,16},{28,20},{1,9},{5... | collective-permute-start | bytes 344072 | tf_op jit(solution)/shard_map/ppermute | solution.py:278
  43.2 3.6 %collective-permute-start.14 = (f32[4,32,896]{2,1,0:T(8,128)S(1)}, f32[4,32,896]{2,1,0:T(8,128)S(1)}, u32[]{:S(2)}, u32[]{:S(2)}) collective-permute-start(f32[4,32,896]{2,1,0:T(8,128)S(1)} %pad_maximum_fusion), channel_id=1, source_target_pairs={{0,4},{4,0},{8,12},{12,8},{16,20},{20,16},{24,28},{28,24},{1,5},{5... | collective-permute-start | bytes 1376264 | tf_op jit(solution)/shard_map/ppermute | solution.py:278

commit v6 on v5

--- a/solution.py
+++ b/solution.py
@@ -98,8 +98,7 @@
     )(gradient, feedback, right)
 
 
-def right_kernel(own, left, high, low, *refs):
-    *before, pieces = refs
+def right_kernel(own, left, high, low, pieces):
     chips, rank, width = pieces.shape
     half = chips * width
     core, _ = position()
@@ -114,23 +113,21 @@
         while start < (i + 1) * block:
             piece = start // width
             stop = min((i + 1) * block, (piece + 1) * width)
-            there = (piece, slice(None), slice(start - piece * width, stop - piece * width))
-            part = total[:, start - i * block : stop - i * block]
-            pieces[there] = before[0][there] + part if before else part
+            pieces[piece, :, start - piece * width : stop - piece * width] = total[:, start - i * block : stop - i * block]
             start = stop
 
 
-def right_product(own, left, high, low, chips, width, *before):
+def right_product(own, left, high, low, chips, width):
     rank, rows = left.shape
     return pl.pallas_call(
         functools.partial(right_kernel, own),
-        in_specs=[VMEM] * (3 + len(before)),
+        in_specs=[VMEM] * 3,
         out_specs=VMEM,
         out_shape=pltpu.VMEM((chips, rank, width), F32),
         compiler_params=params(8),
         cost_estimate=cost(8 * rows * chips * width * rank, 4 * rows * chips * width),
         name="right",
-    )(left, high, low, *before)
+    )(left, high, low)
 
 
 def share_kernel(a, b, *outs):
@@ -284,12 +281,48 @@
     return terms[0]
 
 
-def sum_over(x, axis, low, high):
+def lead(dim, mask):
+    pairs = []
+    for i in range(1, lax.axis_size("dp"), 2):
+        for j in range(lax.axis_size("tensor")):
+            there = (i ^ mask, j) if dim == 0 else (i, j ^ mask)
+            pairs.append((index_of(i, j), index_of(*there)))
+    return pairs
+
+
+def index_of(i, j):
+    return i * lax.axis_size("tensor") + j
+
+
+def sum_over(x, dim, low, high):
     while low < high:
         step = min(2, high - low)
-        x = tree([x] + [swap(x, axis, k << low) for k in range(1, 1 << step)])
+        came = [lax.ppermute(x, ("dp", "tensor"), lead(dim, k << low)) for k in range(1, 1 << step)]
+        x = tree([x] + came)
         low += step
     return x
+
+
+def hand_over(x):
+    pairs = [(i, i - 1) for i in range(1, lax.axis_size("dp"), 2)]
+    return lax.ppermute(x, "dp", pairs)
+
+
+def settle_kernel(mine, came, out):
+    core, _ = position()
+    out[...] = jnp.where(core == 1, mine[...], came[...])
+
+
+def settle(mine, came):
+    return pl.pallas_call(
+        settle_kernel,
+        in_specs=[VMEM] * 2,
+        out_specs=VMEM,
+        out_shape=pltpu.VMEM(mine.shape, F32),
+        compiler_params=params(8),
+        cost_estimate=cost(mine.size, 12 * mine.size),
+        name="settle",
+    )(mine, came)
 
 
 def bits(axis):
@@ -309,19 +342,19 @@
     given = [keep(x, pltpu.HBM) for x in (gradient, feedback, right_factor.T)]
     combined, high, low, left = left_product(*given, replicas * width)
     combined, high, low = (keep(x, pltpu.VMEM) for x in (combined, high, low))
-    left = sum_over(left, "dp", 1, bits("dp"))
-    left = sum_over(left, "tensor", 0, bits("tensor"))
-
-    beside = swap(left, "dp", 1)
-    theirs, half = (right_product(side, left, high, low, chips, width) for side in (False, True))
-    theirs = swap(right_product(False, beside, high, low, chips, width, theirs), "dp", 1)
-    half = right_product(True, beside, high, low, chips, width, half)
-    left = (left + beside) / replicas
+    left = left + swap(left, "dp", 1)
+    left = sum_over(left, 0, 1, bits("dp"))
+    left = sum_over(left, 1, 0, bits("tensor"))
+    left = settle(left, hand_over(left)) / replicas
+
+    theirs = swap(right_product(False, left, high, low, chips, width), "dp", 1)
+    half = right_product(True, left, high, low, chips, width)
     own, *away = share(half, theirs)
-    own = tree([own] + [swap(x, "dp", 2 * k) for k, x in enumerate(away, 1)])
+    came = [swap(x, "dp", 2 * k) for k, x in enumerate(away, 1)]
+    own = tree(came[::-1] + [own])
 
     inverse, factor, stacked = factors(left)
-    own = jnp.dot(inverse, own, precision=HIGHEST, preferred_element_type=F32) / replicas**2
+    own = jnp.dot(inverse, own, precision=HIGHEST, preferred_element_type=F32) / replicas
 
     got = [own] + [swap(own, "dp", 2 * k) for k in range(1, chips)]
     other = swap(jnp.stack(got), "dp", 1)

time: 49.3 us -> 59.3 us (1.20)
  starting transfers between devices: 17.8 us -> 26.5 us
  waiting for transfers between devices: 13.6 us -> 16.3 us
  Pallas kernels: 16.7 us -> 15.3 us
    ppermute x0 -> x7, starting transfers between devices: none -> 20 us  [the longest x6 18.7 us: sum_over(): lax.ppermute(x, ('dp', 'tensor'), lead(dim, k << low))]
    ppermute x15 -> x9, starting transfers between devices: 17.8 us -> 6.48 us  [swap(): return lax.ppermute(x, axis, [(i, i ^ mask) for i in range(size)])]
    ppermute x0 -> x7, waiting for transfers between devices: none -> 5.96 us  [the longest x6 5.12 us: sum_over(): lax.ppermute(x, ('dp', 'tensor'), lead(dim, k << low))]
    ppermute x15 -> x9, waiting for transfers between devices: 13.6 us -> 10.3 us  [swap(): return lax.ppermute(x, axis, [(i, i ^ mask) for i in range(size)])]
    pallas_call x4 -> x3, Pallas kernels: 2.96 us -> 1.49 us  [the longest x2 1.48 us: right_product(): pl.pallas_call(functools.partial(right_kernel, own), in_specs=[VMEM] * 3,...]
  transfers between devices with their start and end apart: 15 -> 16, of which waited for: 9 -> 10; matrix products, arithmetic and copies ran while one was open for 0% -> 0% of each run, Pallas kernels for 16% -> 10%
where the time goes in v6:
time: 59.3 us; the launch traced here: 59 us
  starting transfers between devices  26.5 us (45%)
  waiting for transfers between devices  16.3 us (27%)
  Pallas kernels  15.3 us (26%)
  between operations  0.78 us (1%)
    ppermute x6, starting transfers between devices, sum_over(): lax.ppermute(x, ('dp', 'tensor'), lead(dim, k << low))  18.7 us
    ppermute x9, waiting for transfers between devices, swap(): return lax.ppermute(x, axis, [(i, i ^ mask) for i in range(size)])  10.3 us
    ppermute x9, starting transfers between devices, swap(): return lax.ppermute(x, axis, [(i, i ^ mask) for i in range(size)])  6.48 us
    pallas_call x1, Pallas kernels, left_product(): pl.pallas_call(functools.partial(left_kernel, chunk), in_specs=[ANY] * 3,...  5.94 us
    ppermute x6, waiting for transfers between devices, sum_over(): lax.ppermute(x, ('dp', 'tensor'), lead(dim, k << low))  5.12 us
    pallas_call x2, Pallas kernels, new_feedback(): pl.pallas_call(kernel, in_specs=[VMEM] * (2 + len(given)) + ([VMEM] if ow...  4.67 us
    pallas_call x1, Pallas kernels, factors(): pl.pallas_call(factor_kernel, in_specs=[VMEM], out_specs=[VMEM] * 3, out_...  3.12 us
    pallas_call x2, Pallas kernels, right_product(): pl.pallas_call(functools.partial(right_kernel, own), in_specs=[VMEM] * 3,...  1.48 us
  transfers between devices with their start and end apart: 16, of which 10 were waited for; matrix products, arithmetic and copies ran while one was open for 0% of the time, Pallas kernels for 10%

profile of v6, /device:TPU:1, one launch (start us, length us, event | category | flops | bytes accessed | tf_op | source)
XLA Modules:
  0.0 59.0 jit_solution(9665670312335682305)
XLA Ops:
  0.6 5.9 %left.1 = (f32[256,7168]{1,0:T(8,128)S(1)}, bf16[256,7168]{1,0:T(8,128)(2,1)S(1)}, bf16[256,7168]{1,0:T(8,128)(2,1)S(1)}, f32[32,256]{1,0:T(8,128)S(1)}) custom-call(bf16[256,7168]{1,0:T(8,128)(2,1)} %bitcast.17, f32[256,7168]{1,0:T(8,128)} %bitcast.15, f32[32,7168]{1,0:T(8,128)} %bitcast.18), custom_call_target="tpu_custom_call" | custom-call | flops 469762048 | bytes 11010048 | tf_op jit(solution)/shard_map/left/pallas_call | solution.py:80
  6.6 0.1 collective-permute-start
  6.7 1.2 %collective-permute-done = f32[32,256]{1,0:T(8,128)S(1)} collective-permute-done((f32[32,256]{1,0:T(8,128)S(1)}, f32[32,256]{1,0:T(8,128)S(1)}, u32[]{:S(2)}, u32[]{:S(2)}) %collective-permute-start) | collective-permute-done | bytes 32800 | tf_op jit(solution)/shard_map/ppermute | solution.py:275
  7.9 5.2 %collective-permute-start.3 = (f32[32,256]{1,0:T(8,128)S(1)}, f32[32,256]{1,0:T(8,128)S(1)}, u32[]{:S(2)}, u32[]{:S(2)}) collective-permute-start(f32[32,256]{1,0:T(8,128)S(1)} %add.30), channel_id=1, source_target_pairs={{4,28},{5,29},{6,30},{7,31},{12,20},{13,21},{14,22},{15,23},{20,12... | collective-permute-start | bytes 98312 | tf_op jit(solution)/shard_map/ppermute | solution.py:300
  13.1 2.1 %collective-permute-start.2 = (f32[32,256]{1,0:T(8,128)S(1)}, f32[32,256]{1,0:T(8,128)S(1)}, u32[]{:S(2)}, u32[]{:S(2)}) collective-permute-start(f32[32,256]{1,0:T(8,128)S(1)} %add.30), channel_id=1, source_target_pairs={{4,20},{5,21},{6,22},{7,23},{12,28},{13,29},{14,30},{15,31},{20,4}... | collective-permute-start | bytes 98312 | tf_op jit(solution)/shard_map/ppermute | solution.py:300
  15.2 2.0 %collective-permute-start.1 = (f32[32,256]{1,0:T(8,128)S(1)}, f32[32,256]{1,0:T(8,128)S(1)}, u32[]{:S(2)}, u32[]{:S(2)}) collective-permute-start(f32[32,256]{1,0:T(8,128)S(1)} %add.30), channel_id=1, source_target_pairs={{4,12},{5,13},{6,14},{7,15},{12,4},{13,5},{14,6},{15,7},{20,28},{2... | collective-permute-start | bytes 98312 | tf_op jit(solution)/shard_map/ppermute | solution.py:300
  17.2 0.0 collective-permute-done.3
  17.2 0.5 collective-permute-done.2
  17.7 2.1 %collective-permute-done.1 = f32[32,256]{1,0:T(8,128)S(1)} collective-permute-done((f32[32,256]{1,0:T(8,128)S(1)}, f32[32,256]{1,0:T(8,128)S(1)}, u32[]{:S(2)}, u32[]{:S(2)}) %collective-permute-start.1) | collective-permute-done | bytes 32800 | tf_op jit(solution)/shard_map/ppermute | solution.py:300
  19.9 5.2 %collective-permute-start.6 = (f32[32,256]{1,0:T(8,128)S(1)}, f32[32,256]{1,0:T(8,128)S(1)}, u32[]{:S(2)}, u32[]{:S(2)}) collective-permute-start(f32[32,256]{1,0:T(8,128)S(1)} %add_add_fusion.1), channel_id=1, source_target_pairs={{4,7},{5,6},{6,5},{7,4},{12,15},{13,14},{14,13},{15,12},{20,23},{2... | collective-permute-start | bytes 98312 | tf_op jit(solution)/shard_map/ppermute | solution.py:300
  25.1 1.9 %collective-permute-start.5 = (f32[32,256]{1,0:T(8,128)S(1)}, f32[32,256]{1,0:T(8,128)S(1)}, u32[]{:S(2)}, u32[]{:S(2)}) collective-permute-start(f32[32,256]{1,0:T(8,128)S(1)} %add_add_fusion.1), channel_id=1, source_target_pairs={{4,6},{5,7},{6,4},{7,5},{12,14},{13,15},{14,12},{15,13},{20,22},{2... | collective-permute-start | bytes 98312 | tf_op jit(solution)/shard_map/ppermute | solution.py:300
  27.1 2.2 %collective-permute-start.4 = (f32[32,256]{1,0:T(8,128)S(1)}, f32[32,256]{1,0:T(8,128)S(1)}, u32[]{:S(2)}, u32[]{:S(2)}) collective-permute-start(f32[32,256]{1,0:T(8,128)S(1)} %add_add_fusion.1), channel_id=1, source_target_pairs={{4,5},{5,4},{6,7},{7,6},{12,13},{13,12},{14,15},{15,14},{20,21},{2... | collective-permute-start | bytes 98312 | tf_op jit(solution)/shard_map/ppermute | solution.py:300
  29.3 0.0 collective-permute-done.6
  29.3 1.4 %collective-permute-done.5 = f32[32,256]{1,0:T(8,128)S(1)} collective-permute-done((f32[32,256]{1,0:T(8,128)S(1)}, f32[32,256]{1,0:T(8,128)S(1)}, u32[]{:S(2)}, u32[]{:S(2)}) %collective-permute-start.5) | collective-permute-done | bytes 32800 | tf_op jit(solution)/shard_map/ppermute | solution.py:300
  30.7 1.0 %collective-permute-done.4 = f32[32,256]{1,0:T(8,128)S(1)} collective-permute-done((f32[32,256]{1,0:T(8,128)S(1)}, f32[32,256]{1,0:T(8,128)S(1)}, u32[]{:S(2)}, u32[]{:S(2)}) %collective-permute-start.4) | collective-permute-done | bytes 32800 | tf_op jit(solution)/shard_map/ppermute | solution.py:300
  31.7 1.3 %collective-permute-start.7 = (f32[32,256]{1,0:T(8,128)S(1)}, f32[32,256]{1,0:T(8,128)S(1)}, u32[]{:S(2)}, u32[]{:S(2)}) collective-permute-start(f32[32,256]{1,0:T(8,128)S(1)} %add_add_fusion.mine), channel_id=1, source_target_pairs={{4,0},{12,8},{20,16},{28,24},{5,1},{13,9},{21,17},{29,25},{6,2},{1... | collective-permute-start | bytes 98312 | tf_op jit(solution)/shard_map/ppermute | solution.py:308
  33.0 0.8 %collective-permute-done.7.came = f32[32,256]{1,0:T(8,128)S(1)} collective-permute-done((f32[32,256]{1,0:T(8,128)S(1)}, f32[32,256]{1,0:T(8,128)S(1)}, u32[]{:S(2)}, u32[]{:S(2)}) %collective-permute-start.7) | collective-permute-done | bytes 32800 | tf_op jit(solution)/shard_map/ppermute | solution.py:308
  33.9 0.7 %right.3 = f32[4,32,896]{2,1,0:T(8,128)S(1)} custom-call(f32[32,256]{1,0:T(8,128)S(1)} %broadcast_multiply_fusion.left, bf16[256,7168]{1,0:T(8,128)(2,1)S(1)} %get-tuple-element.22.high, bf16[256,7168]{1,0:T(8,128)(2,1)S(1)} %get-tuple-element.23.low), custom_call_target="tpu_custom_call" | custom-call | flops 234881024 | bytes 3670016 | tf_op jit(solution)/shard_map/right/pallas_call | solution.py:122
  34.6 0.4 collective-permute-start.8
  35.0 0.7 %right.2.a = f32[4,32,896]{2,1,0:T(8,128)S(1)} custom-call(f32[32,256]{1,0:T(8,128)S(1)} %broadcast_multiply_fusion.left, bf16[256,7168]{1,0:T(8,128)(2,1)S(1)} %get-tuple-element.22.high, bf16[256,7168]{1,0:T(8,128)(2,1)S(1)} %get-tuple-element.23.low), custom_call_target="tpu_custom_call" | custom-call | flops 234881024 | bytes 3670016 | tf_op jit(solution)/shard_map/right/pallas_call | solution.py:122
  35.8 0.7 %collective-permute-done.8.b = f32[4,32,896]{2,1,0:T(8,128)S(1)} collective-permute-done((f32[4,32,896]{2,1,0:T(8,128)S(1)}, f32[4,32,896]{2,1,0:T(8,128)S(1)}, u32[]{:S(2)}, u32[]{:S(2)}) %collective-permute-start.8) | collective-permute-done | bytes 458784 | tf_op jit(solution)/shard_map/ppermute | solution.py:275
  36.5 1.3 %collective-permute-start.9 = (f32[32,896]{1,0:T(8,128)S(1)}, f32[32,896]{1,0:T(8,128)S(1)}, u32[]{:S(2)}, u32[]{:S(2)}) collective-permute-start(f32[32,896]{1,0:T(8,128)S(1)} %get-tuple-element.24), channel_id=1, source_target_pairs={{0,24},{4,28},{8,16},{12,20},{16,8},{20,12},{24,0},{28,4},{1,25},{... | collective-permute-start | bytes 344072 | tf_op jit(solution)/shard_map/ppermute | solution.py:275
  37.8 0.2 collective-permute-start.10
  38.0 1.2 %collective-permute-start.11 = (f32[32,896]{1,0:T(8,128)S(1)}, f32[32,896]{1,0:T(8,128)S(1)}, u32[]{:S(2)}, u32[]{:S(2)}) collective-permute-start(f32[32,896]{1,0:T(8,128)S(1)} %get-tuple-element.26), channel_id=1, source_target_pairs={{0,8},{4,12},{8,0},{12,4},{16,24},{20,28},{24,16},{28,20},{1,9},{5... | collective-permute-start | bytes 344072 | tf_op jit(solution)/shard_map/ppermute | solution.py:275
  39.2 3.1 %factor.1 = (f32[32,32]{1,0:T(8,128)S(1)}, f32[32,256]{1,0:T(8,128)S(1)}, bf16[256,128]{1,0:T(8,128)(2,1)S(1)}) custom-call(f32[32,256]{1,0:T(8,128)S(1)} %broadcast_multiply_fusion.left), custom_call_target="tpu_custom_call" | custom-call | flops 2000000000 | bytes 1000000 | tf_op jit(solution)/shard_map/factor/pallas_call | solution.py:176
  42.4 0.0 collective-permute-done.9
  42.4 2.6 %collective-permute-done.10 = f32[32,896]{1,0:T(8,128)S(1)} collective-permute-done((f32[32,896]{1,0:T(8,128)S(1)}, f32[32,896]{1,0:T(8,128)S(1)}, u32[]{:S(2)}, u32[]{:S(2)}) %collective-permute-start.10) | collective-permute-done | bytes 114720 | tf_op jit(solution)/shard_map/ppermute | solution.py:275
  45.0 0.0 collective-permute-done.11
  45.0 0.2 convolution_multiply_fusion.refs_0_
  45.3 1.3 %collective-permute-start.14 = (f32[32,896]{1,0:T(8,128)S(1)}, f32[32,896]{1,0:T(8,128)S(1)}, u32[]{:S(2)}, u32[]{:S(2)}) collective-permute-start(f32[32,896]{1,0:T(8,128)S(1)} %convolution_multiply_fusion.refs_0_), channel_id=1, source_target_pairs={{0,24},{4,28},{8,16},{12,20},{16,8},{20,12},{24,0},{28,4},{1,25},{... | collective-permute-start | bytes 344072 | tf_op jit(solution)/shard_map/ppermute | solution.py:275
  46.5 0.2 collective-permute-start.13
  46.8 1.2 %collective-permute-start.12 = (f32[32,896]{1,0:T(8,128)S(1)}, f32[32,896]{1,0:T(8,128)S(1)}, u32[]{:S(2)}, u32[]{:S(2)}) collective-permute-start(f32[32,896]{1,0:T(8,128)S(1)} %convolution_multiply_fusion.refs_0_), channel_id=1, source_target_pairs={{0,8},{4,12},{8,0},{12,4},{16,24},{20,28},{24,16},{28,20},{1,9},{5... | collective-permute-start | bytes 344072 | tf_op jit(solution)/shard_map/ppermute | solution.py:275
  48.0 2.3 %collective-permute-done.14.refs_3_ = f32[32,896]{1,0:T(8,128)S(1)} collective-permute-done((f32[32,896]{1,0:T(8,128)S(1)}, f32[32,896]{1,0:T(8,128)S(1)}, u32[]{:S(2)}, u32[]{:S(2)}) %collective-permute-start.14) | collective-permute-done | bytes 114720 | tf_op jit(solution)/shard_map/ppermute | solution.py:275
  50.3 3.4 %collective-permute-done.13.refs_2_ = f32[32,896]{1,0:T(8,128)S(1)} collective-permute-done((f32[32,896]{1,0:T(8,128)S(1)}, f32[32,896]{1,0:T(8,128)S(1)}, u32[]{:S(2)}, u32[]{:S(2)}) %collective-permute-start.13) | collective-permute-done | bytes 114720 | tf_op jit(solution)/shard_map/ppermute | solution.py:275
  53.8 0.0 collective-permute-done.12.refs_1_
  53.8 0.6 collective-permute-start.15
  54.4 2.3 %feedback.2 = (f32[256,7168]{1,0:T(8,128)}, f32[32,7168]{1,0:T(8,128)}, f32[32,256]{1,0:T(8,128)}) custom-call(bf16[256,128]{1,0:T(8,128)(2,1)S(1)} %get-tuple-element.20.stacked, f32[32,896]{1,0:T(8,128)S(1)} %convolution_multiply_fusion.refs_0_, f32[32,896]{1,0:T(8,128)S(1)} %collective-permute-done.12.refs_1_, ...), custom_call_target="tpu_custom_call" | custom-call | flops 234881024 | bytes 3670016 | tf_op jit(solution)/shard_map/feedback/pallas_call | solution.py:252
  56.7 0.0 collective-permute-done.15.refs_0_
  56.7 2.3 %feedback.3 = (f32[256,7168]{1,0:T(8,128)}, f32[32,7168]{1,0:T(8,128)}) custom-call(bf16[256,128]{1,0:T(8,128)(2,1)S(1)} %get-tuple-element.20.stacked, f32[4,32,896]{2,1,0:T(8,128)S(1)} %collective-permute-done.15.refs_0_, f32[256,7168]{1,0:T(8,128)S(1)} %get-tuple-element.28.refs_4_.refs_1_, ...), custom_call_target="tpu_custom_call", output_to_operand_aliasing={{0}: (3, {}), {1}: (4, {})} | custom-call | flops 234881024 | bytes 3670016 | tf_op jit(solution)/shard_map/feedback/pallas_call | solution.py:252
  (7 shorter events, 0.1 us)
Async XLA Ops:
  6.6 1.3 %collective-permute-start = (f32[32,256]{1,0:T(8,128)S(1)}, f32[32,256]{1,0:T(8,128)S(1)}, u32[]{:S(2)}, u32[]{:S(2)}) collective-permute-start(f32[32,256]{1,0:T(8,128)S(1)} %get-tuple-element.19), channel_id=1, source_target_pairs={{0,4},{4,0},{8,12},{12,8},{16,20},{20,16},{24,28},{28,24},{1,5},{5... | collective-permute-start | bytes 98312 | tf_op jit(solution)/shard_map/ppermute | solution.py:275
  7.9 9.4 %collective-permute-start.3 = (f32[32,256]{1,0:T(8,128)S(1)}, f32[32,256]{1,0:T(8,128)S(1)}, u32[]{:S(2)}, u32[]{:S(2)}) collective-permute-start(f32[32,256]{1,0:T(8,128)S(1)} %add.30), channel_id=1, source_target_pairs={{4,28},{5,29},{6,30},{7,31},{12,20},{13,21},{14,22},{15,23},{20,12... | collective-permute-start | bytes 98312 | tf_op jit(solution)/shard_map/ppermute | solution.py:300
  13.1 4.7 %collective-permute-start.2 = (f32[32,256]{1,0:T(8,128)S(1)}, f32[32,256]{1,0:T(8,128)S(1)}, u32[]{:S(2)}, u32[]{:S(2)}) collective-permute-start(f32[32,256]{1,0:T(8,128)S(1)} %add.30), channel_id=1, source_target_pairs={{4,20},{5,21},{6,22},{7,23},{12,28},{13,29},{14,30},{15,31},{20,4}... | collective-permute-start | bytes 98312 | tf_op jit(solution)/shard_map/ppermute | solution.py:300
  15.2 4.7 %collective-permute-start.1 = (f32[32,256]{1,0:T(8,128)S(1)}, f32[32,256]{1,0:T(8,128)S(1)}, u32[]{:S(2)}, u32[]{:S(2)}) collective-permute-start(f32[32,256]{1,0:T(8,128)S(1)} %add.30), channel_id=1, source_target_pairs={{4,12},{5,13},{6,14},{7,15},{12,4},{13,5},{14,6},{15,7},{20,28},{2... | collective-permute-start | bytes 98312 | tf_op jit(solution)/shard_map/ppermute | solution.py:300
  19.9 9.4 %collective-permute-start.6 = (f32[32,256]{1,0:T(8,128)S(1)}, f32[32,256]{1,0:T(8,128)S(1)}, u32[]{:S(2)}, u32[]{:S(2)}) collective-permute-start(f32[32,256]{1,0:T(8,128)S(1)} %add_add_fusion.1), channel_id=1, source_target_pairs={{4,7},{5,6},{6,5},{7,4},{12,15},{13,14},{14,13},{15,12},{20,23},{2... | collective-permute-start | bytes 98312 | tf_op jit(solution)/shard_map/ppermute | solution.py:300
  25.1 5.6 %collective-permute-start.5 = (f32[32,256]{1,0:T(8,128)S(1)}, f32[32,256]{1,0:T(8,128)S(1)}, u32[]{:S(2)}, u32[]{:S(2)}) collective-permute-start(f32[32,256]{1,0:T(8,128)S(1)} %add_add_fusion.1), channel_id=1, source_target_pairs={{4,6},{5,7},{6,4},{7,5},{12,14},{13,15},{14,12},{15,13},{20,22},{2... | collective-permute-start | bytes 98312 | tf_op jit(solution)/shard_map/ppermute | solution.py:300
  27.1 4.7 %collective-permute-start.4 = (f32[32,256]{1,0:T(8,128)S(1)}, f32[32,256]{1,0:T(8,128)S(1)}, u32[]{:S(2)}, u32[]{:S(2)}) collective-permute-start(f32[32,256]{1,0:T(8,128)S(1)} %add_add_fusion.1), channel_id=1, source_target_pairs={{4,5},{5,4},{6,7},{7,6},{12,13},{13,12},{14,15},{15,14},{20,21},{2... | collective-permute-start | bytes 98312 | tf_op jit(solution)/shard_map/ppermute | solution.py:300
  31.7 2.1 %collective-permute-start.7 = (f32[32,256]{1,0:T(8,128)S(1)}, f32[32,256]{1,0:T(8,128)S(1)}, u32[]{:S(2)}, u32[]{:S(2)}) collective-permute-start(f32[32,256]{1,0:T(8,128)S(1)} %add_add_fusion.mine), channel_id=1, source_target_pairs={{4,0},{12,8},{20,16},{28,24},{5,1},{13,9},{21,17},{29,25},{6,2},{1... | collective-permute-start | bytes 98312 | tf_op jit(solution)/shard_map/ppermute | solution.py:308
  34.6 1.8 %collective-permute-start.8 = (f32[4,32,896]{2,1,0:T(8,128)S(1)}, f32[4,32,896]{2,1,0:T(8,128)S(1)}, u32[]{:S(2)}, u32[]{:S(2)}) collective-permute-start(f32[4,32,896]{2,1,0:T(8,128)S(1)} %right.3), channel_id=1, source_target_pairs={{0,4},{4,0},{8,12},{12,8},{16,20},{20,16},{24,28},{28,24},{1,5},{5... | collective-permute-start | bytes 1376264 | tf_op jit(solution)/shard_map/ppermute | solution.py:275
  36.5 5.8 %collective-permute-start.9 = (f32[32,896]{1,0:T(8,128)S(1)}, f32[32,896]{1,0:T(8,128)S(1)}, u32[]{:S(2)}, u32[]{:S(2)}) collective-permute-start(f32[32,896]{1,0:T(8,128)S(1)} %get-tuple-element.24), channel_id=1, source_target_pairs={{0,24},{4,28},{8,16},{12,20},{16,8},{20,12},{24,0},{28,4},{1,25},{... | collective-permute-start | bytes 344072 | tf_op jit(solution)/shard_map/ppermute | solution.py:275
  37.8 7.2 %collective-permute-start.10 = (f32[32,896]{1,0:T(8,128)S(1)}, f32[32,896]{1,0:T(8,128)S(1)}, u32[]{:S(2)}, u32[]{:S(2)}) collective-permute-start(f32[32,896]{1,0:T(8,128)S(1)} %get-tuple-element.25), channel_id=1, source_target_pairs={{0,16},{4,20},{8,24},{12,28},{16,0},{20,4},{24,8},{28,12},{1,17},{... | collective-permute-start | bytes 344072 | tf_op jit(solution)/shard_map/ppermute | solution.py:275
  38.0 7.0 %collective-permute-start.11 = (f32[32,896]{1,0:T(8,128)S(1)}, f32[32,896]{1,0:T(8,128)S(1)}, u32[]{:S(2)}, u32[]{:S(2)}) collective-permute-start(f32[32,896]{1,0:T(8,128)S(1)} %get-tuple-element.26), channel_id=1, source_target_pairs={{0,8},{4,12},{8,0},{12,4},{16,24},{20,28},{24,16},{28,20},{1,9},{5... | collective-permute-start | bytes 344072 | tf_op jit(solution)/shard_map/ppermute | solution.py:275
  45.3 5.1 %collective-permute-start.14 = (f32[32,896]{1,0:T(8,128)S(1)}, f32[32,896]{1,0:T(8,128)S(1)}, u32[]{:S(2)}, u32[]{:S(2)}) collective-permute-start(f32[32,896]{1,0:T(8,128)S(1)} %convolution_multiply_fusion.refs_0_), channel_id=1, source_target_pairs={{0,24},{4,28},{8,16},{12,20},{16,8},{20,12},{24,0},{28,4},{1,25},{... | collective-permute-start | bytes 344072 | tf_op jit(solution)/shard_map/ppermute | solution.py:275
  46.5 7.2 %collective-permute-start.13 = (f32[32,896]{1,0:T(8,128)S(1)}, f32[32,896]{1,0:T(8,128)S(1)}, u32[]{:S(2)}, u32[]{:S(2)}) collective-permute-start(f32[32,896]{1,0:T(8,128)S(1)} %convolution_multiply_fusion.refs_0_), channel_id=1, source_target_pairs={{0,16},{4,20},{8,24},{12,28},{16,0},{20,4},{24,8},{28,12},{1,17},{... | collective-permute-start | bytes 344072 | tf_op jit(solution)/shard_map/ppermute | solution.py:275
  46.8 7.0 %collective-permute-start.12 = (f32[32,896]{1,0:T(8,128)S(1)}, f32[32,896]{1,0:T(8,128)S(1)}, u32[]{:S(2)}, u32[]{:S(2)}) collective-permute-start(f32[32,896]{1,0:T(8,128)S(1)} %convolution_multiply_fusion.refs_0_), channel_id=1, source_target_pairs={{0,8},{4,12},{8,0},{12,4},{16,24},{20,28},{24,16},{28,20},{1,9},{5... | collective-permute-start | bytes 344072 | tf_op jit(solution)/shard_map/ppermute | solution.py:275
  53.8 2.9 %collective-permute-start.15 = (f32[4,32,896]{2,1,0:T(8,128)S(1)}, f32[4,32,896]{2,1,0:T(8,128)S(1)}, u32[]{:S(2)}, u32[]{:S(2)}) collective-permute-start(f32[4,32,896]{2,1,0:T(8,128)S(1)} %pad_maximum_fusion), channel_id=1, source_target_pairs={{0,4},{4,0},{8,12},{12,8},{16,20},{20,16},{24,28},{28,24},{1,5},{5... | collective-permute-start | bytes 1376264 | tf_op jit(solution)/shard_map/ppermute | solution.py:275

commit v7 on v5

--- a/solution.py
+++ b/solution.py
@@ -284,12 +284,43 @@
     return terms[0]
 
 
-def sum_over(x, axis, low, high):
-    while low < high:
-        step = min(2, high - low)
-        x = tree([x] + [swap(x, axis, k << low) for k in range(1, 1 << step)])
-        low += step
-    return x
+def steps(low, high):
+    return [(i, min(2, high - i)) for i in range(low, high, 2)]
+
+
+def sum_stage(x, axis, low, count):
+    if count == 1:
+        return x + swap(x, axis, 1 << low)
+    first = lax.ppermute(x, ("dp", "tensor"), pairs_of(axis, 1 << low, 3 << low))
+    second = lax.ppermute(x, ("dp", "tensor"), pairs_of(axis, 1 << low, 2 << low))
+    return part(x, first, second)
+
+
+def pairs_of(axis, *masks):
+    pairs = []
+    for i in range(lax.axis_size("dp")):
+        for j in range(lax.axis_size("tensor")):
+            mask = masks[i % 2]
+            there = (i ^ mask, j) if axis == "dp" else (i, j ^ mask)
+            pairs.append(tuple(a * lax.axis_size("tensor") + b for a, b in ((i, j), there)))
+    return pairs
+
+
+def part_kernel(mine, first, second, out):
+    core, _ = position()
+    out[...] = first[...] + jnp.where(core == 1, second[...], mine[...])
+
+
+def part(mine, first, second):
+    return pl.pallas_call(
+        part_kernel,
+        in_specs=[VMEM] * 3,
+        out_specs=VMEM,
+        out_shape=pltpu.VMEM(mine.shape, F32),
+        compiler_params=params(8),
+        cost_estimate=cost(mine.size, 16 * mine.size),
+        name="part",
+    )(mine, first, second)
 
 
 def bits(axis):
@@ -309,9 +340,16 @@
     given = [keep(x, pltpu.HBM) for x in (gradient, feedback, right_factor.T)]
     combined, high, low, left = left_product(*given, replicas * width)
     combined, high, low = (keep(x, pltpu.VMEM) for x in (combined, high, low))
-    left = sum_over(left, "dp", 1, bits("dp"))
-    left = sum_over(left, "tensor", 0, bits("tensor"))
-
+    left = left + swap(left, "dp", 1)
+    stages = [("dp", low, count) for low, count in steps(1, bits("dp"))]
+    stages += [("tensor", low, count) for low, count in steps(0, bits("tensor"))]
+    stages.sort(key=lambda stage: stage[2])
+    for i, stage in enumerate(stages):
+        left = sum_stage(left, *stage)
+        if stage[2] == 2 and i < len(stages) - 1:
+            left = left + swap(left, "dp", 1)
+    if stages[-1][2] == 1:
+        left = left * 0.5
     beside = swap(left, "dp", 1)
     theirs, half = (right_product(side, left, high, low, chips, width) for side in (False, True))
     theirs = swap(right_product(False, beside, high, low, chips, width, theirs), "dp", 1)

time: 49.3 us -> 48.8 us (0.990)
  starting transfers between devices: 17.8 us -> 14.9 us
  waiting for transfers between devices: 13.6 us -> 15.9 us
    ppermute x15 -> x11, starting transfers between devices: 17.8 us -> 7.98 us  [swap(): return lax.ppermute(x, axis, [(i, i ^ mask) for i in range(size)])]
    ppermute x0 -> x4, starting transfers between devices: none -> 6.94 us  [the longest x2 4.7 us: sum_stage(): lax.ppermute(x, ('dp', 'tensor'), pairs_of(axis, 1 << low, 2 << low))]
    ppermute x0 -> x4, waiting for transfers between devices: none -> 6.03 us  [the longest x2 5.51 us: sum_stage(): lax.ppermute(x, ('dp', 'tensor'), pairs_of(axis, 1 << low, 3 << low))]
    ppermute x15 -> x11, waiting for transfers between devices: 13.6 us -> 9.83 us  [swap(): return lax.ppermute(x, axis, [(i, i ^ mask) for i in range(size)])]
  transfers between devices with their start and end apart: 15 -> 15, of which waited for: 9 -> 11; matrix products, arithmetic and copies ran while one was open for 0% -> 0% of each run, Pallas kernels for 16% -> 16%
where the time goes in v7:
time: 48.8 us; the launch traced here: 48.6 us
  Pallas kernels  16.8 us (34%)
  waiting for transfers between devices  15.9 us (33%)
  starting transfers between devices  14.9 us (31%)
  between operations  0.73 us (1%)
    ppermute x11, waiting for transfers between devices, swap(): return lax.ppermute(x, axis, [(i, i ^ mask) for i in range(size)])  9.83 us
    ppermute x11, starting transfers between devices, swap(): return lax.ppermute(x, axis, [(i, i ^ mask) for i in range(size)])  7.98 us
    pallas_call x1, Pallas kernels, left_product(): pl.pallas_call(functools.partial(left_kernel, chunk), in_specs=[ANY] * 3,...  5.94 us
    ppermute x2, waiting for transfers between devices, sum_stage(): lax.ppermute(x, ('dp', 'tensor'), pairs_of(axis, 1 << low, 3 << low))  5.51 us
    ppermute x2, starting transfers between devices, sum_stage(): lax.ppermute(x, ('dp', 'tensor'), pairs_of(axis, 1 << low, 2 << low))  4.7 us
    pallas_call x2, Pallas kernels, new_feedback(): pl.pallas_call(kernel, in_specs=[VMEM] * (2 + len(given)) + ([VMEM] if ow...  4.67 us
    pallas_call x1, Pallas kernels, factors(): pl.pallas_call(factor_kernel, in_specs=[VMEM], out_specs=[VMEM] * 3, out_...  3.12 us
    pallas_call x4, Pallas kernels, right_product(): pl.pallas_call(functools.partial(right_kernel, own), in_specs=[VMEM] * (3...  2.98 us
  transfers between devices with their start and end apart: 15, of which 11 were waited for; matrix products, arithmetic and copies ran while one was open for 0% of the time, Pallas kernels for 16%

profile of v7, /device:TPU:1, one launch (start us, length us, event | category | flops | bytes accessed | tf_op | source)
XLA Modules:
  0.0 48.6 jit_solution(18404245475752398497)
XLA Ops:
  0.6 5.9 %left.1 = (f32[256,7168]{1,0:T(8,128)S(1)}, bf16[256,7168]{1,0:T(8,128)(2,1)S(1)}, bf16[256,7168]{1,0:T(8,128)(2,1)S(1)}, f32[32,256]{1,0:T(8,128)S(1)}) custom-call(bf16[256,7168]{1,0:T(8,128)(2,1)} %bitcast.17, f32[256,7168]{1,0:T(8,128)} %bitcast.15, f32[32,7168]{1,0:T(8,128)} %bitcast.18), custom_call_target="tpu_custom_call" | custom-call | flops 469762048 | bytes 11010048 | tf_op jit(solution)/shard_map/left/pallas_call | solution.py:80
  6.6 0.1 collective-permute-start
  6.7 1.2 %collective-permute-done = f32[32,256]{1,0:T(8,128)S(1)} collective-permute-done((f32[32,256]{1,0:T(8,128)S(1)}, f32[32,256]{1,0:T(8,128)S(1)}, u32[]{:S(2)}, u32[]{:S(2)}) %collective-permute-start) | collective-permute-done | bytes 32800 | tf_op jit(solution)/shard_map/ppermute | solution.py:278
  7.9 2.4 %collective-permute-start.2 = (f32[32,256]{1,0:T(8,128)S(1)}, f32[32,256]{1,0:T(8,128)S(1)}, u32[]{:S(2)}, u32[]{:S(2)}) collective-permute-start(f32[32,256]{1,0:T(8,128)S(1)} %add.18.mine), channel_id=1, source_target_pairs={{0,8},{1,9},{2,10},{3,11},{4,20},{5,21},{6,22},{7,23},{8,0},{9,1},... | collective-permute-start | bytes 98312 | tf_op jit(solution)/shard_map/ppermute | solution.py:295
  10.2 1.2 %collective-permute-start.1 = (f32[32,256]{1,0:T(8,128)S(1)}, f32[32,256]{1,0:T(8,128)S(1)}, u32[]{:S(2)}, u32[]{:S(2)}) collective-permute-start(f32[32,256]{1,0:T(8,128)S(1)} %add.18.mine), channel_id=1, source_target_pairs={{0,8},{1,9},{2,10},{3,11},{4,28},{5,29},{6,30},{7,31},{8,0},{9,1},... | collective-permute-start | bytes 98312 | tf_op jit(solution)/shard_map/ppermute | solution.py:294
  11.4 0.1 collective-permute-done.2.second
  11.6 2.4 %collective-permute-done.1.first = f32[32,256]{1,0:T(8,128)S(1)} collective-permute-done((f32[32,256]{1,0:T(8,128)S(1)}, f32[32,256]{1,0:T(8,128)S(1)}, u32[]{:S(2)}, u32[]{:S(2)}) %collective-permute-start.1) | collective-permute-done | bytes 32800 | tf_op jit(solution)/shard_map/ppermute | solution.py:294
  13.9 0.9 %collective-permute-start.3 = (f32[32,256]{1,0:T(8,128)S(1)}, f32[32,256]{1,0:T(8,128)S(1)}, u32[]{:S(2)}, u32[]{:S(2)}) collective-permute-start(f32[32,256]{1,0:T(8,128)S(1)} %part.2), channel_id=1, source_target_pairs={{0,4},{4,0},{8,12},{12,8},{16,20},{20,16},{24,28},{28,24},{1,5},{5... | collective-permute-start | bytes 98312 | tf_op jit(solution)/shard_map/ppermute | solution.py:278
  14.8 0.9 %collective-permute-done.3 = f32[32,256]{1,0:T(8,128)S(1)} collective-permute-done((f32[32,256]{1,0:T(8,128)S(1)}, f32[32,256]{1,0:T(8,128)S(1)}, u32[]{:S(2)}, u32[]{:S(2)}) %collective-permute-start.3) | collective-permute-done | bytes 32800 | tf_op jit(solution)/shard_map/ppermute | solution.py:278
  15.7 2.3 %collective-permute-start.5 = (f32[32,256]{1,0:T(8,128)S(1)}, f32[32,256]{1,0:T(8,128)S(1)}, u32[]{:S(2)}, u32[]{:S(2)}) collective-permute-start(f32[32,256]{1,0:T(8,128)S(1)} %add.19.mine), channel_id=1, source_target_pairs={{0,1},{1,0},{2,3},{3,2},{4,6},{5,7},{6,4},{7,5},{8,9},{9,8},{10,11... | collective-permute-start | bytes 98312 | tf_op jit(solution)/shard_map/ppermute | solution.py:295
  18.0 1.1 %collective-permute-start.4 = (f32[32,256]{1,0:T(8,128)S(1)}, f32[32,256]{1,0:T(8,128)S(1)}, u32[]{:S(2)}, u32[]{:S(2)}) collective-permute-start(f32[32,256]{1,0:T(8,128)S(1)} %add.19.mine), channel_id=1, source_target_pairs={{0,1},{1,0},{2,3},{3,2},{4,7},{5,6},{6,5},{7,4},{8,9},{9,8},{10,11... | collective-permute-start | bytes 98312 | tf_op jit(solution)/shard_map/ppermute | solution.py:294
  19.1 0.4 collective-permute-done.5.second
  19.5 3.1 %collective-permute-done.4.first = f32[32,256]{1,0:T(8,128)S(1)} collective-permute-done((f32[32,256]{1,0:T(8,128)S(1)}, f32[32,256]{1,0:T(8,128)S(1)}, u32[]{:S(2)}, u32[]{:S(2)}) %collective-permute-start.4) | collective-permute-done | bytes 32800 | tf_op jit(solution)/shard_map/ppermute | solution.py:294
  22.6 0.1 collective-permute-start.6
  22.7 0.7 %right.6.refs_0_ = f32[4,32,896]{2,1,0:T(8,128)S(1)} custom-call(f32[32,256]{1,0:T(8,128)S(1)} %part.3.left, bf16[256,7168]{1,0:T(8,128)(2,1)S(1)} %get-tuple-element.22.high, bf16[256,7168]{1,0:T(8,128)(2,1)S(1)} %get-tuple-element.23.low), custom_call_target="tpu_custom_call" | custom-call | flops 234881024 | bytes 3670016 | tf_op jit(solution)/shard_map/right/pallas_call | solution.py:125
  23.5 0.4 collective-permute-done.6.left
  23.9 0.7 %right.7 = f32[4,32,896]{2,1,0:T(8,128)S(1)} custom-call(f32[32,256]{1,0:T(8,128)S(1)} %collective-permute-done.6.left, bf16[256,7168]{1,0:T(8,128)(2,1)S(1)} %get-tuple-element.22.high, bf16[256,7168]{1,0:T(8,128)(2,1)S(1)} %get-tuple-element.23.low, f32[4,32,896]{2,1,0:T(8,128)S(1)} %right.6.refs_0_), custom_call_target="tpu_custom_call" | custom-call | flops 234881024 | bytes 3670016 | tf_op jit(solution)/shard_map/right/pallas_call | solution.py:125
  24.7 0.2 collective-permute-start.7
  24.8 0.7 %right.4.refs_0_ = f32[4,32,896]{2,1,0:T(8,128)S(1)} custom-call(f32[32,256]{1,0:T(8,128)S(1)} %part.3.left, bf16[256,7168]{1,0:T(8,128)(2,1)S(1)} %get-tuple-element.22.high, bf16[256,7168]{1,0:T(8,128)(2,1)S(1)} %get-tuple-element.23.low), custom_call_target="tpu_custom_call" | custom-call | flops 234881024 | bytes 3670016 | tf_op jit(solution)/shard_map/right/pallas_call | solution.py:125
  25.6 0.8 %right.5.a = f32[4,32,896]{2,1,0:T(8,128)S(1)} custom-call(f32[32,256]{1,0:T(8,128)S(1)} %collective-permute-done.6.left, bf16[256,7168]{1,0:T(8,128)(2,1)S(1)} %get-tuple-element.22.high, bf16[256,7168]{1,0:T(8,128)(2,1)S(1)} %get-tuple-element.23.low, f32[4,32,896]{2,1,0:T(8,128)S(1)} %right.4.refs_0_), custom_call_target="tpu_custom_call" | custom-call | flops 234881024 | bytes 3670016 | tf_op jit(solution)/shard_map/right/pallas_call | solution.py:125
  26.4 0.1 collective-permute-done.7.b
  26.5 1.1 %collective-permute-start.8 = (f32[32,896]{1,0:T(8,128)S(1)}, f32[32,896]{1,0:T(8,128)S(1)}, u32[]{:S(2)}, u32[]{:S(2)}) collective-permute-start(f32[32,896]{1,0:T(8,128)S(1)} %get-tuple-element.25), channel_id=1, source_target_pairs={{0,8},{4,12},{8,0},{12,4},{16,24},{20,28},{24,16},{28,20},{1,9},{5... | collective-permute-start | bytes 344072 | tf_op jit(solution)/shard_map/ppermute | solution.py:278
  27.7 0.6 %collective-permute-start.9 = (f32[32,896]{1,0:T(8,128)S(1)}, f32[32,896]{1,0:T(8,128)S(1)}, u32[]{:S(2)}, u32[]{:S(2)}) collective-permute-start(f32[32,896]{1,0:T(8,128)S(1)} %get-tuple-element.26), channel_id=1, source_target_pairs={{0,16},{4,20},{8,24},{12,28},{16,0},{20,4},{24,8},{28,12},{1,17},{... | collective-permute-start | bytes 344072 | tf_op jit(solution)/shard_map/ppermute | solution.py:278
  28.3 1.0 %collective-permute-start.10 = (f32[32,896]{1,0:T(8,128)S(1)}, f32[32,896]{1,0:T(8,128)S(1)}, u32[]{:S(2)}, u32[]{:S(2)}) collective-permute-start(f32[32,896]{1,0:T(8,128)S(1)} %get-tuple-element.27), channel_id=1, source_target_pairs={{0,24},{4,28},{8,16},{12,20},{16,8},{20,12},{24,0},{28,4},{1,25},{... | collective-permute-start | bytes 344072 | tf_op jit(solution)/shard_map/ppermute | solution.py:278
  29.3 3.1 %factor.1 = (f32[32,32]{1,0:T(8,128)S(1)}, f32[32,256]{1,0:T(8,128)S(1)}, bf16[256,128]{1,0:T(8,128)(2,1)S(1)}) custom-call(f32[32,256]{1,0:T(8,128)S(1)} %add_multiply_fusion.left), custom_call_target="tpu_custom_call" | custom-call | flops 2000000000 | bytes 1000000 | tf_op jit(solution)/shard_map/factor/pallas_call | solution.py:179
  32.4 0.0 collective-permute-done.8
  32.4 0.0 collective-permute-done.9
  32.4 2.2 %collective-permute-done.10 = f32[32,896]{1,0:T(8,128)S(1)} collective-permute-done((f32[32,896]{1,0:T(8,128)S(1)}, f32[32,896]{1,0:T(8,128)S(1)}, u32[]{:S(2)}, u32[]{:S(2)}) %collective-permute-start.10) | collective-permute-done | bytes 114720 | tf_op jit(solution)/shard_map/ppermute | solution.py:278
  34.6 0.2 convolution_multiply_fusion.refs_0_
  34.8 1.1 %collective-permute-start.13 = (f32[32,896]{1,0:T(8,128)S(1)}, f32[32,896]{1,0:T(8,128)S(1)}, u32[]{:S(2)}, u32[]{:S(2)}) collective-permute-start(f32[32,896]{1,0:T(8,128)S(1)} %convolution_multiply_fusion.refs_0_), channel_id=1, source_target_pairs={{0,24},{4,28},{8,16},{12,20},{16,8},{20,12},{24,0},{28,4},{1,25},{... | collective-permute-start | bytes 344072 | tf_op jit(solution)/shard_map/ppermute | solution.py:278
  35.9 0.2 collective-permute-start.12
  36.1 1.4 %collective-permute-start.11 = (f32[32,896]{1,0:T(8,128)S(1)}, f32[32,896]{1,0:T(8,128)S(1)}, u32[]{:S(2)}, u32[]{:S(2)}) collective-permute-start(f32[32,896]{1,0:T(8,128)S(1)} %convolution_multiply_fusion.refs_0_), channel_id=1, source_target_pairs={{0,8},{4,12},{8,0},{12,4},{16,24},{20,28},{24,16},{28,20},{1,9},{5... | collective-permute-start | bytes 344072 | tf_op jit(solution)/shard_map/ppermute | solution.py:278
  37.5 2.0 %collective-permute-done.13.refs_3_ = f32[32,896]{1,0:T(8,128)S(1)} collective-permute-done((f32[32,896]{1,0:T(8,128)S(1)}, f32[32,896]{1,0:T(8,128)S(1)}, u32[]{:S(2)}, u32[]{:S(2)}) %collective-permute-start.13) | collective-permute-done | bytes 114720 | tf_op jit(solution)/shard_map/ppermute | solution.py:278
  39.5 3.1 %collective-permute-done.12.refs_2_ = f32[32,896]{1,0:T(8,128)S(1)} collective-permute-done((f32[32,896]{1,0:T(8,128)S(1)}, f32[32,896]{1,0:T(8,128)S(1)}, u32[]{:S(2)}, u32[]{:S(2)}) %collective-permute-start.12) | collective-permute-done | bytes 114720 | tf_op jit(solution)/shard_map/ppermute | solution.py:278
  42.6 0.0 collective-permute-done.11.refs_1_
  42.6 1.3 %collective-permute-start.14 = (f32[4,32,896]{2,1,0:T(8,128)S(1)}, f32[4,32,896]{2,1,0:T(8,128)S(1)}, u32[]{:S(2)}, u32[]{:S(2)}) collective-permute-start(f32[4,32,896]{2,1,0:T(8,128)S(1)} %pad_maximum_fusion), channel_id=1, source_target_pairs={{0,4},{4,0},{8,12},{12,8},{16,20},{20,16},{24,28},{28,24},{1,5},{5... | collective-permute-start | bytes 1376264 | tf_op jit(solution)/shard_map/ppermute | solution.py:278
  43.9 2.3 %feedback.2 = (f32[256,7168]{1,0:T(8,128)}, f32[32,7168]{1,0:T(8,128)}, f32[32,256]{1,0:T(8,128)}) custom-call(bf16[256,128]{1,0:T(8,128)(2,1)S(1)} %get-tuple-element.20.stacked, f32[32,896]{1,0:T(8,128)S(1)} %convolution_multiply_fusion.refs_0_, f32[32,896]{1,0:T(8,128)S(1)} %collective-permute-done.11.refs_1_, ...), custom_call_target="tpu_custom_call" | custom-call | flops 234881024 | bytes 3670016 | tf_op jit(solution)/shard_map/feedback/pallas_call | solution.py:255
  46.2 0.0 collective-permute-done.14.refs_0_
  46.3 2.3 %feedback.3 = (f32[256,7168]{1,0:T(8,128)}, f32[32,7168]{1,0:T(8,128)}) custom-call(bf16[256,128]{1,0:T(8,128)(2,1)S(1)} %get-tuple-element.20.stacked, f32[4,32,896]{2,1,0:T(8,128)S(1)} %collective-permute-done.14.refs_0_, f32[256,7168]{1,0:T(8,128)S(1)} %get-tuple-element.28.refs_4_.refs_1_, ...), custom_call_target="tpu_custom_call", output_to_operand_aliasing={{0}: (3, {}), {1}: (4, {})} | custom-call | flops 234881024 | bytes 3670016 | tf_op jit(solution)/shard_map/feedback/pallas_call | solution.py:255
  (7 shorter events, 0.1 us)
Async XLA Ops:
  6.6 1.3 %collective-permute-start = (f32[32,256]{1,0:T(8,128)S(1)}, f32[32,256]{1,0:T(8,128)S(1)}, u32[]{:S(2)}, u32[]{:S(2)}) collective-permute-start(f32[32,256]{1,0:T(8,128)S(1)} %get-tuple-element.19), channel_id=1, source_target_pairs={{0,4},{4,0},{8,12},{12,8},{16,20},{20,16},{24,28},{28,24},{1,5},{5... | collective-permute-start | bytes 98312 | tf_op jit(solution)/shard_map/ppermute | solution.py:278
  7.9 3.7 %collective-permute-start.2 = (f32[32,256]{1,0:T(8,128)S(1)}, f32[32,256]{1,0:T(8,128)S(1)}, u32[]{:S(2)}, u32[]{:S(2)}) collective-permute-start(f32[32,256]{1,0:T(8,128)S(1)} %add.18.mine), channel_id=1, source_target_pairs={{0,8},{1,9},{2,10},{3,11},{4,20},{5,21},{6,22},{7,23},{8,0},{9,1},... | collective-permute-start | bytes 98312 | tf_op jit(solution)/shard_map/ppermute | solution.py:295
  10.2 3.7 %collective-permute-start.1 = (f32[32,256]{1,0:T(8,128)S(1)}, f32[32,256]{1,0:T(8,128)S(1)}, u32[]{:S(2)}, u32[]{:S(2)}) collective-permute-start(f32[32,256]{1,0:T(8,128)S(1)} %add.18.mine), channel_id=1, source_target_pairs={{0,8},{1,9},{2,10},{3,11},{4,28},{5,29},{6,30},{7,31},{8,0},{9,1},... | collective-permute-start | bytes 98312 | tf_op jit(solution)/shard_map/ppermute | solution.py:294
  13.9 1.8 %collective-permute-start.3 = (f32[32,256]{1,0:T(8,128)S(1)}, f32[32,256]{1,0:T(8,128)S(1)}, u32[]{:S(2)}, u32[]{:S(2)}) collective-permute-start(f32[32,256]{1,0:T(8,128)S(1)} %part.2), channel_id=1, source_target_pairs={{0,4},{4,0},{8,12},{12,8},{16,20},{20,16},{24,28},{28,24},{1,5},{5... | collective-permute-start | bytes 98312 | tf_op jit(solution)/shard_map/ppermute | solution.py:278
  15.7 3.8 %collective-permute-start.5 = (f32[32,256]{1,0:T(8,128)S(1)}, f32[32,256]{1,0:T(8,128)S(1)}, u32[]{:S(2)}, u32[]{:S(2)}) collective-permute-start(f32[32,256]{1,0:T(8,128)S(1)} %add.19.mine), channel_id=1, source_target_pairs={{0,1},{1,0},{2,3},{3,2},{4,6},{5,7},{6,4},{7,5},{8,9},{9,8},{10,11... | collective-permute-start | bytes 98312 | tf_op jit(solution)/shard_map/ppermute | solution.py:295
  18.0 4.6 %collective-permute-start.4 = (f32[32,256]{1,0:T(8,128)S(1)}, f32[32,256]{1,0:T(8,128)S(1)}, u32[]{:S(2)}, u32[]{:S(2)}) collective-permute-start(f32[32,256]{1,0:T(8,128)S(1)} %add.19.mine), channel_id=1, source_target_pairs={{0,1},{1,0},{2,3},{3,2},{4,7},{5,6},{6,5},{7,4},{8,9},{9,8},{10,11... | collective-permute-start | bytes 98312 | tf_op jit(solution)/shard_map/ppermute | solution.py:294
  22.6 1.3 %collective-permute-start.6 = (f32[32,256]{1,0:T(8,128)S(1)}, f32[32,256]{1,0:T(8,128)S(1)}, u32[]{:S(2)}, u32[]{:S(2)}) collective-permute-start(f32[32,256]{1,0:T(8,128)S(1)} %part.3.left), channel_id=1, source_target_pairs={{0,4},{4,0},{8,12},{12,8},{16,20},{20,16},{24,28},{28,24},{1,5},{5... | collective-permute-start | bytes 98312 | tf_op jit(solution)/shard_map/ppermute | solution.py:278
  24.7 1.8 %collective-permute-start.7 = (f32[4,32,896]{2,1,0:T(8,128)S(1)}, f32[4,32,896]{2,1,0:T(8,128)S(1)}, u32[]{:S(2)}, u32[]{:S(2)}) collective-permute-start(f32[4,32,896]{2,1,0:T(8,128)S(1)} %right.7), channel_id=1, source_target_pairs={{0,4},{4,0},{8,12},{12,8},{16,20},{20,16},{24,28},{28,24},{1,5},{5... | collective-permute-start | bytes 1376264 | tf_op jit(solution)/shard_map/ppermute | solution.py:278
  26.5 5.8 %collective-permute-start.8 = (f32[32,896]{1,0:T(8,128)S(1)}, f32[32,896]{1,0:T(8,128)S(1)}, u32[]{:S(2)}, u32[]{:S(2)}) collective-permute-start(f32[32,896]{1,0:T(8,128)S(1)} %get-tuple-element.25), channel_id=1, source_target_pairs={{0,8},{4,12},{8,0},{12,4},{16,24},{20,28},{24,16},{28,20},{1,9},{5... | collective-permute-start | bytes 344072 | tf_op jit(solution)/shard_map/ppermute | solution.py:278
  27.7 4.7 %collective-permute-start.9 = (f32[32,896]{1,0:T(8,128)S(1)}, f32[32,896]{1,0:T(8,128)S(1)}, u32[]{:S(2)}, u32[]{:S(2)}) collective-permute-start(f32[32,896]{1,0:T(8,128)S(1)} %get-tuple-element.26), channel_id=1, source_target_pairs={{0,16},{4,20},{8,24},{12,28},{16,0},{20,4},{24,8},{28,12},{1,17},{... | collective-permute-start | bytes 344072 | tf_op jit(solution)/shard_map/ppermute | solution.py:278
  28.3 6.3 %collective-permute-start.10 = (f32[32,896]{1,0:T(8,128)S(1)}, f32[32,896]{1,0:T(8,128)S(1)}, u32[]{:S(2)}, u32[]{:S(2)}) collective-permute-start(f32[32,896]{1,0:T(8,128)S(1)} %get-tuple-element.27), channel_id=1, source_target_pairs={{0,24},{4,28},{8,16},{12,20},{16,8},{20,12},{24,0},{28,4},{1,25},{... | collective-permute-start | bytes 344072 | tf_op jit(solution)/shard_map/ppermute | solution.py:278
  34.8 4.7 %collective-permute-start.13 = (f32[32,896]{1,0:T(8,128)S(1)}, f32[32,896]{1,0:T(8,128)S(1)}, u32[]{:S(2)}, u32[]{:S(2)}) collective-permute-start(f32[32,896]{1,0:T(8,128)S(1)} %convolution_multiply_fusion.refs_0_), channel_id=1, source_target_pairs={{0,24},{4,28},{8,16},{12,20},{16,8},{20,12},{24,0},{28,4},{1,25},{... | collective-permute-start | bytes 344072 | tf_op jit(solution)/shard_map/ppermute | solution.py:278
  35.9 6.7 %collective-permute-start.12 = (f32[32,896]{1,0:T(8,128)S(1)}, f32[32,896]{1,0:T(8,128)S(1)}, u32[]{:S(2)}, u32[]{:S(2)}) collective-permute-start(f32[32,896]{1,0:T(8,128)S(1)} %convolution_multiply_fusion.refs_0_), channel_id=1, source_target_pairs={{0,16},{4,20},{8,24},{12,28},{16,0},{20,4},{24,8},{28,12},{1,17},{... | collective-permute-start | bytes 344072 | tf_op jit(solution)/shard_map/ppermute | solution.py:278
  36.1 6.5 %collective-permute-start.11 = (f32[32,896]{1,0:T(8,128)S(1)}, f32[32,896]{1,0:T(8,128)S(1)}, u32[]{:S(2)}, u32[]{:S(2)}) collective-permute-start(f32[32,896]{1,0:T(8,128)S(1)} %convolution_multiply_fusion.refs_0_), channel_id=1, source_target_pairs={{0,8},{4,12},{8,0},{12,4},{16,24},{20,28},{24,16},{28,20},{1,9},{5... | collective-permute-start | bytes 344072 | tf_op jit(solution)/shard_map/ppermute | solution.py:278
  42.6 3.6 %collective-permute-start.14 = (f32[4,32,896]{2,1,0:T(8,128)S(1)}, f32[4,32,896]{2,1,0:T(8,128)S(1)}, u32[]{:S(2)}, u32[]{:S(2)}) collective-permute-start(f32[4,32,896]{2,1,0:T(8,128)S(1)} %pad_maximum_fusion), channel_id=1, source_target_pairs={{0,4},{4,0},{8,12},{12,8},{16,20},{20,16},{24,28},{28,24},{1,5},{5... | collective-permute-start | bytes 1376264 | tf_op jit(solution)/shard_map/ppermute | solution.py:278

commit v8 on v7

--- a/solution.py
+++ b/solution.py
@@ -133,26 +133,7 @@
     )(left, high, low, *before)
 
 
-def share_kernel(a, b, *outs):
-    _, chip = position()
-    for k, out in enumerate(outs):
-        out[...] = a[chip ^ k] + b[chip ^ k]
-
-
-def share(a, b):
-    chips, rank, width = a.shape
-    return pl.pallas_call(
-        share_kernel,
-        in_specs=[VMEM] * 2,
-        out_specs=[VMEM] * chips,
-        out_shape=[pltpu.VMEM((rank, width), F32)] * chips,
-        compiler_params=params(8),
-        cost_estimate=cost(chips * rank * width, 12 * chips * rank * width),
-        name="share",
-    )(a, b)
-
-
-def factor_kernel(left, inverse, factor, stacked):
+def factor_kernel(scale, left, inverse, factor, stacked):
     rank, rows = left.shape
     values = left[...]
     gram = dot(values, values, 1, 1, HIGHEST)
@@ -167,17 +148,17 @@
         wide = wide - jnp.where(row_of > j, wide[:, j : j + 1], 0.0) * scaled
     diagonal = jnp.sum(wide[:, :rank] * unit, axis=1, keepdims=True)
     inv = wide[:, rank:] * (1.0 / jnp.sqrt(diagonal))
-    inverse[...] = inv
+    inverse[...] = inv * scale
     q = dot(inv, values, 1, 0, HIGHEST)
     factor[...] = q
     q_high, q_low = (part.astype(F32) for part in split(q))
     stacked[...] = jnp.concatenate([q_high, q_low, q_high, q_low], axis=0).T.astype(BF16)
 
 
-def factors(left):
+def factors(left, scale):
     rank, rows = left.shape
     return pl.pallas_call(
-        factor_kernel,
+        functools.partial(factor_kernel, scale),
         in_specs=[VMEM],
         out_specs=[VMEM] * 3,
         out_shape=[
@@ -191,28 +172,28 @@
     )(left)
 
 
-def feedback_kernel(own, columns, stacked, pieces, combined, factor, feedback, right, factor_out, feedback_buf, sems, factor_sem):
-    rank = pieces[0].shape[-2]
+def feedback_kernel(own, columns, stacked, inverse, pieces, combined, factor, feedback, right, factor_out, feedback_buf, right_buf, sems, factor_sem):
     chips, rows, width = feedback_buf.shape
     whole = combined.shape[1] == columns
-    core, chip = position()
+    core, _ = position()
     side = core if own else 1 - core
     copies = []
     if own:
         factor_copy = pltpu.make_async_copy(factor, factor_out, factor_sem)
         factor_copy.start()
     for k in range(chips):
-        place = side * chips + (chip ^ k)
+        place = side * chips + k
         at = pl.ds(pl.multiple_of(place * width, 128), width)
-        piece = pieces[k]
-        piece_high, piece_low = split(piece[...])
+        piece = dot(inverse[...], pieces[k][...], 1, 0, HIGHEST)
+        right_buf[k] = piece
+        piece_high, piece_low = split(piece)
         four = jnp.concatenate([piece_high, piece_high, piece_low, piece_low], axis=0)
         feedback_buf[k] = combined[:, at] - dot(stacked[...], four, 1, 0)
         copies.append(
             (
                 place * width < columns,
                 pltpu.make_async_copy(feedback_buf.at[k], feedback.at[:, at], sems.at[0, k]),
-                pltpu.make_async_copy(piece, right.at[:, at], sems.at[1, k]),
+                pltpu.make_async_copy(right_buf.at[k], right.at[:, at], sems.at[1, k]),
             )
         )
         start_or_wait(copies[-1], whole, "start")
@@ -235,53 +216,47 @@
         pl.when(inside)(run)
 
 
-def new_feedback(own, stacked, pieces, combined, columns, last):
+def new_feedback(own, stacked, inverse, given, combined, columns, last):
     rows = combined.shape[0]
-    given = pieces if own else [pieces]
-    chips = len(pieces) if own else pieces.shape[0]
+    chips = sum(x.shape[0] for x in given)
     rank, width = given[0].shape[-2:]
     outs = 3 if own else 2
-
-    def kernel(stacked, *refs):
-        parts, rest = refs[: len(given)], refs[len(given) :]
+    first = 3 + len(given)
+
+    def kernel(stacked, inverse, *refs):
+        parts = [x.at[k] for x in refs[: len(given)] for k in range(x.shape[0])]
         if own:
-            combined, factor, feedback, right, factor_out, *scratch = rest
+            combined, factor, feedback, right, factor_out, *scratch = refs[len(given) :]
         else:
-            parts = [parts[0].at[k] for k in range(chips)]
-            combined, _, _, feedback, right, *scratch = rest
+            combined, _, _, feedback, right, *scratch = refs[len(given) :]
             factor = factor_out = None
-        feedback_kernel(own, columns, stacked, parts, combined, factor, feedback, right, factor_out, *scratch)
+        feedback_kernel(own, columns, stacked, inverse, parts, combined, factor, feedback, right, factor_out, *scratch)
 
     return pl.pallas_call(
         kernel,
-        in_specs=[VMEM] * (2 + len(given)) + ([VMEM] if own else [ANY] * 2),
+        in_specs=[VMEM] * first + ([VMEM] if own else [ANY] * 2),
         out_specs=[ANY] * outs,
         out_shape=[
             pltpu.HBM((rows, columns), F32),
             pltpu.HBM((rank, columns), F32),
             pltpu.HBM((rank, rows), F32),
         ][:outs],
-        input_output_aliases={} if own else {3: 0, 4: 1},
+        input_output_aliases={} if own else {first: 0, first + 1: 1},
         scratch_shapes=[
             pltpu.VMEM((chips, rows, width), F32),
+            pltpu.VMEM((chips, rank, width), F32),
             pltpu.SemaphoreType.DMA((2, chips)),
             pltpu.SemaphoreType.DMA,
         ],
         compiler_params=params(16),
         cost_estimate=cost(8 * rows * chips * width * rank, 4 * rows * chips * width),
         name="feedback",
-    )(stacked, *given, combined, *last)
+    )(stacked, inverse, *given, combined, *last)
 
 
 def swap(x, axis, mask):
     size = lax.axis_size(axis)
     return lax.ppermute(x, axis, [(i, i ^ mask) for i in range(size)])
-
-
-def tree(terms):
-    while len(terms) > 1:
-        terms = [a + b for a, b in zip(terms[::2], terms[1::2])]
-    return terms[0]
 
 
 def steps(low, high):
@@ -321,6 +296,10 @@
         cost_estimate=cost(mine.size, 16 * mine.size),
         name="part",
     )(mine, first, second)
+
+
+def after(x, token):
+    return lax.optimization_barrier((x, token))[0]
 
 
 def bits(axis):
@@ -355,16 +334,18 @@
     theirs = swap(right_product(False, beside, high, low, chips, width, theirs), "dp", 1)
     half = right_product(True, beside, high, low, chips, width, half)
     left = (left + beside) / replicas
-    own, *away = share(half, theirs)
-    own = tree([own] + [swap(x, "dp", 2 * k) for k, x in enumerate(away, 1)])
-
-    inverse, factor, stacked = factors(left)
-    own = jnp.dot(inverse, own, precision=HIGHEST, preferred_element_type=F32) / replicas**2
-
-    got = [own] + [swap(own, "dp", 2 * k) for k in range(1, chips)]
-    other = swap(jnp.stack(got), "dp", 1)
-    *outs, factor = new_feedback(True, stacked, got, combined, columns, [factor])
-    outs = new_feedback(False, stacked, other, combined, columns, outs)
+    masks = [1 << i for i in range(1, bits("dp"))]
+    parts = [half[: chips // 2] + theirs[: chips // 2], half[chips // 2 :] + theirs[chips // 2 :]]
+    inverse, factor, stacked = factors(left, 1.0 / replicas**2)
+    for i, pair in enumerate(zip(masks, masks[::-1])):
+        came = [swap(x, "dp", mask) for x, mask in zip(parts, pair)]
+        if i == 0:
+            came = [after(x, inverse) for x in came]
+        parts = [x + y for x, y in zip(parts, came)]
+
+    other = swap(jnp.concatenate(parts), "dp", 1)
+    *outs, factor = new_feedback(True, stacked, inverse, parts, combined, columns, [factor])
+    outs = new_feedback(False, stacked, inverse, [other], combined, columns, outs)
     return (outs[0][None], factor.T, outs[1].T)
 
 

time: 48.8 us -> 48.4 us (level)
  starting transfers between devices: 14.9 us -> 14.1 us
    ppermute x11 -> x9, starting transfers between devices: 7.98 us -> 7.14 us  [swap(): return lax.ppermute(x, axis, [(i, i ^ mask) for i in range(size)])]
    pallas_call x4 -> x3, Pallas kernels: 7.84 us -> 8.2 us  [the longest x2 5.08 us: new_feedback(): pl.pallas_call(kernel, in_specs=[VMEM] * first + ([VMEM] if own else [ANY...]
    ppermute x11 -> x9, waiting for transfers between devices: 9.83 us -> 10.1 us  [swap(): return lax.ppermute(x, axis, [(i, i ^ mask) for i in range(size)])]
  transfers between devices with their start and end apart: 15 -> 13, of which waited for: 11 -> 11; matrix products, arithmetic and copies ran while one was open for 0% -> 0% of each run, Pallas kernels for 16% -> 16%
where the time goes in v8:
time: 48.4 us; the launch traced here: 48.3 us
  Pallas kernels  17.1 us (35%)
  waiting for transfers between devices  16.1 us (33%)
  starting transfers between devices  14.1 us (29%)
  between operations  0.71 us (1%)
    ppermute x9, waiting for transfers between devices, swap(): return lax.ppermute(x, axis, [(i, i ^ mask) for i in range(size)])  10.1 us
    ppermute x9, starting transfers between devices, swap(): return lax.ppermute(x, axis, [(i, i ^ mask) for i in range(size)])  7.14 us
    pallas_call x1, Pallas kernels, left_product(): pl.pallas_call(functools.partial(left_kernel, chunk), in_specs=[ANY] * 3,...  5.94 us
    ppermute x2, waiting for transfers between devices, sum_stage(): lax.ppermute(x, ('dp', 'tensor'), pairs_of(axis, 1 << low, 3 << low))  5.51 us
    pallas_call x2, Pallas kernels, new_feedback(): pl.pallas_call(kernel, in_specs=[VMEM] * first + ([VMEM] if own else [ANY...  5.08 us
    ppermute x2, starting transfers between devices, sum_stage(): lax.ppermute(x, ('dp', 'tensor'), pairs_of(axis, 1 << low, 2 << low))  4.7 us
    pallas_call x1, Pallas kernels, factors(): pl.pallas_call(functools.partial(factor_kernel, scale), in_specs=[VMEM],...  3.12 us
    pallas_call x4, Pallas kernels, right_product(): pl.pallas_call(functools.partial(right_kernel, own), in_specs=[VMEM] * (3...  2.98 us
  transfers between devices with their start and end apart: 13, of which 11 were waited for; matrix products, arithmetic and copies ran while one was open for 0% of the time, Pallas kernels for 16%

profile of v8, /device:TPU:1, one launch (start us, length us, event | category | flops | bytes accessed | tf_op | source)
XLA Modules:
  0.0 48.3 jit_solution(9070668216126061861)
XLA Ops:
  0.6 5.9 %left.1 = (f32[256,7168]{1,0:T(8,128)S(1)}, bf16[256,7168]{1,0:T(8,128)(2,1)S(1)}, bf16[256,7168]{1,0:T(8,128)(2,1)S(1)}, f32[32,256]{1,0:T(8,128)S(1)}) custom-call(bf16[256,7168]{1,0:T(8,128)(2,1)} %bitcast.8, f32[256,7168]{1,0:T(8,128)} %bitcast.7, f32[32,7168]{1,0:T(8,128)} %bitcast.9), custom_call_target="tpu_custom_call" | custom-call | flops 469762048 | bytes 11010048 | tf_op jit(solution)/shard_map/left/pallas_call | solution.py:80
  6.6 0.1 collective-permute-start
  6.7 1.2 %collective-permute-done = f32[32,256]{1,0:T(8,128)S(1)} collective-permute-done((f32[32,256]{1,0:T(8,128)S(1)}, f32[32,256]{1,0:T(8,128)S(1)}, u32[]{:S(2)}, u32[]{:S(2)}) %collective-permute-start) | collective-permute-done | bytes 32800 | tf_op jit(solution)/shard_map/ppermute | solution.py:259
  7.9 2.4 %collective-permute-start.2 = (f32[32,256]{1,0:T(8,128)S(1)}, f32[32,256]{1,0:T(8,128)S(1)}, u32[]{:S(2)}, u32[]{:S(2)}) collective-permute-start(f32[32,256]{1,0:T(8,128)S(1)} %add.27.mine), channel_id=1, source_target_pairs={{0,8},{1,9},{2,10},{3,11},{4,20},{5,21},{6,22},{7,23},{8,0},{9,1},... | collective-permute-start | bytes 98312 | tf_op jit(solution)/shard_map/ppermute | solution.py:270
  10.2 1.2 %collective-permute-start.1 = (f32[32,256]{1,0:T(8,128)S(1)}, f32[32,256]{1,0:T(8,128)S(1)}, u32[]{:S(2)}, u32[]{:S(2)}) collective-permute-start(f32[32,256]{1,0:T(8,128)S(1)} %add.27.mine), channel_id=1, source_target_pairs={{0,8},{1,9},{2,10},{3,11},{4,28},{5,29},{6,30},{7,31},{8,0},{9,1},... | collective-permute-start | bytes 98312 | tf_op jit(solution)/shard_map/ppermute | solution.py:269
  11.4 0.1 collective-permute-done.2.second
  11.6 2.4 %collective-permute-done.1.first = f32[32,256]{1,0:T(8,128)S(1)} collective-permute-done((f32[32,256]{1,0:T(8,128)S(1)}, f32[32,256]{1,0:T(8,128)S(1)}, u32[]{:S(2)}, u32[]{:S(2)}) %collective-permute-start.1) | collective-permute-done | bytes 32800 | tf_op jit(solution)/shard_map/ppermute | solution.py:269
  13.9 0.9 %collective-permute-start.3 = (f32[32,256]{1,0:T(8,128)S(1)}, f32[32,256]{1,0:T(8,128)S(1)}, u32[]{:S(2)}, u32[]{:S(2)}) collective-permute-start(f32[32,256]{1,0:T(8,128)S(1)} %part.2), channel_id=1, source_target_pairs={{0,4},{4,0},{8,12},{12,8},{16,20},{20,16},{24,28},{28,24},{1,5},{5... | collective-permute-start | bytes 98312 | tf_op jit(solution)/shard_map/ppermute | solution.py:259
  14.8 0.9 %collective-permute-done.3 = f32[32,256]{1,0:T(8,128)S(1)} collective-permute-done((f32[32,256]{1,0:T(8,128)S(1)}, f32[32,256]{1,0:T(8,128)S(1)}, u32[]{:S(2)}, u32[]{:S(2)}) %collective-permute-start.3) | collective-permute-done | bytes 32800 | tf_op jit(solution)/shard_map/ppermute | solution.py:259
  15.7 2.3 %collective-permute-start.5 = (f32[32,256]{1,0:T(8,128)S(1)}, f32[32,256]{1,0:T(8,128)S(1)}, u32[]{:S(2)}, u32[]{:S(2)}) collective-permute-start(f32[32,256]{1,0:T(8,128)S(1)} %add.28.mine), channel_id=1, source_target_pairs={{0,1},{1,0},{2,3},{3,2},{4,6},{5,7},{6,4},{7,5},{8,9},{9,8},{10,11... | collective-permute-start | bytes 98312 | tf_op jit(solution)/shard_map/ppermute | solution.py:270
  18.0 1.1 %collective-permute-start.4 = (f32[32,256]{1,0:T(8,128)S(1)}, f32[32,256]{1,0:T(8,128)S(1)}, u32[]{:S(2)}, u32[]{:S(2)}) collective-permute-start(f32[32,256]{1,0:T(8,128)S(1)} %add.28.mine), channel_id=1, source_target_pairs={{0,1},{1,0},{2,3},{3,2},{4,7},{5,6},{6,5},{7,4},{8,9},{9,8},{10,11... | collective-permute-start | bytes 98312 | tf_op jit(solution)/shard_map/ppermute | solution.py:269
  19.1 0.4 collective-permute-done.5.second
  19.5 3.1 %collective-permute-done.4.first = f32[32,256]{1,0:T(8,128)S(1)} collective-permute-done((f32[32,256]{1,0:T(8,128)S(1)}, f32[32,256]{1,0:T(8,128)S(1)}, u32[]{:S(2)}, u32[]{:S(2)}) %collective-permute-start.4) | collective-permute-done | bytes 32800 | tf_op jit(solution)/shard_map/ppermute | solution.py:269
  22.6 0.1 collective-permute-start.6
  22.7 0.7 %right.6.refs_0_ = f32[4,32,896]{2,1,0:T(8,128)S(1)} custom-call(f32[32,256]{1,0:T(8,128)S(1)} %part.3.left, bf16[256,7168]{1,0:T(8,128)(2,1)S(1)} %get-tuple-element.20.high, bf16[256,7168]{1,0:T(8,128)(2,1)S(1)} %get-tuple-element.21.low), custom_call_target="tpu_custom_call" | custom-call | flops 234881024 | bytes 3670016 | tf_op jit(solution)/shard_map/right/pallas_call | solution.py:125
  23.5 0.4 collective-permute-done.6.left
  23.9 0.7 %right.7 = f32[4,32,896]{2,1,0:T(8,128)S(1)} custom-call(f32[32,256]{1,0:T(8,128)S(1)} %collective-permute-done.6.left, bf16[256,7168]{1,0:T(8,128)(2,1)S(1)} %get-tuple-element.20.high, bf16[256,7168]{1,0:T(8,128)(2,1)S(1)} %get-tuple-element.21.low, f32[4,32,896]{2,1,0:T(8,128)S(1)} %right.6.refs_0_), custom_call_target="tpu_custom_call" | custom-call | flops 234881024 | bytes 3670016 | tf_op jit(solution)/shard_map/right/pallas_call | solution.py:125
  24.7 0.2 collective-permute-start.7
  24.8 0.7 %right.4.refs_0_ = f32[4,32,896]{2,1,0:T(8,128)S(1)} custom-call(f32[32,256]{1,0:T(8,128)S(1)} %part.3.left, bf16[256,7168]{1,0:T(8,128)(2,1)S(1)} %get-tuple-element.20.high, bf16[256,7168]{1,0:T(8,128)(2,1)S(1)} %get-tuple-element.21.low), custom_call_target="tpu_custom_call" | custom-call | flops 234881024 | bytes 3670016 | tf_op jit(solution)/shard_map/right/pallas_call | solution.py:125
  25.6 0.8 %right.5 = f32[4,32,896]{2,1,0:T(8,128)S(1)} custom-call(f32[32,256]{1,0:T(8,128)S(1)} %collective-permute-done.6.left, bf16[256,7168]{1,0:T(8,128)(2,1)S(1)} %get-tuple-element.20.high, bf16[256,7168]{1,0:T(8,128)(2,1)S(1)} %get-tuple-element.21.low, f32[4,32,896]{2,1,0:T(8,128)S(1)} %right.4.refs_0_), custom_call_target="tpu_custom_call" | custom-call | flops 234881024 | bytes 3670016 | tf_op jit(solution)/shard_map/right/pallas_call | solution.py:125
  26.3 0.2 collective-permute-done.7
  26.5 1.1 %collective-permute-start.8 = (f32[2,32,896]{2,1,0:T(8,128)S(1)}, f32[2,32,896]{2,1,0:T(8,128)S(1)}, u32[]{:S(2)}, u32[]{:S(2)}) collective-permute-start(f32[2,32,896]{2,1,0:T(8,128)S(1)} %get-tuple-element.31), channel_id=1, source_target_pairs={{0,8},{4,12},{8,0},{12,4},{16,24},{20,28},{24,16},{28,20},{1,9},{5... | collective-permute-start | bytes 688136 | tf_op jit(solution)/shard_map/ppermute | solution.py:259
  27.7 0.6 %collective-permute-start.10 = (f32[2,32,896]{2,1,0:T(8,128)S(1)}, f32[2,32,896]{2,1,0:T(8,128)S(1)}, u32[]{:S(2)}, u32[]{:S(2)}) collective-permute-start(f32[2,32,896]{2,1,0:T(8,128)S(1)} %get-tuple-element.32), channel_id=1, source_target_pairs={{0,16},{4,20},{8,24},{12,28},{16,0},{20,4},{24,8},{28,12},{1,17},{... | collective-permute-start | bytes 688136 | tf_op jit(solution)/shard_map/ppermute | solution.py:259
  28.3 3.1 %factor.1 = (f32[32,32]{1,0:T(8,128)S(1)}, f32[32,256]{1,0:T(8,128)S(1)}, bf16[256,128]{1,0:T(8,128)(2,1)S(1)}) custom-call(f32[32,256]{1,0:T(8,128)S(1)} %add_multiply_fusion.left), custom_call_target="tpu_custom_call" | custom-call | flops 2000000000 | bytes 1000000 | tf_op jit(solution)/shard_map/factor/pallas_call | solution.py:160
  31.4 2.2 %collective-permute-done.8 = f32[2,32,896]{2,1,0:T(8,128)S(1)} collective-permute-done((f32[2,32,896]{2,1,0:T(8,128)S(1)}, f32[2,32,896]{2,1,0:T(8,128)S(1)}, u32[]{:S(2)}, u32[]{:S(2)}) %collective-permute-start.8) | collective-permute-done | bytes 229408 | tf_op jit(solution)/shard_map/ppermute | solution.py:259
  33.6 1.3 %collective-permute-start.9 = (f32[2,32,896]{2,1,0:T(8,128)S(1)}, f32[2,32,896]{2,1,0:T(8,128)S(1)}, u32[]{:S(2)}, u32[]{:S(2)}) collective-permute-start(f32[2,32,896]{2,1,0:T(8,128)S(1)} %add.31), channel_id=1, source_target_pairs={{0,16},{4,20},{8,24},{12,28},{16,0},{20,4},{24,8},{28,12},{1,17},{... | collective-permute-start | bytes 688136 | tf_op jit(solution)/shard_map/ppermute | solution.py:259
  34.9 0.0 collective-permute-done.10
  35.0 0.5 %collective-permute-start.11 = (f32[2,32,896]{2,1,0:T(8,128)S(1)}, f32[2,32,896]{2,1,0:T(8,128)S(1)}, u32[]{:S(2)}, u32[]{:S(2)}) collective-permute-start(f32[2,32,896]{2,1,0:T(8,128)S(1)} %add.34), channel_id=1, source_target_pairs={{0,8},{4,12},{8,0},{12,4},{16,24},{20,28},{24,16},{28,20},{1,9},{5... | collective-permute-start | bytes 688136 | tf_op jit(solution)/shard_map/ppermute | solution.py:259
  35.5 4.3 %collective-permute-done.9 = f32[2,32,896]{2,1,0:T(8,128)S(1)} collective-permute-done((f32[2,32,896]{2,1,0:T(8,128)S(1)}, f32[2,32,896]{2,1,0:T(8,128)S(1)}, u32[]{:S(2)}, u32[]{:S(2)}) %collective-permute-start.9) | collective-permute-done | bytes 229408 | tf_op jit(solution)/shard_map/ppermute | solution.py:259
  39.8 1.0 %collective-permute-done.11 = f32[2,32,896]{2,1,0:T(8,128)S(1)} collective-permute-done((f32[2,32,896]{2,1,0:T(8,128)S(1)}, f32[2,32,896]{2,1,0:T(8,128)S(1)}, u32[]{:S(2)}, u32[]{:S(2)}) %collective-permute-start.11) | collective-permute-done | bytes 229408 | tf_op jit(solution)/shard_map/ppermute | solution.py:259
  40.9 2.3 %collective-permute-start.12 = (f32[4,32,896]{2,1,0:T(8,128)S(1)}, f32[4,32,896]{2,1,0:T(8,128)S(1)}, u32[]{:S(2)}, u32[]{:S(2)}) collective-permute-start(f32[4,32,896]{2,1,0:T(8,128)S(1)} %pad_maximum_fusion), channel_id=1, source_target_pairs={{0,4},{4,0},{8,12},{12,8},{16,20},{20,16},{24,28},{28,24},{1,5},{5... | collective-permute-start | bytes 1376264 | tf_op jit(solution)/shard_map/ppermute | solution.py:259
  43.2 2.5 %feedback.2 = (f32[256,7168]{1,0:T(8,128)}, f32[32,7168]{1,0:T(8,128)}, f32[32,256]{1,0:T(8,128)}) custom-call(bf16[256,128]{1,0:T(8,128)(2,1)S(1)} %get-tuple-element.18.stacked, f32[32,32]{1,0:T(8,128)S(1)} %get-tuple-element.19.inverse, f32[2,32,896]{2,1,0:T(8,128)S(1)} %add.32.refs_0_, f32[2,32,896]{2,1,0:T(8,128)S(1)} %add.35.refs_1_, ...), custom_call_target="tpu_custom_call" | custom-call | flops 234881024 | bytes 3670016 | tf_op jit(solution)/shard_map/feedback/pallas_call | solution.py:235
  45.7 0.0 collective-permute-done.12.refs_0_
  45.7 2.5 %feedback.3 = (f32[256,7168]{1,0:T(8,128)}, f32[32,7168]{1,0:T(8,128)}) custom-call(bf16[256,128]{1,0:T(8,128)(2,1)S(1)} %get-tuple-element.18.stacked, f32[32,32]{1,0:T(8,128)S(1)} %get-tuple-element.19.inverse, f32[4,32,896]{2,1,0:T(8,128)S(1)} %collective-permute-done.12.refs_0_, ...), custom_call_target="tpu_custom_call", output_to_operand_aliasing={{0}: (4, {}), {1}: (5, {})} | custom-call | flops 234881024 | bytes 3670016 | tf_op jit(solution)/shard_map/feedback/pallas_call | solution.py:235
  (11 shorter events, 0.2 us)
Async XLA Ops:
  6.6 1.3 %collective-permute-start = (f32[32,256]{1,0:T(8,128)S(1)}, f32[32,256]{1,0:T(8,128)S(1)}, u32[]{:S(2)}, u32[]{:S(2)}) collective-permute-start(f32[32,256]{1,0:T(8,128)S(1)} %get-tuple-element.17), channel_id=1, source_target_pairs={{0,4},{4,0},{8,12},{12,8},{16,20},{20,16},{24,28},{28,24},{1,5},{5... | collective-permute-start | bytes 98312 | tf_op jit(solution)/shard_map/ppermute | solution.py:259
  7.9 3.7 %collective-permute-start.2 = (f32[32,256]{1,0:T(8,128)S(1)}, f32[32,256]{1,0:T(8,128)S(1)}, u32[]{:S(2)}, u32[]{:S(2)}) collective-permute-start(f32[32,256]{1,0:T(8,128)S(1)} %add.27.mine), channel_id=1, source_target_pairs={{0,8},{1,9},{2,10},{3,11},{4,20},{5,21},{6,22},{7,23},{8,0},{9,1},... | collective-permute-start | bytes 98312 | tf_op jit(solution)/shard_map/ppermute | solution.py:270
  10.2 3.7 %collective-permute-start.1 = (f32[32,256]{1,0:T(8,128)S(1)}, f32[32,256]{1,0:T(8,128)S(1)}, u32[]{:S(2)}, u32[]{:S(2)}) collective-permute-start(f32[32,256]{1,0:T(8,128)S(1)} %add.27.mine), channel_id=1, source_target_pairs={{0,8},{1,9},{2,10},{3,11},{4,28},{5,29},{6,30},{7,31},{8,0},{9,1},... | collective-permute-start | bytes 98312 | tf_op jit(solution)/shard_map/ppermute | solution.py:269
  13.9 1.8 %collective-permute-start.3 = (f32[32,256]{1,0:T(8,128)S(1)}, f32[32,256]{1,0:T(8,128)S(1)}, u32[]{:S(2)}, u32[]{:S(2)}) collective-permute-start(f32[32,256]{1,0:T(8,128)S(1)} %part.2), channel_id=1, source_target_pairs={{0,4},{4,0},{8,12},{12,8},{16,20},{20,16},{24,28},{28,24},{1,5},{5... | collective-permute-start | bytes 98312 | tf_op jit(solution)/shard_map/ppermute | solution.py:259
  15.7 3.8 %collective-permute-start.5 = (f32[32,256]{1,0:T(8,128)S(1)}, f32[32,256]{1,0:T(8,128)S(1)}, u32[]{:S(2)}, u32[]{:S(2)}) collective-permute-start(f32[32,256]{1,0:T(8,128)S(1)} %add.28.mine), channel_id=1, source_target_pairs={{0,1},{1,0},{2,3},{3,2},{4,6},{5,7},{6,4},{7,5},{8,9},{9,8},{10,11... | collective-permute-start | bytes 98312 | tf_op jit(solution)/shard_map/ppermute | solution.py:270
  18.0 4.6 %collective-permute-start.4 = (f32[32,256]{1,0:T(8,128)S(1)}, f32[32,256]{1,0:T(8,128)S(1)}, u32[]{:S(2)}, u32[]{:S(2)}) collective-permute-start(f32[32,256]{1,0:T(8,128)S(1)} %add.28.mine), channel_id=1, source_target_pairs={{0,1},{1,0},{2,3},{3,2},{4,7},{5,6},{6,5},{7,4},{8,9},{9,8},{10,11... | collective-permute-start | bytes 98312 | tf_op jit(solution)/shard_map/ppermute | solution.py:269
  22.6 1.3 %collective-permute-start.6 = (f32[32,256]{1,0:T(8,128)S(1)}, f32[32,256]{1,0:T(8,128)S(1)}, u32[]{:S(2)}, u32[]{:S(2)}) collective-permute-start(f32[32,256]{1,0:T(8,128)S(1)} %part.3.left), channel_id=1, source_target_pairs={{0,4},{4,0},{8,12},{12,8},{16,20},{20,16},{24,28},{28,24},{1,5},{5... | collective-permute-start | bytes 98312 | tf_op jit(solution)/shard_map/ppermute | solution.py:259
  24.7 1.8 %collective-permute-start.7 = (f32[4,32,896]{2,1,0:T(8,128)S(1)}, f32[4,32,896]{2,1,0:T(8,128)S(1)}, u32[]{:S(2)}, u32[]{:S(2)}) collective-permute-start(f32[4,32,896]{2,1,0:T(8,128)S(1)} %right.7), channel_id=1, source_target_pairs={{0,4},{4,0},{8,12},{12,8},{16,20},{20,16},{24,28},{28,24},{1,5},{5... | collective-permute-start | bytes 1376264 | tf_op jit(solution)/shard_map/ppermute | solution.py:259
  26.5 7.1 %collective-permute-start.8 = (f32[2,32,896]{2,1,0:T(8,128)S(1)}, f32[2,32,896]{2,1,0:T(8,128)S(1)}, u32[]{:S(2)}, u32[]{:S(2)}) collective-permute-start(f32[2,32,896]{2,1,0:T(8,128)S(1)} %get-tuple-element.31), channel_id=1, source_target_pairs={{0,8},{4,12},{8,0},{12,4},{16,24},{20,28},{24,16},{28,20},{1,9},{5... | collective-permute-start | bytes 688136 | tf_op jit(solution)/shard_map/ppermute | solution.py:259
  27.7 7.2 %collective-permute-start.10 = (f32[2,32,896]{2,1,0:T(8,128)S(1)}, f32[2,32,896]{2,1,0:T(8,128)S(1)}, u32[]{:S(2)}, u32[]{:S(2)}) collective-permute-start(f32[2,32,896]{2,1,0:T(8,128)S(1)} %get-tuple-element.32), channel_id=1, source_target_pairs={{0,16},{4,20},{8,24},{12,28},{16,0},{20,4},{24,8},{28,12},{1,17},{... | collective-permute-start | bytes 688136 | tf_op jit(solution)/shard_map/ppermute | solution.py:259
  33.6 6.1 %collective-permute-start.9 = (f32[2,32,896]{2,1,0:T(8,128)S(1)}, f32[2,32,896]{2,1,0:T(8,128)S(1)}, u32[]{:S(2)}, u32[]{:S(2)}) collective-permute-start(f32[2,32,896]{2,1,0:T(8,128)S(1)} %add.31), channel_id=1, source_target_pairs={{0,16},{4,20},{8,24},{12,28},{16,0},{20,4},{24,8},{28,12},{1,17},{... | collective-permute-start | bytes 688136 | tf_op jit(solution)/shard_map/ppermute | solution.py:259
  35.0 5.9 %collective-permute-start.11 = (f32[2,32,896]{2,1,0:T(8,128)S(1)}, f32[2,32,896]{2,1,0:T(8,128)S(1)}, u32[]{:S(2)}, u32[]{:S(2)}) collective-permute-start(f32[2,32,896]{2,1,0:T(8,128)S(1)} %add.34), channel_id=1, source_target_pairs={{0,8},{4,12},{8,0},{12,4},{16,24},{20,28},{24,16},{28,20},{1,9},{5... | collective-permute-start | bytes 688136 | tf_op jit(solution)/shard_map/ppermute | solution.py:259
  40.9 4.8 %collective-permute-start.12 = (f32[4,32,896]{2,1,0:T(8,128)S(1)}, f32[4,32,896]{2,1,0:T(8,128)S(1)}, u32[]{:S(2)}, u32[]{:S(2)}) collective-permute-start(f32[4,32,896]{2,1,0:T(8,128)S(1)} %pad_maximum_fusion), channel_id=1, source_target_pairs={{0,4},{4,0},{8,12},{12,8},{16,20},{20,16},{24,28},{28,24},{1,5},{5... | collective-permute-start | bytes 1376264 | tf_op jit(solution)/shard_map/ppermute | solution.py:259

commit v9 on v8

--- a/solution.py
+++ b/solution.py
@@ -8,6 +8,7 @@
 from jax.sharding import PartitionSpec as P
 
 F32, BF16 = jnp.float32, jnp.bfloat16
+BLOCK = 256
 HIGHEST = lax.Precision.HIGHEST
 ANY = pl.BlockSpec(memory_space=pl.ANY)
 VMEM = pl.BlockSpec(memory_space=pltpu.VMEM)
@@ -39,7 +40,7 @@
     return pl.CostEstimate(flops=int(flops), bytes_accessed=int(bytes_accessed), transcendentals=0)
 
 
-def left_kernel(chunk, gradient, feedback, right, combined, high, low, left, gradient_buf, right_buf, sems):
+def left_kernel(chunk, gradient, feedback, right, high, low, left, gradient_buf, feedback_buf, right_buf, sems):
     rows, columns = gradient.shape
     rank = right.shape[0]
     blocks = [pl.ds(i * chunk, chunk) for i in range(columns // chunk)]
@@ -47,16 +48,15 @@
     for i, at in enumerate(blocks):
         group = [
             pltpu.make_async_copy(gradient.at[:, at], gradient_buf.at[:, at], sems.at[0, i]),
-            pltpu.make_async_copy(feedback.at[:, at], combined.at[:, at], sems.at[1, i]),
+            pltpu.make_async_copy(feedback.at[:, at], feedback_buf.at[:, at], sems.at[1, i]),
             pltpu.make_async_copy(right.at[:, at], right_buf.at[:, at], sems.at[2, i]),
         ]
         for copy in group:
             copy.start()
         copies.append(group)
-    padded = combined.shape[1]
+    padded = high.shape[1]
     if padded > columns:
         rest = pl.ds(columns, padded - columns)
-        combined[:, rest] = jnp.zeros((rows, padded - columns), F32)
         high[:, rest] = jnp.zeros((rows, padded - columns), BF16)
         low[:, rest] = jnp.zeros((rows, padded - columns), BF16)
     total = jnp.zeros((rows, 2 * rank), F32)
@@ -64,9 +64,7 @@
         for copy in group:
             copy.wait()
         both = jnp.concatenate(split(right_buf[:, at]), axis=0)
-        c = combined[:, at] + gradient_buf[:, at].astype(F32)
-        c_high, c_low = split(c)
-        combined[:, at] = c
+        c_high, c_low = split(feedback_buf[:, at] + gradient_buf[:, at].astype(F32))
         high[:, at] = c_high
         low[:, at] = c_low
         total += dot(c_high, both, 1, 1) + dot(c_low, both, 1, 1)
@@ -80,15 +78,15 @@
     return pl.pallas_call(
         functools.partial(left_kernel, chunk),
         in_specs=[ANY] * 3,
-        out_specs=[VMEM] * 4,
+        out_specs=[VMEM] * 3,
         out_shape=[
-            pltpu.VMEM((rows, padded), F32),
             pltpu.VMEM((rows, padded), BF16),
             pltpu.VMEM((rows, padded), BF16),
             pltpu.VMEM((rank, rows), F32),
         ],
         scratch_shapes=[
             pltpu.VMEM((rows, columns), BF16),
+            pltpu.VMEM((rows, columns), F32),
             pltpu.VMEM((rank, columns), F32),
             pltpu.SemaphoreType.DMA((3, columns // chunk)),
         ],
@@ -172,9 +170,9 @@
     )(left)
 
 
-def feedback_kernel(own, columns, stacked, inverse, pieces, combined, factor, feedback, right, factor_out, feedback_buf, right_buf, sems, factor_sem):
+def feedback_kernel(own, columns, stacked, inverse, pieces, high, low, factor, feedback, right, factor_out, feedback_buf, right_buf, sems, factor_sem):
     chips, rows, width = feedback_buf.shape
-    whole = combined.shape[1] == columns
+    whole = high.shape[1] == columns
     core, _ = position()
     side = core if own else 1 - core
     copies = []
@@ -183,19 +181,20 @@
         factor_copy.start()
     for k in range(chips):
         place = side * chips + k
+        for i, start in enumerate(range(0, width, BLOCK)):
+            size = min(BLOCK, width - start)
+            here = pl.ds(start, size)
+            at = pl.ds(pl.multiple_of(place * width + start, 128), size)
+            piece = dot(inverse[...], pieces[k][:, here], 1, 0, lax.Precision.HIGH)
+            right_buf[k, :, here] = piece
+            piece_high, piece_low = split(piece)
+            four = jnp.concatenate([piece_high, piece_high, piece_low, piece_low], axis=0)
+            combined = high[:, at].astype(F32) + low[:, at].astype(F32)
+            feedback_buf[k, :, here] = combined - dot(stacked[...], four, 1, 0)
+            copies.append((place * width < columns, pltpu.make_async_copy(feedback_buf.at[k, :, here], feedback.at[:, at], sems.at[k, i])))
+            start_or_wait(copies[-1], whole, "start")
         at = pl.ds(pl.multiple_of(place * width, 128), width)
-        piece = dot(inverse[...], pieces[k][...], 1, 0, HIGHEST)
-        right_buf[k] = piece
-        piece_high, piece_low = split(piece)
-        four = jnp.concatenate([piece_high, piece_high, piece_low, piece_low], axis=0)
-        feedback_buf[k] = combined[:, at] - dot(stacked[...], four, 1, 0)
-        copies.append(
-            (
-                place * width < columns,
-                pltpu.make_async_copy(feedback_buf.at[k], feedback.at[:, at], sems.at[0, k]),
-                pltpu.make_async_copy(right_buf.at[k], right.at[:, at], sems.at[1, k]),
-            )
-        )
+        copies.append((place * width < columns, pltpu.make_async_copy(right_buf.at[k], right.at[:, at], sems.at[k, sems.shape[1] - 1])))
         start_or_wait(copies[-1], whole, "start")
     for copy in copies:
         start_or_wait(copy, whole, "wait")
@@ -204,11 +203,10 @@
 
 
 def start_or_wait(copy, whole, action):
-    inside, *both = copy
+    inside, one = copy
 
     def run():
-        for one in both:
-            getattr(one, action)()
+        getattr(one, action)()
 
     if whole:
         run()
@@ -216,21 +214,21 @@
         pl.when(inside)(run)
 
 
-def new_feedback(own, stacked, inverse, given, combined, columns, last):
-    rows = combined.shape[0]
+def new_feedback(own, stacked, inverse, given, high, low, columns, last):
+    rows = high.shape[0]
     chips = sum(x.shape[0] for x in given)
     rank, width = given[0].shape[-2:]
     outs = 3 if own else 2
-    first = 3 + len(given)
+    first = 4 + len(given)
 
     def kernel(stacked, inverse, *refs):
         parts = [x.at[k] for x in refs[: len(given)] for k in range(x.shape[0])]
         if own:
-            combined, factor, feedback, right, factor_out, *scratch = refs[len(given) :]
+            high, low, factor, feedback, right, factor_out, *scratch = refs[len(given) :]
         else:
-            combined, _, _, feedback, right, *scratch = refs[len(given) :]
+            high, low, _, _, feedback, right, *scratch = refs[len(given) :]
             factor = factor_out = None
-        feedback_kernel(own, columns, stacked, inverse, parts, combined, factor, feedback, right, factor_out, *scratch)
+        feedback_kernel(own, columns, stacked, inverse, parts, high, low, factor, feedback, right, factor_out, *scratch)
 
     return pl.pallas_call(
         kernel,
@@ -245,13 +243,13 @@
         scratch_shapes=[
             pltpu.VMEM((chips, rows, width), F32),
             pltpu.VMEM((chips, rank, width), F32),
-            pltpu.SemaphoreType.DMA((2, chips)),
+            pltpu.SemaphoreType.DMA((chips, -(-width // BLOCK) + 1)),
             pltpu.SemaphoreType.DMA,
         ],
         compiler_params=params(16),
         cost_estimate=cost(8 * rows * chips * width * rank, 4 * rows * chips * width),
         name="feedback",
-    )(stacked, inverse, *given, combined, *last)
+    )(stacked, inverse, *given, high, low, *last)
 
 
 def swap(x, axis, mask):
@@ -317,8 +315,8 @@
     assert columns % width == 0
 
     given = [keep(x, pltpu.HBM) for x in (gradient, feedback, right_factor.T)]
-    combined, high, low, left = left_product(*given, replicas * width)
-    combined, high, low = (keep(x, pltpu.VMEM) for x in (combined, high, low))
+    high, low, left = left_product(*given, replicas * width)
+    high, low = (keep(x, pltpu.VMEM) for x in (high, low))
     left = left + swap(left, "dp", 1)
     stages = [("dp", low, count) for low, count in steps(1, bits("dp"))]
     stages += [("tensor", low, count) for low, count in steps(0, bits("tensor"))]
@@ -344,8 +342,8 @@
         parts = [x + y for x, y in zip(parts, came)]
 
     other = swap(jnp.concatenate(parts), "dp", 1)
-    *outs, factor = new_feedback(True, stacked, inverse, parts, combined, columns, [factor])
-    outs = new_feedback(False, stacked, inverse, [other], combined, columns, outs)
+    *outs, factor = new_feedback(True, stacked, inverse, parts, high, low, columns, [factor])
+    outs = new_feedback(False, stacked, inverse, [other], high, low, columns, outs)
     return (outs[0][None], factor.T, outs[1].T)
 
 

time: 48.4 us -> 49 us (1.012)
  Pallas kernels: 17.1 us -> 17.7 us
    pallas_call x2, Pallas kernels: 5.08 us -> 5.88 us  [new_feedback(): pl.pallas_call(kernel, in_specs=[VMEM] * first + ([VMEM] if own else [ANY...]
  transfers between devices with their start and end apart: 13 -> 13, of which waited for: 11 -> 11; matrix products, arithmetic and copies ran while one was open for 0% -> 0% of each run, Pallas kernels for 16% -> 17%
where the time goes in v9:
time: 49 us; the launch traced here: 48.9 us
  Pallas kernels  17.7 us (36%)
  waiting for transfers between devices  16.2 us (33%)
  starting transfers between devices  14.1 us (29%)
  between operations  0.71 us (1%)
    ppermute x9, waiting for transfers between devices, swap(): return lax.ppermute(x, axis, [(i, i ^ mask) for i in range(size)])  10.1 us
    ppermute x9, starting transfers between devices, swap(): return lax.ppermute(x, axis, [(i, i ^ mask) for i in range(size)])  7.15 us
    pallas_call x2, Pallas kernels, new_feedback(): pl.pallas_call(kernel, in_specs=[VMEM] * first + ([VMEM] if own else [ANY...  5.88 us
    pallas_call x1, Pallas kernels, left_product(): pl.pallas_call(functools.partial(left_kernel, chunk), in_specs=[ANY] * 3,...  5.7 us
    ppermute x2, waiting for transfers between devices, sum_stage(): lax.ppermute(x, ('dp', 'tensor'), pairs_of(axis, 1 << low, 3 << low))  5.51 us
    ppermute x2, starting transfers between devices, sum_stage(): lax.ppermute(x, ('dp', 'tensor'), pairs_of(axis, 1 << low, 2 << low))  4.71 us
    pallas_call x1, Pallas kernels, factors(): pl.pallas_call(functools.partial(factor_kernel, scale), in_specs=[VMEM],...  3.12 us
    pallas_call x4, Pallas kernels, right_product(): pl.pallas_call(functools.partial(right_kernel, own), in_specs=[VMEM] * (3...  2.98 us
  transfers between devices with their start and end apart: 13, of which 11 were waited for; matrix products, arithmetic and copies ran while one was open for 0% of the time, Pallas kernels for 17%

profile of v9, /device:TPU:1, one launch (start us, length us, event | category | flops | bytes accessed | tf_op | source)
XLA Modules:
  0.0 48.9 jit_solution(3821563513903277308)
XLA Ops:
  0.6 5.7 %left.1 = (bf16[256,7168]{1,0:T(8,128)(2,1)S(1)}, bf16[256,7168]{1,0:T(8,128)(2,1)S(1)}, f32[32,256]{1,0:T(8,128)S(1)}) custom-call(bf16[256,7168]{1,0:T(8,128)(2,1)} %bitcast.8, f32[256,7168]{1,0:T(8,128)} %bitcast.7, f32[32,7168]{1,0:T(8,128)} %bitcast.9), custom_call_target="tpu_custom_call" | custom-call | flops 469762048 | bytes 11010048 | tf_op jit(solution)/shard_map/left/pallas_call | solution.py:78
  6.3 0.1 collective-permute-start
  6.5 1.1 %collective-permute-done = f32[32,256]{1,0:T(8,128)S(1)} collective-permute-done((f32[32,256]{1,0:T(8,128)S(1)}, f32[32,256]{1,0:T(8,128)S(1)}, u32[]{:S(2)}, u32[]{:S(2)}) %collective-permute-start) | collective-permute-done | bytes 32800 | tf_op jit(solution)/shard_map/ppermute | solution.py:257
  7.6 2.4 %collective-permute-start.2 = (f32[32,256]{1,0:T(8,128)S(1)}, f32[32,256]{1,0:T(8,128)S(1)}, u32[]{:S(2)}, u32[]{:S(2)}) collective-permute-start(f32[32,256]{1,0:T(8,128)S(1)} %add.27.mine), channel_id=1, source_target_pairs={{0,8},{1,9},{2,10},{3,11},{4,20},{5,21},{6,22},{7,23},{8,0},{9,1},... | collective-permute-start | bytes 98312 | tf_op jit(solution)/shard_map/ppermute | solution.py:268
  10.0 1.2 %collective-permute-start.1 = (f32[32,256]{1,0:T(8,128)S(1)}, f32[32,256]{1,0:T(8,128)S(1)}, u32[]{:S(2)}, u32[]{:S(2)}) collective-permute-start(f32[32,256]{1,0:T(8,128)S(1)} %add.27.mine), channel_id=1, source_target_pairs={{0,8},{1,9},{2,10},{3,11},{4,28},{5,29},{6,30},{7,31},{8,0},{9,1},... | collective-permute-start | bytes 98312 | tf_op jit(solution)/shard_map/ppermute | solution.py:267
  11.2 0.1 collective-permute-done.2.second
  11.3 2.4 %collective-permute-done.1.first = f32[32,256]{1,0:T(8,128)S(1)} collective-permute-done((f32[32,256]{1,0:T(8,128)S(1)}, f32[32,256]{1,0:T(8,128)S(1)}, u32[]{:S(2)}, u32[]{:S(2)}) %collective-permute-start.1) | collective-permute-done | bytes 32800 | tf_op jit(solution)/shard_map/ppermute | solution.py:267
  13.7 0.9 %collective-permute-start.3 = (f32[32,256]{1,0:T(8,128)S(1)}, f32[32,256]{1,0:T(8,128)S(1)}, u32[]{:S(2)}, u32[]{:S(2)}) collective-permute-start(f32[32,256]{1,0:T(8,128)S(1)} %part.2), channel_id=1, source_target_pairs={{0,4},{4,0},{8,12},{12,8},{16,20},{20,16},{24,28},{28,24},{1,5},{5... | collective-permute-start | bytes 98312 | tf_op jit(solution)/shard_map/ppermute | solution.py:257
  14.6 0.9 %collective-permute-done.3 = f32[32,256]{1,0:T(8,128)S(1)} collective-permute-done((f32[32,256]{1,0:T(8,128)S(1)}, f32[32,256]{1,0:T(8,128)S(1)}, u32[]{:S(2)}, u32[]{:S(2)}) %collective-permute-start.3) | collective-permute-done | bytes 32800 | tf_op jit(solution)/shard_map/ppermute | solution.py:257
  15.5 2.3 %collective-permute-start.5 = (f32[32,256]{1,0:T(8,128)S(1)}, f32[32,256]{1,0:T(8,128)S(1)}, u32[]{:S(2)}, u32[]{:S(2)}) collective-permute-start(f32[32,256]{1,0:T(8,128)S(1)} %add.28.mine), channel_id=1, source_target_pairs={{0,1},{1,0},{2,3},{3,2},{4,6},{5,7},{6,4},{7,5},{8,9},{9,8},{10,11... | collective-permute-start | bytes 98312 | tf_op jit(solution)/shard_map/ppermute | solution.py:268
  17.8 1.1 %collective-permute-start.4 = (f32[32,256]{1,0:T(8,128)S(1)}, f32[32,256]{1,0:T(8,128)S(1)}, u32[]{:S(2)}, u32[]{:S(2)}) collective-permute-start(f32[32,256]{1,0:T(8,128)S(1)} %add.28.mine), channel_id=1, source_target_pairs={{0,1},{1,0},{2,3},{3,2},{4,7},{5,6},{6,5},{7,4},{8,9},{9,8},{10,11... | collective-permute-start | bytes 98312 | tf_op jit(solution)/shard_map/ppermute | solution.py:267
  18.9 0.4 collective-permute-done.5.second
  19.2 3.1 %collective-permute-done.4.first = f32[32,256]{1,0:T(8,128)S(1)} collective-permute-done((f32[32,256]{1,0:T(8,128)S(1)}, f32[32,256]{1,0:T(8,128)S(1)}, u32[]{:S(2)}, u32[]{:S(2)}) %collective-permute-start.4) | collective-permute-done | bytes 32800 | tf_op jit(solution)/shard_map/ppermute | solution.py:267
  22.4 0.1 collective-permute-start.6
  22.5 0.7 %right.6.refs_0_ = f32[4,32,896]{2,1,0:T(8,128)S(1)} custom-call(f32[32,256]{1,0:T(8,128)S(1)} %part.3.left, bf16[256,7168]{1,0:T(8,128)(2,1)S(1)} %get-tuple-element.19.high.refs_2_.refs_1_, bf16[256,7168]{1,0:T(8,128)(2,1)S(1)} %get-tuple-element.20.low.refs_3_.refs_2_), custom_call_target="tpu_custom_call" | custom-call | flops 234881024 | bytes 3670016 | tf_op jit(solution)/shard_map/right/pallas_call | solution.py:123
  23.2 0.4 collective-permute-done.6.left
  23.7 0.7 %right.7 = f32[4,32,896]{2,1,0:T(8,128)S(1)} custom-call(f32[32,256]{1,0:T(8,128)S(1)} %collective-permute-done.6.left, bf16[256,7168]{1,0:T(8,128)(2,1)S(1)} %get-tuple-element.19.high.refs_2_.refs_1_, bf16[256,7168]{1,0:T(8,128)(2,1)S(1)} %get-tuple-element.20.low.refs_3_.refs_2_, f32[4,32,896]{2,1,0:T(8,128)S(1)} %right.6.refs_0_), custom_call_target="tpu_custom_call" | custom-call | flops 234881024 | bytes 3670016 | tf_op jit(solution)/shard_map/right/pallas_call | solution.py:123
  24.4 0.2 collective-permute-start.7
  24.6 0.7 %right.4.refs_0_ = f32[4,32,896]{2,1,0:T(8,128)S(1)} custom-call(f32[32,256]{1,0:T(8,128)S(1)} %part.3.left, bf16[256,7168]{1,0:T(8,128)(2,1)S(1)} %get-tuple-element.19.high.refs_2_.refs_1_, bf16[256,7168]{1,0:T(8,128)(2,1)S(1)} %get-tuple-element.20.low.refs_3_.refs_2_), custom_call_target="tpu_custom_call" | custom-call | flops 234881024 | bytes 3670016 | tf_op jit(solution)/shard_map/right/pallas_call | solution.py:123
  25.3 0.8 %right.5 = f32[4,32,896]{2,1,0:T(8,128)S(1)} custom-call(f32[32,256]{1,0:T(8,128)S(1)} %collective-permute-done.6.left, bf16[256,7168]{1,0:T(8,128)(2,1)S(1)} %get-tuple-element.19.high.refs_2_.refs_1_, bf16[256,7168]{1,0:T(8,128)(2,1)S(1)} %get-tuple-element.20.low.refs_3_.refs_2_, f32[4,32,896]{2,1,0:T(8,128)S(1)} %right.4.refs_0_), custom_call_target="tpu_custom_call" | custom-call | flops 234881024 | bytes 3670016 | tf_op jit(solution)/shard_map/right/pallas_call | solution.py:123
  26.1 0.2 collective-permute-done.7
  26.3 1.2 %collective-permute-start.8 = (f32[2,32,896]{2,1,0:T(8,128)S(1)}, f32[2,32,896]{2,1,0:T(8,128)S(1)}, u32[]{:S(2)}, u32[]{:S(2)}) collective-permute-start(f32[2,32,896]{2,1,0:T(8,128)S(1)} %get-tuple-element.29), channel_id=1, source_target_pairs={{0,8},{4,12},{8,0},{12,4},{16,24},{20,28},{24,16},{28,20},{1,9},{5... | collective-permute-start | bytes 688136 | tf_op jit(solution)/shard_map/ppermute | solution.py:257
  27.5 0.6 %collective-permute-start.10 = (f32[2,32,896]{2,1,0:T(8,128)S(1)}, f32[2,32,896]{2,1,0:T(8,128)S(1)}, u32[]{:S(2)}, u32[]{:S(2)}) collective-permute-start(f32[2,32,896]{2,1,0:T(8,128)S(1)} %get-tuple-element.30), channel_id=1, source_target_pairs={{0,16},{4,20},{8,24},{12,28},{16,0},{20,4},{24,8},{28,12},{1,17},{... | collective-permute-start | bytes 688136 | tf_op jit(solution)/shard_map/ppermute | solution.py:257
  28.1 3.1 %factor.1 = (f32[32,32]{1,0:T(8,128)S(1)}, f32[32,256]{1,0:T(8,128)S(1)}, bf16[256,128]{1,0:T(8,128)(2,1)S(1)}) custom-call(f32[32,256]{1,0:T(8,128)S(1)} %add_multiply_fusion.left), custom_call_target="tpu_custom_call" | custom-call | flops 2000000000 | bytes 1000000 | tf_op jit(solution)/shard_map/factor/pallas_call | solution.py:158
  31.2 2.2 %collective-permute-done.8 = f32[2,32,896]{2,1,0:T(8,128)S(1)} collective-permute-done((f32[2,32,896]{2,1,0:T(8,128)S(1)}, f32[2,32,896]{2,1,0:T(8,128)S(1)}, u32[]{:S(2)}, u32[]{:S(2)}) %collective-permute-start.8) | collective-permute-done | bytes 229408 | tf_op jit(solution)/shard_map/ppermute | solution.py:257
  33.4 1.3 %collective-permute-start.9 = (f32[2,32,896]{2,1,0:T(8,128)S(1)}, f32[2,32,896]{2,1,0:T(8,128)S(1)}, u32[]{:S(2)}, u32[]{:S(2)}) collective-permute-start(f32[2,32,896]{2,1,0:T(8,128)S(1)} %add.31), channel_id=1, source_target_pairs={{0,16},{4,20},{8,24},{12,28},{16,0},{20,4},{24,8},{28,12},{1,17},{... | collective-permute-start | bytes 688136 | tf_op jit(solution)/shard_map/ppermute | solution.py:257
  34.7 0.0 collective-permute-done.10
  34.7 0.5 %collective-permute-start.11 = (f32[2,32,896]{2,1,0:T(8,128)S(1)}, f32[2,32,896]{2,1,0:T(8,128)S(1)}, u32[]{:S(2)}, u32[]{:S(2)}) collective-permute-start(f32[2,32,896]{2,1,0:T(8,128)S(1)} %add.34), channel_id=1, source_target_pairs={{0,8},{4,12},{8,0},{12,4},{16,24},{20,28},{24,16},{28,20},{1,9},{5... | collective-permute-start | bytes 688136 | tf_op jit(solution)/shard_map/ppermute | solution.py:257
  35.3 4.3 %collective-permute-done.9 = f32[2,32,896]{2,1,0:T(8,128)S(1)} collective-permute-done((f32[2,32,896]{2,1,0:T(8,128)S(1)}, f32[2,32,896]{2,1,0:T(8,128)S(1)}, u32[]{:S(2)}, u32[]{:S(2)}) %collective-permute-start.9) | collective-permute-done | bytes 229408 | tf_op jit(solution)/shard_map/ppermute | solution.py:257
  39.6 1.0 %collective-permute-done.11 = f32[2,32,896]{2,1,0:T(8,128)S(1)} collective-permute-done((f32[2,32,896]{2,1,0:T(8,128)S(1)}, f32[2,32,896]{2,1,0:T(8,128)S(1)}, u32[]{:S(2)}, u32[]{:S(2)}) %collective-permute-start.11) | collective-permute-done | bytes 229408 | tf_op jit(solution)/shard_map/ppermute | solution.py:257
  40.7 2.3 %collective-permute-start.12 = (f32[4,32,896]{2,1,0:T(8,128)S(1)}, f32[4,32,896]{2,1,0:T(8,128)S(1)}, u32[]{:S(2)}, u32[]{:S(2)}) collective-permute-start(f32[4,32,896]{2,1,0:T(8,128)S(1)} %pad_maximum_fusion), channel_id=1, source_target_pairs={{0,4},{4,0},{8,12},{12,8},{16,20},{20,16},{24,28},{28,24},{1,5},{5... | collective-permute-start | bytes 1376264 | tf_op jit(solution)/shard_map/ppermute | solution.py:257
  43.0 2.9 %feedback.2 = (f32[256,7168]{1,0:T(8,128)}, f32[32,7168]{1,0:T(8,128)}, f32[32,256]{1,0:T(8,128)}) custom-call(bf16[256,128]{1,0:T(8,128)(2,1)S(1)} %get-tuple-element.17.stacked, f32[32,32]{1,0:T(8,128)S(1)} %get-tuple-element.18.inverse, f32[2,32,896]{2,1,0:T(8,128)S(1)} %add.32.refs_0_, f32[2,32,896]{2,1,0:T(8,128)S(1)} %add.35.refs_1_, ...), custom_call_target="tpu_custom_call" | custom-call | flops 234881024 | bytes 3670016 | tf_op jit(solution)/shard_map/feedback/pallas_call | solution.py:233
  45.9 0.0 collective-permute-done.12.refs_0_
  45.9 2.9 %feedback.3 = (f32[256,7168]{1,0:T(8,128)}, f32[32,7168]{1,0:T(8,128)}) custom-call(bf16[256,128]{1,0:T(8,128)(2,1)S(1)} %get-tuple-element.17.stacked, f32[32,32]{1,0:T(8,128)S(1)} %get-tuple-element.18.inverse, f32[4,32,896]{2,1,0:T(8,128)S(1)} %collective-permute-done.12.refs_0_, ...), custom_call_target="tpu_custom_call", output_to_operand_aliasing={{0}: (5, {}), {1}: (6, {})} | custom-call | flops 234881024 | bytes 3670016 | tf_op jit(solution)/shard_map/feedback/pallas_call | solution.py:233
  (11 shorter events, 0.2 us)
Async XLA Ops:
  6.3 1.3 %collective-permute-start = (f32[32,256]{1,0:T(8,128)S(1)}, f32[32,256]{1,0:T(8,128)S(1)}, u32[]{:S(2)}, u32[]{:S(2)}) collective-permute-start(f32[32,256]{1,0:T(8,128)S(1)} %get-tuple-element.16), channel_id=1, source_target_pairs={{0,4},{4,0},{8,12},{12,8},{16,20},{20,16},{24,28},{28,24},{1,5},{5... | collective-permute-start | bytes 98312 | tf_op jit(solution)/shard_map/ppermute | solution.py:257
  7.6 3.7 %collective-permute-start.2 = (f32[32,256]{1,0:T(8,128)S(1)}, f32[32,256]{1,0:T(8,128)S(1)}, u32[]{:S(2)}, u32[]{:S(2)}) collective-permute-start(f32[32,256]{1,0:T(8,128)S(1)} %add.27.mine), channel_id=1, source_target_pairs={{0,8},{1,9},{2,10},{3,11},{4,20},{5,21},{6,22},{7,23},{8,0},{9,1},... | collective-permute-start | bytes 98312 | tf_op jit(solution)/shard_map/ppermute | solution.py:268
  10.0 3.7 %collective-permute-start.1 = (f32[32,256]{1,0:T(8,128)S(1)}, f32[32,256]{1,0:T(8,128)S(1)}, u32[]{:S(2)}, u32[]{:S(2)}) collective-permute-start(f32[32,256]{1,0:T(8,128)S(1)} %add.27.mine), channel_id=1, source_target_pairs={{0,8},{1,9},{2,10},{3,11},{4,28},{5,29},{6,30},{7,31},{8,0},{9,1},... | collective-permute-start | bytes 98312 | tf_op jit(solution)/shard_map/ppermute | solution.py:267
  13.7 1.8 %collective-permute-start.3 = (f32[32,256]{1,0:T(8,128)S(1)}, f32[32,256]{1,0:T(8,128)S(1)}, u32[]{:S(2)}, u32[]{:S(2)}) collective-permute-start(f32[32,256]{1,0:T(8,128)S(1)} %part.2), channel_id=1, source_target_pairs={{0,4},{4,0},{8,12},{12,8},{16,20},{20,16},{24,28},{28,24},{1,5},{5... | collective-permute-start | bytes 98312 | tf_op jit(solution)/shard_map/ppermute | solution.py:257
  15.5 3.8 %collective-permute-start.5 = (f32[32,256]{1,0:T(8,128)S(1)}, f32[32,256]{1,0:T(8,128)S(1)}, u32[]{:S(2)}, u32[]{:S(2)}) collective-permute-start(f32[32,256]{1,0:T(8,128)S(1)} %add.28.mine), channel_id=1, source_target_pairs={{0,1},{1,0},{2,3},{3,2},{4,6},{5,7},{6,4},{7,5},{8,9},{9,8},{10,11... | collective-permute-start | bytes 98312 | tf_op jit(solution)/shard_map/ppermute | solution.py:268
  17.8 4.6 %collective-permute-start.4 = (f32[32,256]{1,0:T(8,128)S(1)}, f32[32,256]{1,0:T(8,128)S(1)}, u32[]{:S(2)}, u32[]{:S(2)}) collective-permute-start(f32[32,256]{1,0:T(8,128)S(1)} %add.28.mine), channel_id=1, source_target_pairs={{0,1},{1,0},{2,3},{3,2},{4,7},{5,6},{6,5},{7,4},{8,9},{9,8},{10,11... | collective-permute-start | bytes 98312 | tf_op jit(solution)/shard_map/ppermute | solution.py:267
  22.4 1.3 %collective-permute-start.6 = (f32[32,256]{1,0:T(8,128)S(1)}, f32[32,256]{1,0:T(8,128)S(1)}, u32[]{:S(2)}, u32[]{:S(2)}) collective-permute-start(f32[32,256]{1,0:T(8,128)S(1)} %part.3.left), channel_id=1, source_target_pairs={{0,4},{4,0},{8,12},{12,8},{16,20},{20,16},{24,28},{28,24},{1,5},{5... | collective-permute-start | bytes 98312 | tf_op jit(solution)/shard_map/ppermute | solution.py:257
  24.4 1.8 %collective-permute-start.7 = (f32[4,32,896]{2,1,0:T(8,128)S(1)}, f32[4,32,896]{2,1,0:T(8,128)S(1)}, u32[]{:S(2)}, u32[]{:S(2)}) collective-permute-start(f32[4,32,896]{2,1,0:T(8,128)S(1)} %right.7), channel_id=1, source_target_pairs={{0,4},{4,0},{8,12},{12,8},{16,20},{20,16},{24,28},{28,24},{1,5},{5... | collective-permute-start | bytes 1376264 | tf_op jit(solution)/shard_map/ppermute | solution.py:257
  26.3 7.1 %collective-permute-start.8 = (f32[2,32,896]{2,1,0:T(8,128)S(1)}, f32[2,32,896]{2,1,0:T(8,128)S(1)}, u32[]{:S(2)}, u32[]{:S(2)}) collective-permute-start(f32[2,32,896]{2,1,0:T(8,128)S(1)} %get-tuple-element.29), channel_id=1, source_target_pairs={{0,8},{4,12},{8,0},{12,4},{16,24},{20,28},{24,16},{28,20},{1,9},{5... | collective-permute-start | bytes 688136 | tf_op jit(solution)/shard_map/ppermute | solution.py:257
  27.5 7.2 %collective-permute-start.10 = (f32[2,32,896]{2,1,0:T(8,128)S(1)}, f32[2,32,896]{2,1,0:T(8,128)S(1)}, u32[]{:S(2)}, u32[]{:S(2)}) collective-permute-start(f32[2,32,896]{2,1,0:T(8,128)S(1)} %get-tuple-element.30), channel_id=1, source_target_pairs={{0,16},{4,20},{8,24},{12,28},{16,0},{20,4},{24,8},{28,12},{1,17},{... | collective-permute-start | bytes 688136 | tf_op jit(solution)/shard_map/ppermute | solution.py:257
  33.4 6.1 %collective-permute-start.9 = (f32[2,32,896]{2,1,0:T(8,128)S(1)}, f32[2,32,896]{2,1,0:T(8,128)S(1)}, u32[]{:S(2)}, u32[]{:S(2)}) collective-permute-start(f32[2,32,896]{2,1,0:T(8,128)S(1)} %add.31), channel_id=1, source_target_pairs={{0,16},{4,20},{8,24},{12,28},{16,0},{20,4},{24,8},{28,12},{1,17},{... | collective-permute-start | bytes 688136 | tf_op jit(solution)/shard_map/ppermute | solution.py:257
  34.7 5.9 %collective-permute-start.11 = (f32[2,32,896]{2,1,0:T(8,128)S(1)}, f32[2,32,896]{2,1,0:T(8,128)S(1)}, u32[]{:S(2)}, u32[]{:S(2)}) collective-permute-start(f32[2,32,896]{2,1,0:T(8,128)S(1)} %add.34), channel_id=1, source_target_pairs={{0,8},{4,12},{8,0},{12,4},{16,24},{20,28},{24,16},{28,20},{1,9},{5... | collective-permute-start | bytes 688136 | tf_op jit(solution)/shard_map/ppermute | solution.py:257
  40.7 5.2 %collective-permute-start.12 = (f32[4,32,896]{2,1,0:T(8,128)S(1)}, f32[4,32,896]{2,1,0:T(8,128)S(1)}, u32[]{:S(2)}, u32[]{:S(2)}) collective-permute-start(f32[4,32,896]{2,1,0:T(8,128)S(1)} %pad_maximum_fusion), channel_id=1, source_target_pairs={{0,4},{4,0},{8,12},{12,8},{16,20},{20,16},{24,28},{28,24},{1,5},{5... | collective-permute-start | bytes 1376264 | tf_op jit(solution)/shard_map/ppermute | solution.py:257

commit v10 on v8

--- a/solution.py
+++ b/solution.py
@@ -181,11 +181,12 @@
     if own:
         factor_copy = pltpu.make_async_copy(factor, factor_out, factor_sem)
         factor_copy.start()
-    for k in range(chips):
+    rights = [dot(inverse[...], pieces[k][...], 1, 0, lax.Precision.HIGH) for k in range(chips)]
+    for k, piece in enumerate(rights):
+        right_buf[k] = piece
+    for k, piece in enumerate(rights):
         place = side * chips + k
         at = pl.ds(pl.multiple_of(place * width, 128), width)
-        piece = dot(inverse[...], pieces[k][...], 1, 0, HIGHEST)
-        right_buf[k] = piece
         piece_high, piece_low = split(piece)
         four = jnp.concatenate([piece_high, piece_high, piece_low, piece_low], axis=0)
         feedback_buf[k] = combined[:, at] - dot(stacked[...], four, 1, 0)

time: 48.4 us -> 48.4 us (level)
  no operation moved by 1% of the time
where the time goes in v10:
time: 48.4 us; the launch traced here: 48.3 us
  Pallas kernels  17.1 us (35%)
  waiting for transfers between devices  16.1 us (33%)
  starting transfers between devices  14.1 us (29%)
  between operations  0.71 us (1%)
    ppermute x9, waiting for transfers between devices, swap(): return lax.ppermute(x, axis, [(i, i ^ mask) for i in range(size)])  10.1 us
    ppermute x9, starting transfers between devices, swap(): return lax.ppermute(x, axis, [(i, i ^ mask) for i in range(size)])  7.14 us
    pallas_call x1, Pallas kernels, left_product(): pl.pallas_call(functools.partial(left_kernel, chunk), in_specs=[ANY] * 3,...  5.94 us
    ppermute x2, waiting for transfers between devices, sum_stage(): lax.ppermute(x, ('dp', 'tensor'), pairs_of(axis, 1 << low, 3 << low))  5.51 us
    pallas_call x2, Pallas kernels, new_feedback(): pl.pallas_call(kernel, in_specs=[VMEM] * first + ([VMEM] if own else [ANY...  5.08 us
    ppermute x2, starting transfers between devices, sum_stage(): lax.ppermute(x, ('dp', 'tensor'), pairs_of(axis, 1 << low, 2 << low))  4.7 us
    pallas_call x1, Pallas kernels, factors(): pl.pallas_call(functools.partial(factor_kernel, scale), in_specs=[VMEM],...  3.12 us
    pallas_call x4, Pallas kernels, right_product(): pl.pallas_call(functools.partial(right_kernel, own), in_specs=[VMEM] * (3...  2.98 us
  transfers between devices with their start and end apart: 13, of which 11 were waited for; matrix products, arithmetic and copies ran while one was open for 0% of the time, Pallas kernels for 16%

profile of v10, /device:TPU:1, one launch (start us, length us, event | category | flops | bytes accessed | tf_op | source)
XLA Modules:
  0.0 48.3 jit_solution(1829353611227332378)
XLA Ops:
  0.6 5.9 %left.1 = (f32[256,7168]{1,0:T(8,128)S(1)}, bf16[256,7168]{1,0:T(8,128)(2,1)S(1)}, bf16[256,7168]{1,0:T(8,128)(2,1)S(1)}, f32[32,256]{1,0:T(8,128)S(1)}) custom-call(bf16[256,7168]{1,0:T(8,128)(2,1)} %bitcast.8, f32[256,7168]{1,0:T(8,128)} %bitcast.7, f32[32,7168]{1,0:T(8,128)} %bitcast.9), custom_call_target="tpu_custom_call" | custom-call | flops 469762048 | bytes 11010048 | tf_op jit(solution)/shard_map/left/pallas_call | solution.py:80
  6.6 0.1 collective-permute-start
  6.7 1.2 %collective-permute-done = f32[32,256]{1,0:T(8,128)S(1)} collective-permute-done((f32[32,256]{1,0:T(8,128)S(1)}, f32[32,256]{1,0:T(8,128)S(1)}, u32[]{:S(2)}, u32[]{:S(2)}) %collective-permute-start) | collective-permute-done | bytes 32800 | tf_op jit(solution)/shard_map/ppermute | solution.py:260
  7.9 2.4 %collective-permute-start.2 = (f32[32,256]{1,0:T(8,128)S(1)}, f32[32,256]{1,0:T(8,128)S(1)}, u32[]{:S(2)}, u32[]{:S(2)}) collective-permute-start(f32[32,256]{1,0:T(8,128)S(1)} %add.27.mine), channel_id=1, source_target_pairs={{0,8},{1,9},{2,10},{3,11},{4,20},{5,21},{6,22},{7,23},{8,0},{9,1},... | collective-permute-start | bytes 98312 | tf_op jit(solution)/shard_map/ppermute | solution.py:271
  10.2 1.2 %collective-permute-start.1 = (f32[32,256]{1,0:T(8,128)S(1)}, f32[32,256]{1,0:T(8,128)S(1)}, u32[]{:S(2)}, u32[]{:S(2)}) collective-permute-start(f32[32,256]{1,0:T(8,128)S(1)} %add.27.mine), channel_id=1, source_target_pairs={{0,8},{1,9},{2,10},{3,11},{4,28},{5,29},{6,30},{7,31},{8,0},{9,1},... | collective-permute-start | bytes 98312 | tf_op jit(solution)/shard_map/ppermute | solution.py:270
  11.4 0.1 collective-permute-done.2.second
  11.6 2.4 %collective-permute-done.1.first = f32[32,256]{1,0:T(8,128)S(1)} collective-permute-done((f32[32,256]{1,0:T(8,128)S(1)}, f32[32,256]{1,0:T(8,128)S(1)}, u32[]{:S(2)}, u32[]{:S(2)}) %collective-permute-start.1) | collective-permute-done | bytes 32800 | tf_op jit(solution)/shard_map/ppermute | solution.py:270
  13.9 0.9 %collective-permute-start.3 = (f32[32,256]{1,0:T(8,128)S(1)}, f32[32,256]{1,0:T(8,128)S(1)}, u32[]{:S(2)}, u32[]{:S(2)}) collective-permute-start(f32[32,256]{1,0:T(8,128)S(1)} %part.2), channel_id=1, source_target_pairs={{0,4},{4,0},{8,12},{12,8},{16,20},{20,16},{24,28},{28,24},{1,5},{5... | collective-permute-start | bytes 98312 | tf_op jit(solution)/shard_map/ppermute | solution.py:260
  14.8 0.9 %collective-permute-done.3 = f32[32,256]{1,0:T(8,128)S(1)} collective-permute-done((f32[32,256]{1,0:T(8,128)S(1)}, f32[32,256]{1,0:T(8,128)S(1)}, u32[]{:S(2)}, u32[]{:S(2)}) %collective-permute-start.3) | collective-permute-done | bytes 32800 | tf_op jit(solution)/shard_map/ppermute | solution.py:260
  15.7 2.3 %collective-permute-start.5 = (f32[32,256]{1,0:T(8,128)S(1)}, f32[32,256]{1,0:T(8,128)S(1)}, u32[]{:S(2)}, u32[]{:S(2)}) collective-permute-start(f32[32,256]{1,0:T(8,128)S(1)} %add.28.mine), channel_id=1, source_target_pairs={{0,1},{1,0},{2,3},{3,2},{4,6},{5,7},{6,4},{7,5},{8,9},{9,8},{10,11... | collective-permute-start | bytes 98312 | tf_op jit(solution)/shard_map/ppermute | solution.py:271
  18.0 1.1 %collective-permute-start.4 = (f32[32,256]{1,0:T(8,128)S(1)}, f32[32,256]{1,0:T(8,128)S(1)}, u32[]{:S(2)}, u32[]{:S(2)}) collective-permute-start(f32[32,256]{1,0:T(8,128)S(1)} %add.28.mine), channel_id=1, source_target_pairs={{0,1},{1,0},{2,3},{3,2},{4,7},{5,6},{6,5},{7,4},{8,9},{9,8},{10,11... | collective-permute-start | bytes 98312 | tf_op jit(solution)/shard_map/ppermute | solution.py:270
  19.1 0.4 collective-permute-done.5.second
  19.5 3.1 %collective-permute-done.4.first = f32[32,256]{1,0:T(8,128)S(1)} collective-permute-done((f32[32,256]{1,0:T(8,128)S(1)}, f32[32,256]{1,0:T(8,128)S(1)}, u32[]{:S(2)}, u32[]{:S(2)}) %collective-permute-start.4) | collective-permute-done | bytes 32800 | tf_op jit(solution)/shard_map/ppermute | solution.py:270
  22.6 0.1 collective-permute-start.6
  22.7 0.7 %right.6.refs_0_ = f32[4,32,896]{2,1,0:T(8,128)S(1)} custom-call(f32[32,256]{1,0:T(8,128)S(1)} %part.3.left, bf16[256,7168]{1,0:T(8,128)(2,1)S(1)} %get-tuple-element.20.high, bf16[256,7168]{1,0:T(8,128)(2,1)S(1)} %get-tuple-element.21.low), custom_call_target="tpu_custom_call" | custom-call | flops 234881024 | bytes 3670016 | tf_op jit(solution)/shard_map/right/pallas_call | solution.py:125
  23.5 0.4 collective-permute-done.6.left
  23.9 0.7 %right.7 = f32[4,32,896]{2,1,0:T(8,128)S(1)} custom-call(f32[32,256]{1,0:T(8,128)S(1)} %collective-permute-done.6.left, bf16[256,7168]{1,0:T(8,128)(2,1)S(1)} %get-tuple-element.20.high, bf16[256,7168]{1,0:T(8,128)(2,1)S(1)} %get-tuple-element.21.low, f32[4,32,896]{2,1,0:T(8,128)S(1)} %right.6.refs_0_), custom_call_target="tpu_custom_call" | custom-call | flops 234881024 | bytes 3670016 | tf_op jit(solution)/shard_map/right/pallas_call | solution.py:125
  24.7 0.2 collective-permute-start.7
  24.8 0.7 %right.4.refs_0_ = f32[4,32,896]{2,1,0:T(8,128)S(1)} custom-call(f32[32,256]{1,0:T(8,128)S(1)} %part.3.left, bf16[256,7168]{1,0:T(8,128)(2,1)S(1)} %get-tuple-element.20.high, bf16[256,7168]{1,0:T(8,128)(2,1)S(1)} %get-tuple-element.21.low), custom_call_target="tpu_custom_call" | custom-call | flops 234881024 | bytes 3670016 | tf_op jit(solution)/shard_map/right/pallas_call | solution.py:125
  25.6 0.8 %right.5 = f32[4,32,896]{2,1,0:T(8,128)S(1)} custom-call(f32[32,256]{1,0:T(8,128)S(1)} %collective-permute-done.6.left, bf16[256,7168]{1,0:T(8,128)(2,1)S(1)} %get-tuple-element.20.high, bf16[256,7168]{1,0:T(8,128)(2,1)S(1)} %get-tuple-element.21.low, f32[4,32,896]{2,1,0:T(8,128)S(1)} %right.4.refs_0_), custom_call_target="tpu_custom_call" | custom-call | flops 234881024 | bytes 3670016 | tf_op jit(solution)/shard_map/right/pallas_call | solution.py:125
  26.3 0.2 collective-permute-done.7
  26.5 1.1 %collective-permute-start.8 = (f32[2,32,896]{2,1,0:T(8,128)S(1)}, f32[2,32,896]{2,1,0:T(8,128)S(1)}, u32[]{:S(2)}, u32[]{:S(2)}) collective-permute-start(f32[2,32,896]{2,1,0:T(8,128)S(1)} %get-tuple-element.31), channel_id=1, source_target_pairs={{0,8},{4,12},{8,0},{12,4},{16,24},{20,28},{24,16},{28,20},{1,9},{5... | collective-permute-start | bytes 688136 | tf_op jit(solution)/shard_map/ppermute | solution.py:260
  27.7 0.6 %collective-permute-start.10 = (f32[2,32,896]{2,1,0:T(8,128)S(1)}, f32[2,32,896]{2,1,0:T(8,128)S(1)}, u32[]{:S(2)}, u32[]{:S(2)}) collective-permute-start(f32[2,32,896]{2,1,0:T(8,128)S(1)} %get-tuple-element.32), channel_id=1, source_target_pairs={{0,16},{4,20},{8,24},{12,28},{16,0},{20,4},{24,8},{28,12},{1,17},{... | collective-permute-start | bytes 688136 | tf_op jit(solution)/shard_map/ppermute | solution.py:260
  28.3 3.1 %factor.1 = (f32[32,32]{1,0:T(8,128)S(1)}, f32[32,256]{1,0:T(8,128)S(1)}, bf16[256,128]{1,0:T(8,128)(2,1)S(1)}) custom-call(f32[32,256]{1,0:T(8,128)S(1)} %add_multiply_fusion.left), custom_call_target="tpu_custom_call" | custom-call | flops 2000000000 | bytes 1000000 | tf_op jit(solution)/shard_map/factor/pallas_call | solution.py:160
  31.4 2.2 %collective-permute-done.8 = f32[2,32,896]{2,1,0:T(8,128)S(1)} collective-permute-done((f32[2,32,896]{2,1,0:T(8,128)S(1)}, f32[2,32,896]{2,1,0:T(8,128)S(1)}, u32[]{:S(2)}, u32[]{:S(2)}) %collective-permute-start.8) | collective-permute-done | bytes 229408 | tf_op jit(solution)/shard_map/ppermute | solution.py:260
  33.6 1.3 %collective-permute-start.9 = (f32[2,32,896]{2,1,0:T(8,128)S(1)}, f32[2,32,896]{2,1,0:T(8,128)S(1)}, u32[]{:S(2)}, u32[]{:S(2)}) collective-permute-start(f32[2,32,896]{2,1,0:T(8,128)S(1)} %add.31), channel_id=1, source_target_pairs={{0,16},{4,20},{8,24},{12,28},{16,0},{20,4},{24,8},{28,12},{1,17},{... | collective-permute-start | bytes 688136 | tf_op jit(solution)/shard_map/ppermute | solution.py:260
  34.9 0.0 collective-permute-done.10
  35.0 0.5 %collective-permute-start.11 = (f32[2,32,896]{2,1,0:T(8,128)S(1)}, f32[2,32,896]{2,1,0:T(8,128)S(1)}, u32[]{:S(2)}, u32[]{:S(2)}) collective-permute-start(f32[2,32,896]{2,1,0:T(8,128)S(1)} %add.34), channel_id=1, source_target_pairs={{0,8},{4,12},{8,0},{12,4},{16,24},{20,28},{24,16},{28,20},{1,9},{5... | collective-permute-start | bytes 688136 | tf_op jit(solution)/shard_map/ppermute | solution.py:260
  35.5 4.3 %collective-permute-done.9 = f32[2,32,896]{2,1,0:T(8,128)S(1)} collective-permute-done((f32[2,32,896]{2,1,0:T(8,128)S(1)}, f32[2,32,896]{2,1,0:T(8,128)S(1)}, u32[]{:S(2)}, u32[]{:S(2)}) %collective-permute-start.9) | collective-permute-done | bytes 229408 | tf_op jit(solution)/shard_map/ppermute | solution.py:260
  39.8 1.0 %collective-permute-done.11 = f32[2,32,896]{2,1,0:T(8,128)S(1)} collective-permute-done((f32[2,32,896]{2,1,0:T(8,128)S(1)}, f32[2,32,896]{2,1,0:T(8,128)S(1)}, u32[]{:S(2)}, u32[]{:S(2)}) %collective-permute-start.11) | collective-permute-done | bytes 229408 | tf_op jit(solution)/shard_map/ppermute | solution.py:260
  40.9 2.3 %collective-permute-start.12 = (f32[4,32,896]{2,1,0:T(8,128)S(1)}, f32[4,32,896]{2,1,0:T(8,128)S(1)}, u32[]{:S(2)}, u32[]{:S(2)}) collective-permute-start(f32[4,32,896]{2,1,0:T(8,128)S(1)} %pad_maximum_fusion), channel_id=1, source_target_pairs={{0,4},{4,0},{8,12},{12,8},{16,20},{20,16},{24,28},{28,24},{1,5},{5... | collective-permute-start | bytes 1376264 | tf_op jit(solution)/shard_map/ppermute | solution.py:260
  43.2 2.5 %feedback.2 = (f32[256,7168]{1,0:T(8,128)}, f32[32,7168]{1,0:T(8,128)}, f32[32,256]{1,0:T(8,128)}) custom-call(bf16[256,128]{1,0:T(8,128)(2,1)S(1)} %get-tuple-element.18.stacked, f32[32,32]{1,0:T(8,128)S(1)} %get-tuple-element.19.inverse, f32[2,32,896]{2,1,0:T(8,128)S(1)} %add.32.refs_0_, f32[2,32,896]{2,1,0:T(8,128)S(1)} %add.35.refs_1_, ...), custom_call_target="tpu_custom_call" | custom-call | flops 234881024 | bytes 3670016 | tf_op jit(solution)/shard_map/feedback/pallas_call | solution.py:236
  45.7 0.0 collective-permute-done.12.refs_0_
  45.7 2.5 %feedback.3 = (f32[256,7168]{1,0:T(8,128)}, f32[32,7168]{1,0:T(8,128)}) custom-call(bf16[256,128]{1,0:T(8,128)(2,1)S(1)} %get-tuple-element.18.stacked, f32[32,32]{1,0:T(8,128)S(1)} %get-tuple-element.19.inverse, f32[4,32,896]{2,1,0:T(8,128)S(1)} %collective-permute-done.12.refs_0_, ...), custom_call_target="tpu_custom_call", output_to_operand_aliasing={{0}: (4, {}), {1}: (5, {})} | custom-call | flops 234881024 | bytes 3670016 | tf_op jit(solution)/shard_map/feedback/pallas_call | solution.py:236
  (11 shorter events, 0.2 us)
Async XLA Ops:
  6.6 1.3 %collective-permute-start = (f32[32,256]{1,0:T(8,128)S(1)}, f32[32,256]{1,0:T(8,128)S(1)}, u32[]{:S(2)}, u32[]{:S(2)}) collective-permute-start(f32[32,256]{1,0:T(8,128)S(1)} %get-tuple-element.17), channel_id=1, source_target_pairs={{0,4},{4,0},{8,12},{12,8},{16,20},{20,16},{24,28},{28,24},{1,5},{5... | collective-permute-start | bytes 98312 | tf_op jit(solution)/shard_map/ppermute | solution.py:260
  7.9 3.7 %collective-permute-start.2 = (f32[32,256]{1,0:T(8,128)S(1)}, f32[32,256]{1,0:T(8,128)S(1)}, u32[]{:S(2)}, u32[]{:S(2)}) collective-permute-start(f32[32,256]{1,0:T(8,128)S(1)} %add.27.mine), channel_id=1, source_target_pairs={{0,8},{1,9},{2,10},{3,11},{4,20},{5,21},{6,22},{7,23},{8,0},{9,1},... | collective-permute-start | bytes 98312 | tf_op jit(solution)/shard_map/ppermute | solution.py:271
  10.2 3.7 %collective-permute-start.1 = (f32[32,256]{1,0:T(8,128)S(1)}, f32[32,256]{1,0:T(8,128)S(1)}, u32[]{:S(2)}, u32[]{:S(2)}) collective-permute-start(f32[32,256]{1,0:T(8,128)S(1)} %add.27.mine), channel_id=1, source_target_pairs={{0,8},{1,9},{2,10},{3,11},{4,28},{5,29},{6,30},{7,31},{8,0},{9,1},... | collective-permute-start | bytes 98312 | tf_op jit(solution)/shard_map/ppermute | solution.py:270
  13.9 1.8 %collective-permute-start.3 = (f32[32,256]{1,0:T(8,128)S(1)}, f32[32,256]{1,0:T(8,128)S(1)}, u32[]{:S(2)}, u32[]{:S(2)}) collective-permute-start(f32[32,256]{1,0:T(8,128)S(1)} %part.2), channel_id=1, source_target_pairs={{0,4},{4,0},{8,12},{12,8},{16,20},{20,16},{24,28},{28,24},{1,5},{5... | collective-permute-start | bytes 98312 | tf_op jit(solution)/shard_map/ppermute | solution.py:260
  15.7 3.8 %collective-permute-start.5 = (f32[32,256]{1,0:T(8,128)S(1)}, f32[32,256]{1,0:T(8,128)S(1)}, u32[]{:S(2)}, u32[]{:S(2)}) collective-permute-start(f32[32,256]{1,0:T(8,128)S(1)} %add.28.mine), channel_id=1, source_target_pairs={{0,1},{1,0},{2,3},{3,2},{4,6},{5,7},{6,4},{7,5},{8,9},{9,8},{10,11... | collective-permute-start | bytes 98312 | tf_op jit(solution)/shard_map/ppermute | solution.py:271
  18.0 4.6 %collective-permute-start.4 = (f32[32,256]{1,0:T(8,128)S(1)}, f32[32,256]{1,0:T(8,128)S(1)}, u32[]{:S(2)}, u32[]{:S(2)}) collective-permute-start(f32[32,256]{1,0:T(8,128)S(1)} %add.28.mine), channel_id=1, source_target_pairs={{0,1},{1,0},{2,3},{3,2},{4,7},{5,6},{6,5},{7,4},{8,9},{9,8},{10,11... | collective-permute-start | bytes 98312 | tf_op jit(solution)/shard_map/ppermute | solution.py:270
  22.6 1.3 %collective-permute-start.6 = (f32[32,256]{1,0:T(8,128)S(1)}, f32[32,256]{1,0:T(8,128)S(1)}, u32[]{:S(2)}, u32[]{:S(2)}) collective-permute-start(f32[32,256]{1,0:T(8,128)S(1)} %part.3.left), channel_id=1, source_target_pairs={{0,4},{4,0},{8,12},{12,8},{16,20},{20,16},{24,28},{28,24},{1,5},{5... | collective-permute-start | bytes 98312 | tf_op jit(solution)/shard_map/ppermute | solution.py:260
  24.7 1.8 %collective-permute-start.7 = (f32[4,32,896]{2,1,0:T(8,128)S(1)}, f32[4,32,896]{2,1,0:T(8,128)S(1)}, u32[]{:S(2)}, u32[]{:S(2)}) collective-permute-start(f32[4,32,896]{2,1,0:T(8,128)S(1)} %right.7), channel_id=1, source_target_pairs={{0,4},{4,0},{8,12},{12,8},{16,20},{20,16},{24,28},{28,24},{1,5},{5... | collective-permute-start | bytes 1376264 | tf_op jit(solution)/shard_map/ppermute | solution.py:260
  26.5 7.1 %collective-permute-start.8 = (f32[2,32,896]{2,1,0:T(8,128)S(1)}, f32[2,32,896]{2,1,0:T(8,128)S(1)}, u32[]{:S(2)}, u32[]{:S(2)}) collective-permute-start(f32[2,32,896]{2,1,0:T(8,128)S(1)} %get-tuple-element.31), channel_id=1, source_target_pairs={{0,8},{4,12},{8,0},{12,4},{16,24},{20,28},{24,16},{28,20},{1,9},{5... | collective-permute-start | bytes 688136 | tf_op jit(solution)/shard_map/ppermute | solution.py:260
  27.7 7.2 %collective-permute-start.10 = (f32[2,32,896]{2,1,0:T(8,128)S(1)}, f32[2,32,896]{2,1,0:T(8,128)S(1)}, u32[]{:S(2)}, u32[]{:S(2)}) collective-permute-start(f32[2,32,896]{2,1,0:T(8,128)S(1)} %get-tuple-element.32), channel_id=1, source_target_pairs={{0,16},{4,20},{8,24},{12,28},{16,0},{20,4},{24,8},{28,12},{1,17},{... | collective-permute-start | bytes 688136 | tf_op jit(solution)/shard_map/ppermute | solution.py:260
  33.6 6.1 %collective-permute-start.9 = (f32[2,32,896]{2,1,0:T(8,128)S(1)}, f32[2,32,896]{2,1,0:T(8,128)S(1)}, u32[]{:S(2)}, u32[]{:S(2)}) collective-permute-start(f32[2,32,896]{2,1,0:T(8,128)S(1)} %add.31), channel_id=1, source_target_pairs={{0,16},{4,20},{8,24},{12,28},{16,0},{20,4},{24,8},{28,12},{1,17},{... | collective-permute-start | bytes 688136 | tf_op jit(solution)/shard_map/ppermute | solution.py:260
  35.0 5.9 %collective-permute-start.11 = (f32[2,32,896]{2,1,0:T(8,128)S(1)}, f32[2,32,896]{2,1,0:T(8,128)S(1)}, u32[]{:S(2)}, u32[]{:S(2)}) collective-permute-start(f32[2,32,896]{2,1,0:T(8,128)S(1)} %add.34), channel_id=1, source_target_pairs={{0,8},{4,12},{8,0},{12,4},{16,24},{20,28},{24,16},{28,20},{1,9},{5... | collective-permute-start | bytes 688136 | tf_op jit(solution)/shard_map/ppermute | solution.py:260
  40.9 4.8 %collective-permute-start.12 = (f32[4,32,896]{2,1,0:T(8,128)S(1)}, f32[4,32,896]{2,1,0:T(8,128)S(1)}, u32[]{:S(2)}, u32[]{:S(2)}) collective-permute-start(f32[4,32,896]{2,1,0:T(8,128)S(1)} %pad_maximum_fusion), channel_id=1, source_target_pairs={{0,4},{4,0},{8,12},{12,8},{16,20},{20,16},{24,28},{28,24},{1,5},{5... | collective-permute-start | bytes 1376264 | tf_op jit(solution)/shard_map/ppermute | solution.py:260

commit v11 on v10

--- a/solution.py
+++ b/solution.py
@@ -339,7 +339,7 @@
     parts = [half[: chips // 2] + theirs[: chips // 2], half[chips // 2 :] + theirs[chips // 2 :]]
     inverse, factor, stacked = factors(left, 1.0 / replicas**2)
     for i, pair in enumerate(zip(masks, masks[::-1])):
-        came = [swap(x, "dp", mask) for x, mask in zip(parts, pair)]
+        came = [lax.ppermute(x, ("dp", "tensor"), pairs_of("dp", *order)) for x, order in zip(parts, (pair, pair[::-1]))]
         if i == 0:
             came = [after(x, inverse) for x in came]
         parts = [x + y for x, y in zip(parts, came)]

time: 48.4 us -> 48.2 us (level)
    ppermute x0 -> x4, waiting for transfers between devices: none -> 7.58 us  [per_device(): lax.ppermute(x, ('dp', 'tensor'), pairs_of('dp', *order))]
    ppermute x9 -> x5, waiting for transfers between devices: 10.1 us -> 2.62 us  [swap(): return lax.ppermute(x, axis, [(i, i ^ mask) for i in range(size)])]
    ppermute x9 -> x5, starting transfers between devices: 7.14 us -> 2.4 us  [swap(): return lax.ppermute(x, axis, [(i, i ^ mask) for i in range(size)])]
    ppermute x0 -> x4, starting transfers between devices: none -> 4.38 us  [per_device(): lax.ppermute(x, ('dp', 'tensor'), pairs_of('dp', *order))]
  transfers between devices with their start and end apart: 13 -> 13, of which waited for: 11 -> 12; matrix products, arithmetic and copies ran while one was open for 0% -> 0% of each run, Pallas kernels for 16% -> 16%
where the time goes in v11:
time: 48.2 us; the launch traced here: 48 us
  Pallas kernels  17.2 us (36%)
  waiting for transfers between devices  16.2 us (34%)
  starting transfers between devices  13.7 us (28%)
  between operations  0.71 us (1%)
    ppermute x4, waiting for transfers between devices, per_device(): lax.ppermute(x, ('dp', 'tensor'), pairs_of('dp', *order))  7.58 us
    pallas_call x1, Pallas kernels, left_product(): pl.pallas_call(functools.partial(left_kernel, chunk), in_specs=[ANY] * 3,...  5.94 us
    ppermute x2, waiting for transfers between devices, sum_stage(): lax.ppermute(x, ('dp', 'tensor'), pairs_of(axis, 1 << low, 3 << low))  5.51 us
    pallas_call x2, Pallas kernels, new_feedback(): pl.pallas_call(kernel, in_specs=[VMEM] * first + ([VMEM] if own else [ANY...  5.1 us
    ppermute x2, starting transfers between devices, sum_stage(): lax.ppermute(x, ('dp', 'tensor'), pairs_of(axis, 1 << low, 2 << low))  4.7 us
    ppermute x4, starting transfers between devices, per_device(): lax.ppermute(x, ('dp', 'tensor'), pairs_of('dp', *order))  4.38 us
    pallas_call x1, Pallas kernels, factors(): pl.pallas_call(functools.partial(factor_kernel, scale), in_specs=[VMEM],...  3.12 us
    pallas_call x4, Pallas kernels, right_product(): pl.pallas_call(functools.partial(right_kernel, own), in_specs=[VMEM] * (3...  2.98 us
  transfers between devices with their start and end apart: 13, of which 12 were waited for; matrix products, arithmetic and copies ran while one was open for 0% of the time, Pallas kernels for 16%

profile of v11, /device:TPU:1, one launch (start us, length us, event | category | flops | bytes accessed | tf_op | source)
XLA Modules:
  0.0 48.0 jit_solution(4104401848954519658)
XLA Ops:
  0.6 5.9 %left.1 = (f32[256,7168]{1,0:T(8,128)S(1)}, bf16[256,7168]{1,0:T(8,128)(2,1)S(1)}, bf16[256,7168]{1,0:T(8,128)(2,1)S(1)}, f32[32,256]{1,0:T(8,128)S(1)}) custom-call(bf16[256,7168]{1,0:T(8,128)(2,1)} %bitcast.8, f32[256,7168]{1,0:T(8,128)} %bitcast.7, f32[32,7168]{1,0:T(8,128)} %bitcast.9), custom_call_target="tpu_custom_call" | custom-call | flops 469762048 | bytes 11010048 | tf_op jit(solution)/shard_map/left/pallas_call | solution.py:80
  6.6 0.1 collective-permute-start
  6.7 1.2 %collective-permute-done = f32[32,256]{1,0:T(8,128)S(1)} collective-permute-done((f32[32,256]{1,0:T(8,128)S(1)}, f32[32,256]{1,0:T(8,128)S(1)}, u32[]{:S(2)}, u32[]{:S(2)}) %collective-permute-start) | collective-permute-done | bytes 32800 | tf_op jit(solution)/shard_map/ppermute | solution.py:260
  7.9 2.4 %collective-permute-start.2 = (f32[32,256]{1,0:T(8,128)S(1)}, f32[32,256]{1,0:T(8,128)S(1)}, u32[]{:S(2)}, u32[]{:S(2)}) collective-permute-start(f32[32,256]{1,0:T(8,128)S(1)} %add.27.mine), channel_id=1, source_target_pairs={{0,8},{1,9},{2,10},{3,11},{4,20},{5,21},{6,22},{7,23},{8,0},{9,1},... | collective-permute-start | bytes 98312 | tf_op jit(solution)/shard_map/ppermute | solution.py:271
  10.2 1.2 %collective-permute-start.1 = (f32[32,256]{1,0:T(8,128)S(1)}, f32[32,256]{1,0:T(8,128)S(1)}, u32[]{:S(2)}, u32[]{:S(2)}) collective-permute-start(f32[32,256]{1,0:T(8,128)S(1)} %add.27.mine), channel_id=1, source_target_pairs={{0,8},{1,9},{2,10},{3,11},{4,28},{5,29},{6,30},{7,31},{8,0},{9,1},... | collective-permute-start | bytes 98312 | tf_op jit(solution)/shard_map/ppermute | solution.py:270
  11.4 0.1 collective-permute-done.2.second
  11.6 2.4 %collective-permute-done.1.first = f32[32,256]{1,0:T(8,128)S(1)} collective-permute-done((f32[32,256]{1,0:T(8,128)S(1)}, f32[32,256]{1,0:T(8,128)S(1)}, u32[]{:S(2)}, u32[]{:S(2)}) %collective-permute-start.1) | collective-permute-done | bytes 32800 | tf_op jit(solution)/shard_map/ppermute | solution.py:270
  13.9 0.9 %collective-permute-start.3 = (f32[32,256]{1,0:T(8,128)S(1)}, f32[32,256]{1,0:T(8,128)S(1)}, u32[]{:S(2)}, u32[]{:S(2)}) collective-permute-start(f32[32,256]{1,0:T(8,128)S(1)} %part.2), channel_id=1, source_target_pairs={{0,4},{4,0},{8,12},{12,8},{16,20},{20,16},{24,28},{28,24},{1,5},{5... | collective-permute-start | bytes 98312 | tf_op jit(solution)/shard_map/ppermute | solution.py:260
  14.8 0.9 %collective-permute-done.3 = f32[32,256]{1,0:T(8,128)S(1)} collective-permute-done((f32[32,256]{1,0:T(8,128)S(1)}, f32[32,256]{1,0:T(8,128)S(1)}, u32[]{:S(2)}, u32[]{:S(2)}) %collective-permute-start.3) | collective-permute-done | bytes 32800 | tf_op jit(solution)/shard_map/ppermute | solution.py:260
  15.7 2.3 %collective-permute-start.5 = (f32[32,256]{1,0:T(8,128)S(1)}, f32[32,256]{1,0:T(8,128)S(1)}, u32[]{:S(2)}, u32[]{:S(2)}) collective-permute-start(f32[32,256]{1,0:T(8,128)S(1)} %add.28.mine), channel_id=1, source_target_pairs={{0,1},{1,0},{2,3},{3,2},{4,6},{5,7},{6,4},{7,5},{8,9},{9,8},{10,11... | collective-permute-start | bytes 98312 | tf_op jit(solution)/shard_map/ppermute | solution.py:271
  18.0 1.1 %collective-permute-start.4 = (f32[32,256]{1,0:T(8,128)S(1)}, f32[32,256]{1,0:T(8,128)S(1)}, u32[]{:S(2)}, u32[]{:S(2)}) collective-permute-start(f32[32,256]{1,0:T(8,128)S(1)} %add.28.mine), channel_id=1, source_target_pairs={{0,1},{1,0},{2,3},{3,2},{4,7},{5,6},{6,5},{7,4},{8,9},{9,8},{10,11... | collective-permute-start | bytes 98312 | tf_op jit(solution)/shard_map/ppermute | solution.py:270
  19.1 0.4 collective-permute-done.5.second
  19.5 3.1 %collective-permute-done.4.first = f32[32,256]{1,0:T(8,128)S(1)} collective-permute-done((f32[32,256]{1,0:T(8,128)S(1)}, f32[32,256]{1,0:T(8,128)S(1)}, u32[]{:S(2)}, u32[]{:S(2)}) %collective-permute-start.4) | collective-permute-done | bytes 32800 | tf_op jit(solution)/shard_map/ppermute | solution.py:270
  22.6 0.1 collective-permute-start.6
  22.7 0.7 %right.6.refs_0_ = f32[4,32,896]{2,1,0:T(8,128)S(1)} custom-call(f32[32,256]{1,0:T(8,128)S(1)} %part.3.left, bf16[256,7168]{1,0:T(8,128)(2,1)S(1)} %get-tuple-element.20.high, bf16[256,7168]{1,0:T(8,128)(2,1)S(1)} %get-tuple-element.21.low), custom_call_target="tpu_custom_call" | custom-call | flops 234881024 | bytes 3670016 | tf_op jit(solution)/shard_map/right/pallas_call | solution.py:125
  23.5 0.4 collective-permute-done.6.left
  23.9 0.7 %right.7 = f32[4,32,896]{2,1,0:T(8,128)S(1)} custom-call(f32[32,256]{1,0:T(8,128)S(1)} %collective-permute-done.6.left, bf16[256,7168]{1,0:T(8,128)(2,1)S(1)} %get-tuple-element.20.high, bf16[256,7168]{1,0:T(8,128)(2,1)S(1)} %get-tuple-element.21.low, f32[4,32,896]{2,1,0:T(8,128)S(1)} %right.6.refs_0_), custom_call_target="tpu_custom_call" | custom-call | flops 234881024 | bytes 3670016 | tf_op jit(solution)/shard_map/right/pallas_call | solution.py:125
  24.7 0.2 collective-permute-start.7
  24.8 0.7 %right.4.refs_0_ = f32[4,32,896]{2,1,0:T(8,128)S(1)} custom-call(f32[32,256]{1,0:T(8,128)S(1)} %part.3.left, bf16[256,7168]{1,0:T(8,128)(2,1)S(1)} %get-tuple-element.20.high, bf16[256,7168]{1,0:T(8,128)(2,1)S(1)} %get-tuple-element.21.low), custom_call_target="tpu_custom_call" | custom-call | flops 234881024 | bytes 3670016 | tf_op jit(solution)/shard_map/right/pallas_call | solution.py:125
  25.6 0.8 %right.5 = f32[4,32,896]{2,1,0:T(8,128)S(1)} custom-call(f32[32,256]{1,0:T(8,128)S(1)} %collective-permute-done.6.left, bf16[256,7168]{1,0:T(8,128)(2,1)S(1)} %get-tuple-element.20.high, bf16[256,7168]{1,0:T(8,128)(2,1)S(1)} %get-tuple-element.21.low, f32[4,32,896]{2,1,0:T(8,128)S(1)} %right.4.refs_0_), custom_call_target="tpu_custom_call" | custom-call | flops 234881024 | bytes 3670016 | tf_op jit(solution)/shard_map/right/pallas_call | solution.py:125
  26.3 0.2 collective-permute-done.7
  26.5 1.3 %collective-permute-start.8 = (f32[2,32,896]{2,1,0:T(8,128)S(1)}, f32[2,32,896]{2,1,0:T(8,128)S(1)}, u32[]{:S(2)}, u32[]{:S(2)}) collective-permute-start(f32[2,32,896]{2,1,0:T(8,128)S(1)} %get-tuple-element.31), channel_id=1, source_target_pairs={{0,8},{1,9},{2,10},{3,11},{4,20},{5,21},{6,22},{7,23},{8,0},{9,1},... | collective-permute-start | bytes 688136 | tf_op jit(solution)/shard_map/ppermute | solution.py:342
  27.8 0.4 collective-permute-start.10
  28.3 3.1 %factor.1 = (f32[32,32]{1,0:T(8,128)S(1)}, f32[32,256]{1,0:T(8,128)S(1)}, bf16[256,128]{1,0:T(8,128)(2,1)S(1)}) custom-call(f32[32,256]{1,0:T(8,128)S(1)} %add_multiply_fusion.left), custom_call_target="tpu_custom_call" | custom-call | flops 2000000000 | bytes 1000000 | tf_op jit(solution)/shard_map/factor/pallas_call | solution.py:160
  31.4 0.7 %collective-permute-done.8 = f32[2,32,896]{2,1,0:T(8,128)S(1)} collective-permute-done((f32[2,32,896]{2,1,0:T(8,128)S(1)}, f32[2,32,896]{2,1,0:T(8,128)S(1)}, u32[]{:S(2)}, u32[]{:S(2)}) %collective-permute-start.8) | collective-permute-done | bytes 229408 | tf_op jit(solution)/shard_map/ppermute | solution.py:342
  32.2 1.9 %collective-permute-start.9 = (f32[2,32,896]{2,1,0:T(8,128)S(1)}, f32[2,32,896]{2,1,0:T(8,128)S(1)}, u32[]{:S(2)}, u32[]{:S(2)}) collective-permute-start(f32[2,32,896]{2,1,0:T(8,128)S(1)} %add.31), channel_id=1, source_target_pairs={{0,16},{1,17},{2,18},{3,19},{4,12},{5,13},{6,14},{7,15},{8,24},{9,... | collective-permute-start | bytes 688136 | tf_op jit(solution)/shard_map/ppermute | solution.py:342
  34.0 0.6 %collective-permute-done.10 = f32[2,32,896]{2,1,0:T(8,128)S(1)} collective-permute-done((f32[2,32,896]{2,1,0:T(8,128)S(1)}, f32[2,32,896]{2,1,0:T(8,128)S(1)}, u32[]{:S(2)}, u32[]{:S(2)}) %collective-permute-start.10) | collective-permute-done | bytes 229408 | tf_op jit(solution)/shard_map/ppermute | solution.py:342
  34.6 0.8 %collective-permute-start.11 = (f32[2,32,896]{2,1,0:T(8,128)S(1)}, f32[2,32,896]{2,1,0:T(8,128)S(1)}, u32[]{:S(2)}, u32[]{:S(2)}) collective-permute-start(f32[2,32,896]{2,1,0:T(8,128)S(1)} %add.34), channel_id=1, source_target_pairs={{0,8},{1,9},{2,10},{3,11},{4,20},{5,21},{6,22},{7,23},{8,0},{9,1},... | collective-permute-start | bytes 688136 | tf_op jit(solution)/shard_map/ppermute | solution.py:342
  35.4 2.0 %collective-permute-done.9 = f32[2,32,896]{2,1,0:T(8,128)S(1)} collective-permute-done((f32[2,32,896]{2,1,0:T(8,128)S(1)}, f32[2,32,896]{2,1,0:T(8,128)S(1)}, u32[]{:S(2)}, u32[]{:S(2)}) %collective-permute-start.9) | collective-permute-done | bytes 229408 | tf_op jit(solution)/shard_map/ppermute | solution.py:342
  37.5 4.3 %collective-permute-done.11 = f32[2,32,896]{2,1,0:T(8,128)S(1)} collective-permute-done((f32[2,32,896]{2,1,0:T(8,128)S(1)}, f32[2,32,896]{2,1,0:T(8,128)S(1)}, u32[]{:S(2)}, u32[]{:S(2)}) %collective-permute-start.11) | collective-permute-done | bytes 229408 | tf_op jit(solution)/shard_map/ppermute | solution.py:342
  41.8 1.1 %collective-permute-start.12 = (f32[4,32,896]{2,1,0:T(8,128)S(1)}, f32[4,32,896]{2,1,0:T(8,128)S(1)}, u32[]{:S(2)}, u32[]{:S(2)}) collective-permute-start(f32[4,32,896]{2,1,0:T(8,128)S(1)} %pad_maximum_fusion), channel_id=1, source_target_pairs={{0,4},{4,0},{8,12},{12,8},{16,20},{20,16},{24,28},{28,24},{1,5},{5... | collective-permute-start | bytes 1376264 | tf_op jit(solution)/shard_map/ppermute | solution.py:260
  42.9 2.5 %feedback.2 = (f32[256,7168]{1,0:T(8,128)}, f32[32,7168]{1,0:T(8,128)}, f32[32,256]{1,0:T(8,128)}) custom-call(bf16[256,128]{1,0:T(8,128)(2,1)S(1)} %get-tuple-element.18.stacked, f32[32,32]{1,0:T(8,128)S(1)} %get-tuple-element.19.inverse, f32[2,32,896]{2,1,0:T(8,128)S(1)} %add.32.refs_0_, f32[2,32,896]{2,1,0:T(8,128)S(1)} %add.35.refs_1_, ...), custom_call_target="tpu_custom_call" | custom-call | flops 234881024 | bytes 3670016 | tf_op jit(solution)/shard_map/feedback/pallas_call | solution.py:236
  45.5 0.0 collective-permute-done.12.refs_0_
  45.5 2.5 %feedback.3 = (f32[256,7168]{1,0:T(8,128)}, f32[32,7168]{1,0:T(8,128)}) custom-call(bf16[256,128]{1,0:T(8,128)(2,1)S(1)} %get-tuple-element.18.stacked, f32[32,32]{1,0:T(8,128)S(1)} %get-tuple-element.19.inverse, f32[4,32,896]{2,1,0:T(8,128)S(1)} %collective-permute-done.12.refs_0_, ...), custom_call_target="tpu_custom_call", output_to_operand_aliasing={{0}: (4, {}), {1}: (5, {})} | custom-call | flops 234881024 | bytes 3670016 | tf_op jit(solution)/shard_map/feedback/pallas_call | solution.py:236
  (11 shorter events, 0.2 us)
Async XLA Ops:
  6.6 1.3 %collective-permute-start = (f32[32,256]{1,0:T(8,128)S(1)}, f32[32,256]{1,0:T(8,128)S(1)}, u32[]{:S(2)}, u32[]{:S(2)}) collective-permute-start(f32[32,256]{1,0:T(8,128)S(1)} %get-tuple-element.17), channel_id=1, source_target_pairs={{0,4},{4,0},{8,12},{12,8},{16,20},{20,16},{24,28},{28,24},{1,5},{5... | collective-permute-start | bytes 98312 | tf_op jit(solution)/shard_map/ppermute | solution.py:260
  7.9 3.7 %collective-permute-start.2 = (f32[32,256]{1,0:T(8,128)S(1)}, f32[32,256]{1,0:T(8,128)S(1)}, u32[]{:S(2)}, u32[]{:S(2)}) collective-permute-start(f32[32,256]{1,0:T(8,128)S(1)} %add.27.mine), channel_id=1, source_target_pairs={{0,8},{1,9},{2,10},{3,11},{4,20},{5,21},{6,22},{7,23},{8,0},{9,1},... | collective-permute-start | bytes 98312 | tf_op jit(solution)/shard_map/ppermute | solution.py:271
  10.2 3.7 %collective-permute-start.1 = (f32[32,256]{1,0:T(8,128)S(1)}, f32[32,256]{1,0:T(8,128)S(1)}, u32[]{:S(2)}, u32[]{:S(2)}) collective-permute-start(f32[32,256]{1,0:T(8,128)S(1)} %add.27.mine), channel_id=1, source_target_pairs={{0,8},{1,9},{2,10},{3,11},{4,28},{5,29},{6,30},{7,31},{8,0},{9,1},... | collective-permute-start | bytes 98312 | tf_op jit(solution)/shard_map/ppermute | solution.py:270
  13.9 1.8 %collective-permute-start.3 = (f32[32,256]{1,0:T(8,128)S(1)}, f32[32,256]{1,0:T(8,128)S(1)}, u32[]{:S(2)}, u32[]{:S(2)}) collective-permute-start(f32[32,256]{1,0:T(8,128)S(1)} %part.2), channel_id=1, source_target_pairs={{0,4},{4,0},{8,12},{12,8},{16,20},{20,16},{24,28},{28,24},{1,5},{5... | collective-permute-start | bytes 98312 | tf_op jit(solution)/shard_map/ppermute | solution.py:260
  15.7 3.8 %collective-permute-start.5 = (f32[32,256]{1,0:T(8,128)S(1)}, f32[32,256]{1,0:T(8,128)S(1)}, u32[]{:S(2)}, u32[]{:S(2)}) collective-permute-start(f32[32,256]{1,0:T(8,128)S(1)} %add.28.mine), channel_id=1, source_target_pairs={{0,1},{1,0},{2,3},{3,2},{4,6},{5,7},{6,4},{7,5},{8,9},{9,8},{10,11... | collective-permute-start | bytes 98312 | tf_op jit(solution)/shard_map/ppermute | solution.py:271
  18.0 4.6 %collective-permute-start.4 = (f32[32,256]{1,0:T(8,128)S(1)}, f32[32,256]{1,0:T(8,128)S(1)}, u32[]{:S(2)}, u32[]{:S(2)}) collective-permute-start(f32[32,256]{1,0:T(8,128)S(1)} %add.28.mine), channel_id=1, source_target_pairs={{0,1},{1,0},{2,3},{3,2},{4,7},{5,6},{6,5},{7,4},{8,9},{9,8},{10,11... | collective-permute-start | bytes 98312 | tf_op jit(solution)/shard_map/ppermute | solution.py:270
  22.6 1.3 %collective-permute-start.6 = (f32[32,256]{1,0:T(8,128)S(1)}, f32[32,256]{1,0:T(8,128)S(1)}, u32[]{:S(2)}, u32[]{:S(2)}) collective-permute-start(f32[32,256]{1,0:T(8,128)S(1)} %part.3.left), channel_id=1, source_target_pairs={{0,4},{4,0},{8,12},{12,8},{16,20},{20,16},{24,28},{28,24},{1,5},{5... | collective-permute-start | bytes 98312 | tf_op jit(solution)/shard_map/ppermute | solution.py:260
  24.7 1.8 %collective-permute-start.7 = (f32[4,32,896]{2,1,0:T(8,128)S(1)}, f32[4,32,896]{2,1,0:T(8,128)S(1)}, u32[]{:S(2)}, u32[]{:S(2)}) collective-permute-start(f32[4,32,896]{2,1,0:T(8,128)S(1)} %right.7), channel_id=1, source_target_pairs={{0,4},{4,0},{8,12},{12,8},{16,20},{20,16},{24,28},{28,24},{1,5},{5... | collective-permute-start | bytes 1376264 | tf_op jit(solution)/shard_map/ppermute | solution.py:260
  26.5 5.6 %collective-permute-start.8 = (f32[2,32,896]{2,1,0:T(8,128)S(1)}, f32[2,32,896]{2,1,0:T(8,128)S(1)}, u32[]{:S(2)}, u32[]{:S(2)}) collective-permute-start(f32[2,32,896]{2,1,0:T(8,128)S(1)} %get-tuple-element.31), channel_id=1, source_target_pairs={{0,8},{1,9},{2,10},{3,11},{4,20},{5,21},{6,22},{7,23},{8,0},{9,1},... | collective-permute-start | bytes 688136 | tf_op jit(solution)/shard_map/ppermute | solution.py:342
  27.8 6.8 %collective-permute-start.10 = (f32[2,32,896]{2,1,0:T(8,128)S(1)}, f32[2,32,896]{2,1,0:T(8,128)S(1)}, u32[]{:S(2)}, u32[]{:S(2)}) collective-permute-start(f32[2,32,896]{2,1,0:T(8,128)S(1)} %get-tuple-element.32), channel_id=1, source_target_pairs={{0,16},{1,17},{2,18},{3,19},{4,12},{5,13},{6,14},{7,15},{8,24},{9,... | collective-permute-start | bytes 688136 | tf_op jit(solution)/shard_map/ppermute | solution.py:342
  32.2 5.3 %collective-permute-start.9 = (f32[2,32,896]{2,1,0:T(8,128)S(1)}, f32[2,32,896]{2,1,0:T(8,128)S(1)}, u32[]{:S(2)}, u32[]{:S(2)}) collective-permute-start(f32[2,32,896]{2,1,0:T(8,128)S(1)} %add.31), channel_id=1, source_target_pairs={{0,16},{1,17},{2,18},{3,19},{4,12},{5,13},{6,14},{7,15},{8,24},{9,... | collective-permute-start | bytes 688136 | tf_op jit(solution)/shard_map/ppermute | solution.py:342
  34.6 7.1 %collective-permute-start.11 = (f32[2,32,896]{2,1,0:T(8,128)S(1)}, f32[2,32,896]{2,1,0:T(8,128)S(1)}, u32[]{:S(2)}, u32[]{:S(2)}) collective-permute-start(f32[2,32,896]{2,1,0:T(8,128)S(1)} %add.34), channel_id=1, source_target_pairs={{0,8},{1,9},{2,10},{3,11},{4,20},{5,21},{6,22},{7,23},{8,0},{9,1},... | collective-permute-start | bytes 688136 | tf_op jit(solution)/shard_map/ppermute | solution.py:342
  41.8 3.7 %collective-permute-start.12 = (f32[4,32,896]{2,1,0:T(8,128)S(1)}, f32[4,32,896]{2,1,0:T(8,128)S(1)}, u32[]{:S(2)}, u32[]{:S(2)}) collective-permute-start(f32[4,32,896]{2,1,0:T(8,128)S(1)} %pad_maximum_fusion), channel_id=1, source_target_pairs={{0,4},{4,0},{8,12},{12,8},{16,20},{20,16},{24,28},{28,24},{1,5},{5... | collective-permute-start | bytes 1376264 | tf_op jit(solution)/shard_map/ppermute | solution.py:260
